TPU v7x, 256 devices: a whole 4x4x8 slice. The times are simulated.
256 devices in a mesh: seq: 16 (over y, x), asset: 16 (over z, core).
Axes of the slice: x: 4, y: 4, z: 8, core: 2. Of those that a mesh axis runs over, the one named last changes fastest.
Arguments:
- tokens: bfloat16 [16, 8192, 1024], P('asset', 'seq'), may hold values from -6 to 6
- w_query: bfloat16 [1024, 1024], replicated, may hold values from -0.1875 to 0.1875
- w_key: bfloat16 [1024, 1024], replicated, may hold values from -0.1875 to 0.1875
- w_value: bfloat16 [1024, 1024], replicated, may hold values from -0.1875 to 0.1875
- decay_log: float32 [16, 8, 8192], P('asset', None, 'seq'), may hold values from -1 to 0, as said below
- lengths: int32 [16], P('asset'), may hold values from 128 to 8192, as said below
- sources: int32 [16], replicated, may hold values from 0 to 15, as said below
- targets: int32 [16], replicated, may hold values from 0 to 15, as said below
- stash: float32 [16, 8, 128, 128], P('asset', None, 'seq'), may hold values from -24 to 24
- whiten: bfloat16 [16, 1024, 1024], P('asset'), may hold values from -0.1875 to 0.1875
Outputs:
- features: bfloat16 [16, 8192, 1024], P('asset', 'seq')
- kept_states: float32 [16, 8, 128, 128], P('asset', None, 'seq')
Inputs may be any that keep to these rules, and one draw needn't show every extreme that they name: `decay_log`: negative. `lengths`: multiples of 128; some asset has 8192 valid steps and another 128. `sources`: a permutation of the asset numbers. `targets`: a permutation of the asset numbers.
All inputs are finite; a program needn't handle non-finite values.
Results may differ from a plain program's by a relative error of at most 0.0067.
Values sent between devices are 32-bit elements; how exact they have to be, the bound alone decides.
No kernel may reach another device: no remote copies, remote signals or barrier semaphores. Data moves between devices by JAX's collectives and lax.ppermute only.
A program may use at most 128 MiB of HBM per device.

v0:
```python
import jax
import jax.numpy as jnp
from jax import lax
from jax.sharding import PartitionSpec as P

SPAN = 128


HIGHEST_PRECISION = lax.Precision.HIGHEST
EPSILON = 1e-05


def entering(part, axis, combine, identity):
    place = lax.axis_index(axis)
    gathered = jax.tree.map(lambda a: lax.all_gather(a, axis), part)
    state = jax.tree.map(lambda a, e: jnp.zeros_like(a) + jnp.asarray(e, a.dtype), part, identity)

    def one(hop, state):
        return combine(
            state, jax.tree.map(lambda a: lax.dynamic_index_in_dim(a, hop, 0, False), gathered)
        )

    return lax.fori_loop(0, place, one, state)


def broadcast(value, axis, source):
    kept = jnp.where(lax.axis_index(axis) == source, value, 0).astype(value.dtype)
    return lax.psum(kept, axis)


def local_pass(tokens, decay_rates, live_mask, w_query, w_key, w_value):
    asset_count, step_count, model_width = tokens.shape
    head_count = decay_rates.shape[1]
    head_dim = model_width // head_count
    blocks = step_count // SPAN
    block_shape = (asset_count, blocks, SPAN, head_count, head_dim)
    queries = jnp.einsum("ald,de->ale", tokens, w_query, preferred_element_type=jnp.float32).astype(
        jnp.bfloat16
    )
    key_rows = jnp.einsum("ald,de->ale", tokens, w_key, preferred_element_type=jnp.float32)
    key_rows = (key_rows * head_dim ** (-0.5)).astype(jnp.bfloat16)
    value_rows = jnp.einsum(
        "ald,de->ale", tokens, w_value, preferred_element_type=jnp.float32
    ).astype(jnp.bfloat16)
    silent = jnp.zeros((), jnp.bfloat16)
    key_rows = jnp.where(live_mask[:, :, None], key_rows, silent)
    value_rows = jnp.where(live_mask[:, :, None], value_rows, silent)
    query_blocks = queries.reshape(block_shape)
    key_blocks = key_rows.reshape(block_shape)
    value_blocks = value_rows.reshape(block_shape)
    within = jnp.cumsum(
        decay_rates.reshape(asset_count, head_count, blocks, SPAN), axis=-1
    ).transpose(0, 2, 1, 3)
    causal = jnp.arange(SPAN)[:, None] >= jnp.arange(SPAN)[None, :]
    scores = jnp.einsum(
        "anchd,anehd->anhce", query_blocks, key_blocks, preferred_element_type=jnp.float32
    )
    decay_gaps = jnp.where(causal, within[..., :, None] - within[..., None, :], 0.0)
    weights = jnp.where(causal, scores * jnp.exp(decay_gaps), 0.0).astype(jnp.bfloat16)
    inner_part = jnp.einsum(
        "anhce,anehd->anchd", weights, value_blocks, preferred_element_type=jnp.float32
    )
    block_ends = within[..., -1]
    tail_decay = jnp.exp(block_ends[..., None] - within).transpose(0, 1, 3, 2)
    decayed = (key_blocks.astype(jnp.float32) * tail_decay[..., None]).astype(jnp.bfloat16)
    pieces = jnp.einsum(
        "anchd,anche->anhde", decayed, value_blocks, preferred_element_type=jnp.float32
    )

    def advance(carried, inputs):
        block_end, block_piece = inputs
        return (jnp.exp(block_end)[..., None, None] * carried + block_piece, carried)

    empty_state = jnp.zeros((asset_count, head_count, head_dim, head_dim), jnp.float32)
    local_total, starts = lax.scan(
        advance, empty_state, (jnp.moveaxis(block_ends, 1, 0), jnp.moveaxis(pieces, 1, 0))
    )
    starts = jnp.moveaxis(starts, 0, 1)
    prior_decay = jnp.cumsum(block_ends, axis=1) - block_ends
    growth = jnp.sum(block_ends, axis=1)
    return (query_blocks, inner_part, within, starts, prior_decay, growth, local_total)


def link_states(earlier, later_part):
    return (
        earlier[0] + later_part[0],
        jnp.exp(later_part[0])[..., None, None] * earlier[1] + later_part[1],
    )


def on_device(tokens, w_query, w_key, w_value, decay_log, lengths, sources, targets, stash, whiten):
    asset_count, step_count, model_width = tokens.shape
    head_count = decay_log.shape[1]
    head_dim = model_width // head_count
    seq_count = lax.axis_size("seq")
    seq_rank = lax.axis_index("seq")
    own_rows = head_dim // seq_count
    owned_ids = lax.axis_index("asset") * asset_count + jnp.arange(asset_count, dtype=jnp.int32)
    positions = seq_rank * step_count + jnp.arange(step_count, dtype=jnp.int32)
    live_mask = positions[None, :] < lengths[:, None]
    decay_rates = jnp.where(live_mask[:, None, :], decay_log, 0.0)
    gathered = lax.all_gather(stash, "asset", axis=0, tiled=True)
    picked = jnp.take(gathered, jnp.take(sources, owned_ids), axis=0)
    start_state = lax.all_gather(picked, "seq", axis=2, tiled=True)
    operands = (tokens, decay_rates, live_mask, w_query, w_key, w_value)
    outcome = local_pass(*operands)
    query_blocks, inner_part, within, starts, prior_decay, growth, local_total = outcome
    before, handed = entering(
        (growth, local_total),
        "seq",
        link_states,
        (jnp.zeros_like(growth), jnp.zeros_like(local_total)),
    )
    carry_in = jnp.exp(before)[..., None, None] * start_state + handed
    closing = jnp.exp(growth)[..., None, None] * carry_in + local_total
    broadcast_state = broadcast(closing, "seq", seq_count - 1)
    final_rows = lax.dynamic_slice_in_dim(broadcast_state, seq_rank * own_rows, own_rows, 2)
    everyone = lax.all_gather(final_rows, "asset", axis=0, tiled=True)
    matches = (targets[None, :] == owned_ids[:, None]).astype(jnp.int32)
    anchor = jnp.argmax(matches, axis=1)
    kept_states = jnp.take(everyone, anchor, axis=0)
    block_state = starts + jnp.exp(prior_decay)[..., None, None] * carry_in[:, None]
    query_float = query_blocks.astype(jnp.float32)
    cross_part = jnp.einsum(
        "anchd,anhde->anche", query_float, block_state, precision=HIGHEST_PRECISION
    )
    retained = inner_part + cross_part * jnp.exp(within).transpose(0, 1, 3, 2)[..., None]
    retained = retained.reshape(asset_count, step_count, head_count, head_dim)
    average = jnp.mean(retained, axis=-1, keepdims=True)
    centered = retained - average
    spread = jnp.mean(centered * centered, axis=-1, keepdims=True)
    normed = jnp.where(live_mask[:, :, None, None], centered * lax.rsqrt(spread + EPSILON), 0.0)
    normed = normed.reshape(asset_count, step_count, model_width).astype(jnp.bfloat16)
    features = jnp.einsum(
        "ald,ade->ale", normed, whiten, preferred_element_type=jnp.float32
    ).astype(jnp.bfloat16)
    return (features, kept_states)


def solution(mesh):
    return jax.shard_map(
        on_device,
        mesh=mesh,
        in_specs=(
            P("asset", "seq", None),
            P(),
            P(),
            P(),
            P("asset", None, "seq"),
            P("asset"),
            P(),
            P(),
            P("asset", None, "seq", None),
            P("asset", None, None),
        ),
        out_specs=(P("asset", "seq", None), P("asset", None, "seq", None)),
        check_vma=False,
    )
```

profile of v0, /device:TPU:1, one launch (start us, length us, event | category | flops | bytes accessed | tf_op | source)
XLA Modules:
  0.0 286.3 jit_solution(9099652103553079799)
XLA Ops:
  10.2 2.5 fusion.17
  12.7 1.3 copy.51
  14.0 2.5 copy.36
  16.5 3.2 %fusion.19 = bf16[64,8,8,128]{3,1,2,0:T(8,128)(2,1)S(1)} fusion(bf16[1024,1024]{1,0:T(8,128)(2,1)} %param.19, bf16[1,512,1024]{2,1,0:T(8,128)(2,1)} %param.16, pred[512]{0:T(512)(128)(4,1)S(1)} %add_compare_fusion), kind=kOutput, calls=%fused_computation.32 | convolution fusion | flops 1074790400 | bytes 4194816 | tf_op jit(solution)/shard_map/ald,de->ale/dot_general | solution.py:42
  19.6 1.3 copy.49
  20.9 3.3 %convolution_bitcast_fusion = f32[4,1,8,128,128]{4,3,2,1,0:T(8,128)} fusion(bf16[4,128,8,128]{1,3,2,0:T(8,128)(2,1)} %copy.36, f32[4,128,8]{1,2,0:T(8,128)S(1)} %get-tuple-element.173, bf16[4,128,8,128]{3,2,1,0:T(8,128)(2,1)} %bitcast.135), kind=kOutput, calls=%fused_computation.22 | convolution fusion | flops 135790592 | bytes 4210688 | tf_op jit(solution)/shard_map/anchd,anche->anhde/dot_general | solution.py:66
  24.2 8.1 %while.28 = (s32[]{:T(128)}, f32[1,8,128,128]{3,2,1,0:T(8,128)S(1)}, f32[4,1,8,128,128]{4,3,2,1,0:T(8,128)}, f32[4,1,8]{2,1,0:T(1,128)S(1)}, f32[4,1,8,128,128]{4,3,2,1,0:T(8,128)}, /*index=5*/s32[]{:T(128)}, s32[]{:T(128)}) while((s32[]{:T(128)}, f32[1,8,128,128]{3,2,1,0:T(8,128)S(1)}, f32[4,1,8,128,128]{4,3,2,1,0:T(8,128)}, ...), condition=%wide.region_2.3_spmd.clone, body=%wide.region_1.2_spmd.clone.sunk | while | flops 524291 | bytes 2622144 | solution.py:75
  25.1 1.2 bitcast_add_fusion.12
  27.1 1.2 bitcast_add_fusion.12
  29.1 1.2 bitcast_add_fusion.12
  38.9 34.5 %all-reduce = f32[128]{0:T(128)S(1)} all-reduce(f32[128]{0:T(128)S(1)} %dynamic-update-slice.2), channel_id=2, replica_groups=mesh['seq'=16,'asset'=16] {'seq'}, use_global_device_ids=true, to_apply=%add | all-reduce | flops 128 | bytes 1024
  73.5 3.2 %fusion.11 = bf16[64,8,8,128]{3,1,2,0:T(8,128)(2,1)S(1)} fusion(bf16[1024,1024]{1,0:T(8,128)(2,1)} %param.17, bf16[1,512,1024]{2,1,0:T(8,128)(2,1)} %param.16), kind=kOutput, calls=%fused_computation.26 | convolution fusion | flops 1074266112 | bytes 4194304 | tf_op jit(solution)/shard_map/ald,de->ale/dot_general | solution.py:37
  76.7 1.3 copy.50
  78.0 29.1 %all_gather.25 = f32[16,8,8,128]{3,2,1,0:T(8,128)S(1)} all-gather(f32[1,8,8,128]{3,2,1,0:T(8,128)S(1)} %copy-done.5), channel_id=1, replica_groups=mesh['seq'=16,'asset'=16] {'asset'}, dimensions={0}, use_global_device_ids=true | all-gather | bytes 557056 | tf_op jit(solution)/shard_map/all_gather | solution.py:102
  107.1 18.9 %all_gather.26 = f32[1,8,128,128]{3,2,1,0:T(8,128)} all-gather(f32[1,8,8,128]{3,2,1,0:T(8,128)S(1)} %dynamic-slice_select_fusion.1), channel_id=1, replica_groups=mesh['seq'=16,'asset'=16] {'seq'}, dimensions={2}, use_global_device_ids=true | all-gather | bytes 557056 | tf_op jit(solution)/shard_map/all_gather | solution.py:104
  126.0 4.4 %fusion.15 = f32[4,8,128,128]{3,2,1,0:T(8,128)} fusion(bf16[4,128,8,128]{1,3,2,0:T(8,128)(2,1)} %copy.36, f32[4,8,128]{2,1,0:T(8,128)S(1)} %bitcast.139, pred[128,128]{1,0:T(8,128)(4,1)S(1)} %iota_compare_fusion, bf16[4,128,8,128]{3,2,1,0:T(8,128)(2,1)} %bitcast.136, bf16[4,128,8,128]{3,2,1,0:T(8,128)(2,1)} %bitcast.132), kind=kOutput, calls=%fused_computation.28 | convolution fusion | flops 271056896 | bytes 5275648 | tf_op jit(solution)/shard_map/anhce,anehd->anchd/dot_general | solution.py:60
  131.5 2.0 add_select_fusion
  133.6 5.6 %fusion.45 = (f32[4,128,8]{1,2,0:T(8,128)S(1)}, f32[1,4,128,8,128]{2,4,3,1,0:T(8,128)}) fusion(f32[4,128,8]{1,2,0:T(8,128)S(1)} %get-tuple-element.172, bf16[4,128,8,128]{3,2,1,0:T(8,128)(2,1)S(1)} %bitcast.133, f32[4,1,8,128,128]{4,3,2,1,0:T(8,128)} %get-tuple-element.66, f32[8,128,128]{2,1,0:T(8,128)S(1)} %get-tuple-element.169, ...), kind=kOutput, calls=%fused_computation.74 | convolution fusion | flops 807923712 | bytes 7897216 | tf_op jit(solution)/shard_map/anchd,anhde->anche/dot_general | solution.py:124
  139.2 2.9 %copy.44 = f32[1,4,128,8,128]{4,3,0,2,1:T(8,128)} copy(f32[1,4,128,8,128]{2,4,3,1,0:T(8,128)} %get-tuple-element.175) | data formatting | bytes 4194304 | tf_op jit(solution)/shard_map/add | solution.py:127
  142.1 1.9 multiply_reduce_fusion
  145.9 4.4 %fusion.7 = bf16[1,512,1,1,1,1,1024]{6,0,1,5,4,3,2:T(2,128)(2,1)S(1)} fusion(f32[1,512,1,1,1,1,1024]{6,0,1,5,4,3,2:T(1,128)S(1)} %bitcast.130, f32[1,512,1,1,1,1,1024]{6,0,1,5,4,3,2:T(1,128)S(1)} %bitcast.129, f32[1,512,1,1,1,1,1024]{6,0,1,5,4,3,2:T(1,128)S(1)} %bitcast.131, pred[512]{0:T(512)(128)(4,1)S(1)} %add_compare_fusion), kind=kLoop, calls=%fused_computation.21 | loop fusion | flops 2097152 | bytes 7340544 | tf_op jit(solution)/shard_map/convert_element_type | solution.py:133
  150.4 2.2 fusion.12
  152.6 104.8 %all-reduce.3.cloned.1.call-done = f32[1,8,128,128]{3,2,1,0:T(8,128)} async-done(((f32[1,8,128,128]{3,2,1,0:T(8,128)}), f32[1,8,128,128]{3,2,1,0:T(8,128)}) %all-reduce.3.cloned.1.call-update) | async-done | bytes 524304 | tf_op jit(solution)/shard_map/psum | solution.py:28
  258.2 20.7 %all_gather.27 = f32[16,8,8,128]{3,2,1,0:T(8,128)S(1)} all-gather(f32[1,8,8,128]{3,2,1,0:T(8,128)S(1)} %constant_dynamic-slice_fusion.2), channel_id=1, replica_groups=mesh['seq'=16,'asset'=16] {'asset'}, dimensions={0}, use_global_device_ids=true | all-gather | bytes 557056 | tf_op jit(solution)/shard_map/all_gather | solution.py:118
  (64 shorter events, 14.3 us)
Async XLA Ops:
  7.2 3.0 %copy-start = (bf16[1024,1024]{1,0:T(8,128)(2,1)S(1)}, bf16[1024,1024]{1,0:T(8,128)(2,1)}, u32[]{:S(2)}) copy-start(bf16[1024,1024]{1,0:T(8,128)(2,1)} %param.18) | copy-start | bytes 6291460
  7.2 123.3 %all-gather.4.cloned.1.call-start = ((), (), s32[]{:S(2)}) async-start(), calls=%async_computation.1 | async-start | bytes 8912896 | tf_op jit(solution)/shard_map/all_gather | solution.py:15
  24.2 9.0 %copy-start.8 = (s32[16]{0:T(128)S(1)}, s32[16]{0:T(128)}, u32[]{:S(2)}) copy-start(s32[16]{0:T(128)} %param.22) | copy-start | bytes 196
  24.2 10.4 %copy-start.6 = (s32[16]{0:T(128)S(1)}, s32[16]{0:T(128)}, u32[]{:S(2)}) copy-start(s32[16]{0:T(128)} %param.23) | copy-start | bytes 196
  24.2 13.2 %copy-start.9 = (u32[256]{0:T(256)S(1)}, u32[256]{0:T(256)}, u32[]{:S(2)}) copy-start(u32[256]{0:T(256)} %constant.146) | copy-start | bytes 3076
  32.4 0.8 copy-start.1
  33.2 224.2 %all-reduce.3.cloned.1.call-start = ((), (), s32[]{:S(2)}) async-start(), calls=%async_computation | async-start | bytes 1048576 | tf_op jit(solution)/shard_map/psum | solution.py:28
  76.7 1.3 copy-start.5
  130.5 1.0 copy-start.2
  130.7 2.9 %copy-start.4 = (bf16[64,8,8,128]{3,2,1,0:T(8,128)(2,1)S(1)}, bf16[64,8,8,128]{3,2,1,0:T(8,128)(2,1)}, u32[]{:S(2)}) copy-start(bf16[64,8,8,128]{3,2,1,0:T(8,128)(2,1)} %copy.50) | copy-start | bytes 3145732
  144.3 1.6 copy-start.3
  145.9 4.5 %copy-start.7 = (bf16[1,1024,1024]{2,1,0:T(8,128)(2,1)S(1)}, bf16[1,1024,1024]{2,1,0:T(8,128)(2,1)}, u32[]{:S(2)}) copy-start(bf16[1,1024,1024]{2,1,0:T(8,128)(2,1)} %param.25) | copy-start | bytes 6291460
Sparse Core Ops, SparseCore 0:
  33.3 79.8 all-gather.3
  144.4 112.9 all-reduce.2
where the time goes:
time: 288 us; the launch traced here: 286 us
  waiting for transfers between devices  105 us (36%)
  blocking collectives  103 us (36%)
  matrix products  24.4 us (8%)
  other arithmetic  20 us (7%)
  between operations  18.4 us (6%)
  local copies, waits for them, and re-layouts  15 us (5%)
    psum x1, waiting for transfers between devices, broadcast(): return lax.psum(kept, axis)  105 us
    unnamed x1, blocking collectives  34.5 us
    all_gather x1, blocking collectives, on_device(): gathered = lax.all_gather(stash, 'asset', axis=0, tiled=True)  29.1 us
    all_gather x1, blocking collectives, on_device(): everyone = lax.all_gather(final_rows, 'asset', axis=0, tiled=True)  20.7 us
    all_gather x1, blocking collectives, on_device(): start_state = lax.all_gather(picked, 'seq', axis=2, tiled=True)  18.9 us
    unnamed x26, local copies, waits for them, and re-layouts  6.62 us
  transfers between devices with their start and end apart: 2, of which 1 were waited for; matrix products, arithmetic and copies ran while one was open for 7% of the time, Pallas kernels for 0%

commit v1 on v0

v1 whole, which is shorter than its diff:
```python
import functools
import jax
import jax.numpy as jnp
from jax import lax
from jax.experimental import pallas as pl
from jax.experimental.pallas import tpu as pltpu
from jax.sharding import PartitionSpec as P

HEADS = 8
DIM = 128
STEPS = 512
WIDTH = 1024
PAIR = 2 * DIM
HALF = 256
EPSILON = 1e-05
LOG2E = 1.4426950408889634
FAR = -1e30


def running_sum(rates):
    lane = lax.broadcasted_iota(jnp.int32, rates.shape, 1)
    shift = 1
    while shift < STEPS:
        moved = pltpu.roll(rates, shift, 1)
        rates = rates + jnp.where(lane >= shift, moved, 0.0)
        shift *= 2
    return rates


def keys_kernel(valid_ref, tokens_ref, w_key_ref, w_value_ref, decay_ref,
                total_ref, keys_ref, values_ref, sums_ref, live_tokens):
    pair = pl.program_id(0)
    valid = valid_ref[0] - lax.axis_index("seq") * STEPS

    @pl.when(pair == 0)
    def _():
        lane = lax.broadcasted_iota(jnp.int32, (HEADS, STEPS), 1)
        rates = jnp.where(lane < valid, decay_ref[...] * LOG2E, 0.0)
        sums = running_sum(rates)
        sums_ref[...] = sums
        growth = jnp.broadcast_to(sums[:, STEPS - 1:], (HEADS, DIM))
        total_ref[:, HEADS] = jnp.broadcast_to(growth[None], (16, HEADS, DIM))
        step = lax.broadcasted_iota(jnp.int32, (STEPS, DIM), 0)
        for g in range(WIDTH // DIM):
            part = tokens_ref[:, g * DIM:(g + 1) * DIM]
            live_tokens[:, g * DIM:(g + 1) * DIM] = jnp.where(
                step < valid, part.astype(jnp.float32), 0.0).astype(jnp.bfloat16)

    tokens = live_tokens[...]
    keys = jnp.dot(tokens, w_key_ref[...], preferred_element_type=jnp.float32)
    keys = (keys * DIM ** (-0.5)).astype(jnp.bfloat16)
    values = jnp.dot(tokens, w_value_ref[...], preferred_element_type=jnp.float32).astype(jnp.bfloat16)
    keys_t = keys.T
    keys_ref[...] = keys_t
    values_ref[...] = values
    for j in range(2):
        head = 2 * pair + j
        row = sums_ref[pl.ds(head, 1), :]
        tail = jnp.exp2(row[:, STEPS - 1:] - row)
        decayed = (keys_t[j * DIM:(j + 1) * DIM].astype(jnp.float32) * tail).astype(jnp.bfloat16)
        total = jnp.dot(decayed, values[:, j * DIM:(j + 1) * DIM], preferred_element_type=jnp.float32)
        total_ref[:, head] = total.reshape(16, 8, DIM)


def keys_call(valid, tokens, w_key, w_value, decay):
    return pl.pallas_call(
        keys_kernel,
        grid_spec=pltpu.PrefetchScalarGridSpec(
            num_scalar_prefetch=1,
            grid=(4,),
            in_specs=[
                pl.BlockSpec((STEPS, WIDTH), lambda i, s: (0, 0)),
                pl.BlockSpec((WIDTH, PAIR), lambda i, s: (0, i)),
                pl.BlockSpec((WIDTH, PAIR), lambda i, s: (0, i)),
                pl.BlockSpec((HEADS, STEPS), lambda i, s: (0, 0)),
            ],
            out_specs=[
                pl.BlockSpec((16, HEADS + 1, 8, DIM), lambda i, s: (0, 0, 0, 0)),
                pl.BlockSpec((PAIR, STEPS), lambda i, s: (i, 0)),
                pl.BlockSpec((STEPS, PAIR), lambda i, s: (0, i)),
                pl.BlockSpec((HEADS, STEPS), lambda i, s: (0, 0)),
            ],
            scratch_shapes=[pltpu.VMEM((STEPS, WIDTH), jnp.bfloat16)],
        ),
        out_shape=[
            jax.ShapeDtypeStruct((16, HEADS + 1, 8, DIM), jnp.float32),
            jax.ShapeDtypeStruct((WIDTH, STEPS), jnp.bfloat16),
            jax.ShapeDtypeStruct((STEPS, WIDTH), jnp.bfloat16),
            jax.ShapeDtypeStruct((HEADS, STEPS), jnp.float32),
        ],
        compiler_params=pltpu.CompilerParams(vmem_limit_bytes=40 * 1024 * 1024),
        cost_estimate=pl.CostEstimate(flops=2 * 2 * STEPS * WIDTH * WIDTH, bytes_accessed=8 * 2 ** 20, transcendentals=0),
        name="keys_values",
    )(valid, tokens, w_key, w_value, decay)


def inner_kernel(tokens_ref, w_query_ref, keys_ref, values_ref, sums_ref, queries_ref, inner_ref, columns):
    pair = pl.program_id(0)

    @pl.when(pair == 0)
    def _():
        columns[...] = jnp.concatenate([sums_ref[...], jnp.zeros((DIM - HEADS, STEPS), jnp.float32)], 0).T

    queries = jnp.dot(tokens_ref[...], w_query_ref[...], preferred_element_type=jnp.float32).astype(jnp.bfloat16)
    queries_ref[...] = queries
    turned = pltpu.roll(columns[...], (DIM - 2 * pair) % DIM, 1)
    causal = (lax.broadcasted_iota(jnp.int32, (DIM, DIM), 0)
              >= lax.broadcasted_iota(jnp.int32, (DIM, DIM), 1))
    for j in range(2):
        head = 2 * pair + j
        lanes = slice(j * DIM, (j + 1) * DIM)
        row = sums_ref[pl.ds(head, 1), :]
        column = jnp.broadcast_to(turned[:, j:j + 1], (STEPS, DIM))
        middle = row[:, HALF - 1:HALF]
        state = None
        for c in range(2):
            base = c * HALF
            k_t = keys_ref[lanes, base:base + HALF]
            v = values_ref[base:base + HALF, lanes]
            for s in range(2):
                rows = slice(base + s * DIM, base + (s + 1) * DIM)
                q = queries[rows, lanes]
                wide = (s + 1) * DIM
                scores = jnp.dot(q, k_t[:, :wide], preferred_element_type=jnp.float32)
                parts = []
                for b in range(s + 1):
                    gap = column[rows] - row[:, base + b * DIM:base + (b + 1) * DIM]
                    if b == s:
                        gap = jnp.where(causal, gap, FAR)
                    parts.append((scores[:, b * DIM:(b + 1) * DIM] * jnp.exp2(gap)).astype(jnp.bfloat16))
                weights = parts[0] if s == 0 else jnp.concatenate(parts, 1)
                part = jnp.dot(weights, v[:wide], preferred_element_type=jnp.float32)
                if c == 1:
                    cross = jnp.dot(jnp.concatenate([q, q], 1), state, preferred_element_type=jnp.float32)
                    part = part + cross * jnp.exp2(column[rows] - middle)
                inner_ref[rows, lanes] = part
            if c == 0:
                tail = jnp.exp2(middle - row[:, :HALF])
                decayed = (k_t.astype(jnp.float32) * tail).astype(jnp.bfloat16)
                state = split(jnp.dot(decayed, v, preferred_element_type=jnp.float32))


def split(state):
    high = state.astype(jnp.bfloat16)
    low = (state - high.astype(jnp.float32)).astype(jnp.bfloat16)
    return jnp.concatenate([high, low], 0)


def inner_call(tokens, w_query, keys, values, sums):
    return pl.pallas_call(
        inner_kernel,
        grid=(4,),
        in_specs=[
            pl.BlockSpec((STEPS, WIDTH), lambda i: (0, 0)),
            pl.BlockSpec((WIDTH, PAIR), lambda i: (0, i)),
            pl.BlockSpec((PAIR, STEPS), lambda i: (i, 0)),
            pl.BlockSpec((STEPS, PAIR), lambda i: (0, i)),
            pl.BlockSpec((HEADS, STEPS), lambda i: (0, 0)),
        ],
        out_specs=[
            pl.BlockSpec((STEPS, PAIR), lambda i: (0, i)),
            pl.BlockSpec((STEPS, PAIR), lambda i: (0, i)),
        ],
        out_shape=[
            jax.ShapeDtypeStruct((STEPS, WIDTH), jnp.bfloat16),
            jax.ShapeDtypeStruct((STEPS, WIDTH), jnp.float32),
        ],
        scratch_shapes=[pltpu.VMEM((STEPS, DIM), jnp.float32)],
        compiler_params=pltpu.CompilerParams(vmem_limit_bytes=40 * 1024 * 1024),
        cost_estimate=pl.CostEstimate(flops=2 * STEPS * WIDTH * WIDTH * 3 // 2, bytes_accessed=8 * 2 ** 20, transcendentals=0),
        name="queries_inner",
    )(tokens, w_query, keys, values, sums)


def scan_kernel(received_ref, start_ref, carried_ref, closing_ref):
    for head in range(HEADS):
        state = start_ref[head]
        for shard in range(16):
            carried_ref[shard, head] = state
            growth = jnp.exp2(received_ref[shard, HEADS, head:head + 1, :])
            state = growth * state + received_ref[shard, head]
        closing_ref[head] = state


def scan_call(received, start):
    return pl.pallas_call(
        scan_kernel,
        out_shape=[
            jax.ShapeDtypeStruct((16, HEADS, 8, DIM), jnp.float32),
            jax.ShapeDtypeStruct((HEADS, 8, DIM), jnp.float32),
        ],
        compiler_params=pltpu.CompilerParams(vmem_limit_bytes=40 * 1024 * 1024),
        cost_estimate=pl.CostEstimate(flops=2 ** 20, bytes_accessed=2 ** 20, transcendentals=0),
        name="scan_rows",
    )(received, start)


ROWS = 256


def outer_kernel(valid_ref, queries_ref, inner_ref, state_ref, sums_ref, whiten_ref, features_ref, normed, states, columns):
    strip = pl.program_id(0)
    valid = valid_ref[0] - lax.axis_index("seq") * STEPS

    @pl.when(strip == 0)
    def _():
        for head in range(HEADS):
            states[head] = split(state_ref[:, head].reshape(DIM, DIM))
        columns[...] = jnp.concatenate([sums_ref[...], jnp.zeros((DIM - HEADS, STEPS), jnp.float32)], 0).T

    base = pl.multiple_of(strip * ROWS, ROWS)
    column = columns[pl.ds(base, ROWS), :]
    column = jnp.exp2(column)
    step = base + lax.broadcasted_iota(jnp.int32, (ROWS, DIM), 0)
    alive = step < valid
    for head in range(HEADS):
        lanes = slice(head * DIM, (head + 1) * DIM)
        q = queries_ref[:, lanes]
        cross = jnp.dot(jnp.concatenate([q, q], 1), states[head], preferred_element_type=jnp.float32)
        retained = inner_ref[:, lanes] + cross * column[:, head:head + 1]
        average = jnp.mean(retained, axis=1, keepdims=True)
        centered = retained - average
        spread = jnp.mean(centered * centered, axis=1, keepdims=True)
        out = centered * lax.rsqrt(spread + EPSILON)
        normed[:, lanes] = jnp.where(alive, out, 0.0).astype(jnp.bfloat16)
    features_ref[...] = jnp.dot(normed[...], whiten_ref[...], preferred_element_type=jnp.float32).astype(jnp.bfloat16)


def outer_call(valid, queries, inner, state, sums, whiten):
    return pl.pallas_call(
        outer_kernel,
        grid_spec=pltpu.PrefetchScalarGridSpec(
            num_scalar_prefetch=1,
            grid=(STEPS // ROWS,),
            in_specs=[
                pl.BlockSpec((ROWS, WIDTH), lambda i, s: (i, 0)),
                pl.BlockSpec((ROWS, WIDTH), lambda i, s: (i, 0)),
                pl.BlockSpec((16, HEADS, 8, DIM), lambda i, s: (0, 0, 0, 0)),
                pl.BlockSpec((HEADS, STEPS), lambda i, s: (0, 0)),
                pl.BlockSpec((WIDTH, WIDTH), lambda i, s: (0, 0)),
            ],
            out_specs=pl.BlockSpec((ROWS, WIDTH), lambda i, s: (i, 0)),
            scratch_shapes=[
                pltpu.VMEM((ROWS, WIDTH), jnp.bfloat16),
                pltpu.VMEM((HEADS, PAIR, DIM), jnp.bfloat16),
                pltpu.VMEM((STEPS, DIM), jnp.float32),
            ],
        ),
        out_shape=jax.ShapeDtypeStruct((STEPS, WIDTH), jnp.bfloat16),
        compiler_params=pltpu.CompilerParams(vmem_limit_bytes=40 * 1024 * 1024),
        cost_estimate=pl.CostEstimate(flops=2 * STEPS * WIDTH * WIDTH * 3 // 2, bytes_accessed=8 * 2 ** 20, transcendentals=0),
        name="outer_whiten",
    )(valid, queries, inner, state, sums, whiten)


def select_kernel(count, choose, *refs):
    route_ref, items, out_ref = refs[0], refs[1:-1], refs[-1]
    for slot, number in enumerate(choose(route_ref)):
        for k, (ref, at) in enumerate(listed(items)):
            @pl.when(number == k)
            def _(ref=ref, at=at):
                out_ref[slot] = ref[at]


def listed(items):
    return [(ref, at) for ref in items for at in range(ref.shape[0])]


def select_call(name, choose, count, route, *items):
    return pl.pallas_call(
        functools.partial(select_kernel, count, choose),
        in_specs=[pl.BlockSpec(memory_space=pltpu.SMEM)] + [pl.BlockSpec(memory_space=pltpu.VMEM)] * len(items),
        out_specs=pl.BlockSpec(memory_space=pltpu.VMEM),
        out_shape=jax.ShapeDtypeStruct((count, HEADS, 8, DIM), jnp.float32),
        cost_estimate=pl.CostEstimate(flops=1024, bytes_accessed=2 ** 17, transcendentals=0),
        name=name,
    )(route, *items)


def giver(inverted, route_ref, slot):
    if not inverted:
        return route_ref[slot]
    found = jnp.int32(0)
    for k in range(1, 16):
        found = jnp.where(route_ref[k] == slot, k, found)
    return found


def third_hop(inverted, route_ref):
    me = lax.axis_index("asset")
    return [(giver(inverted, route_ref, me ^ 4 ^ (8 * t)) ^ me) & 3 for t in range(2)]


def fourth_hop(inverted, route_ref):
    me = lax.axis_index("asset")
    source = giver(inverted, route_ref, me ^ 8)
    return [jnp.where((source >> 2) == (me >> 2), (source ^ me) & 3, 5)]


def arrival(inverted, route_ref):
    me = lax.axis_index("asset")
    source = giver(inverted, route_ref, me)
    near = jnp.where((source >> 2) == (me >> 2), (source ^ me) & 3, 4)
    return [jnp.where((source >> 3) == (me >> 3), near, 6)]


def swap(value, bit):
    return lax.ppermute(value, "asset", [(k, k ^ bit) for k in range(16)])


def on_device(tokens, w_query, w_key, w_value, decay_log, lengths, sources, targets, stash, whiten):
    tokens, decay, whiten = tokens[0], decay_log[0], whiten[0]
    own = stash
    one = swap(own, 1)
    pair = jnp.concatenate([own, one], 0)
    total, keys, values, sums = keys_call(lengths, tokens, w_key, w_value, decay)
    two = swap(pair, 2)
    third = select_call("hop_three", functools.partial(third_hop, False), 2, sources, own, one, two)
    four = swap(third, 4)
    fourth = select_call("hop_four", functools.partial(fourth_hop, False), 1, sources, own, one, two, four)
    eight = swap(fourth, 8)
    received = lax.all_to_all(total, "seq", 0, 0, tiled=True)
    queries, inner = inner_call(tokens, w_query, keys, values, sums)
    start = select_call("arrived", functools.partial(arrival, False), 1, sources, own, one, two, four, eight)
    carried, closing = scan_call(received, start[0])
    own = closing[None]
    one = swap(own, 1)
    pair = jnp.concatenate([own, one], 0)
    two = swap(pair, 2)
    state = lax.all_to_all(carried, "seq", 0, 0, tiled=True)
    third = select_call("hop_three", functools.partial(third_hop, True), 2, targets, own, one, two)
    four = swap(third, 4)
    fourth = select_call("hop_four", functools.partial(fourth_hop, True), 1, targets, own, one, two, four)
    eight = swap(fourth, 8)
    features = outer_call(lengths, queries, inner, state, sums, whiten)
    kept = select_call("arrived", functools.partial(arrival, True), 1, targets, own, one, two, four, eight)
    return (features[None], kept)


def solution(mesh):
    return jax.shard_map(
        on_device,
        mesh=mesh,
        in_specs=(
            P("asset", "seq", None),
            P(),
            P(),
            P(),
            P("asset", None, "seq"),
            P("asset"),
            P(),
            P(),
            P("asset", None, "seq", None),
            P("asset", None, None),
        ),
        out_specs=(P("asset", "seq", None), P("asset", None, "seq", None)),
        check_vma=False,
    )
```

time: 288 us -> 109 us (0.38)
  the two profiles are of different devices: /device:TPU:1 before, /device:TPU:2 now
where the time goes in v1:
time: 109 us; the launch traced here: 108 us
  starting transfers between devices  35.5 us (33%)
  Pallas kernels  31.2 us (29%)
  local copies, waits for them, and re-layouts  22 us (20%)
  waiting for transfers between devices  17.7 us (16%)
  between operations  1.37 us (1%)
    unnamed x52, local copies, waits for them, and re-layouts  22 us
    ppermute x8, starting transfers between devices, swap(): return lax.ppermute(value, 'asset', [(k, k ^ bit) for k in range(16)])  20.7 us
    ppermute x8, waiting for transfers between devices, swap(): return lax.ppermute(value, 'asset', [(k, k ^ bit) for k in range(16)])  17.7 us
    pallas_call x6, Pallas kernels, select_call(): pl.pallas_call(functools.partial(select_kernel, count, choose), in_specs=...  9.44 us
    pallas_call x1, Pallas kernels, inner_call(): pl.pallas_call(inner_kernel, grid=(4,), in_specs=[pl.BlockSpec((STEPS, WI...  8.77 us
    all_to_all x1, starting transfers between devices, on_device(): received = lax.all_to_all(total, 'seq', 0, 0, tiled=True)  7.48 us
    all_to_all x1, starting transfers between devices, on_device(): state = lax.all_to_all(carried, 'seq', 0, 0, tiled=True)  7.23 us
    pallas_call x1, Pallas kernels, keys_call(): pl.pallas_call(keys_kernel, grid_spec=pltpu.PrefetchScalarGridSpec(num_sc...  6.57 us
  transfers between devices with their start and end apart: 10, of which 7 were waited for; matrix products, arithmetic and copies ran while one was open for 0% of the time, Pallas kernels for 17%

profile of v1, /device:TPU:2, one launch (start us, length us, event | category | flops | bytes accessed | tf_op | source)
XLA Modules:
  0.0 107.7 jit_solution(12507174395423080307)
XLA Ops:
  1.3 1.6 %copy-done.7 = bf16[1024,1024]{1,0:T(8,128)(2,1)S(1)} copy-done((bf16[1024,1024]{1,0:T(8,128)(2,1)S(1)}, bf16[1024,1024]{1,0:T(8,128)(2,1)}, u32[]{:S(2)}) %copy-start.7) | copy-done | bytes 2097176
  2.9 1.6 %copy-done.8 = bf16[1024,1024]{1,0:T(8,128)(2,1)S(1)} copy-done((bf16[1024,1024]{1,0:T(8,128)(2,1)S(1)}, bf16[1024,1024]{1,0:T(8,128)(2,1)}, u32[]{:S(2)}) %copy-start.8) | copy-done | bytes 2097176
  6.4 6.6 %keys_values.1 = (f32[16,9,8,128]{3,2,1,0:T(8,128)}, bf16[1024,512]{1,0:T(8,128)(2,1)S(1)}, bf16[512,1024]{1,0:T(8,128)(2,1)S(1)}, f32[8,512]{1,0:T(8,128)S(1)}) custom-call(s32[1]{0:T(128)S(6)} %copy.12.valid_ref, bf16[512,1024]{1,0:T(8,128)(2,1)S(1)} %bitcast.13, bf16[1024,1024]{1,0:T(8,128)(2,1)S(1)} %copy-done.7, bf16[1024,1024]{1,0:T(8,128)(2,1)S(1)} %copy-done.8, ...), custom_call_target="tpu_custom_call" | custom-call | flops 2147483648 | bytes 8388608 | tf_op jit(solution)/shard_map/keys_values/pallas_call | solution.py:66
  14.9 7.5 %all-to-all-start = ((f32[16,9,8,128]{3,2,1,0:T(8,128)}), f32[16,9,8,128]{3,2,1,0:T(8,128)S(1)}, u32[]{:S(2)}, u32[]{:S(2)}) async-start(f32[16,9,8,128]{3,2,1,0:T(8,128)} %get-tuple-element.15), calls=%async_computation | async-start | bytes 1179648 | tf_op jit(solution)/shard_map/all_to_all | solution.py:322
  23.7 2.0 %collective-permute-start.1 = (f32[2,8,8,128]{3,2,1,0:T(8,128)S(1)}, f32[2,8,8,128]{3,2,1,0:T(8,128)S(1)}, u32[]{:S(2)}, u32[]{:S(2)}) collective-permute-start(f32[2,8,8,128]{3,2,1,0:T(8,128)S(1)} %pad_maximum_fusion), channel_id=1, source_target_pairs={{0,2},{1,3},{2,0},{3,1},{4,6},{5,7},{6,4},{7,5},{8,10},{9,11},{10,... | collective-permute-start | bytes 196616 | tf_op jit(solution)/shard_map/ppermute | solution.py:308
  25.7 2.4 %collective-permute-done.1.refs_3_ = f32[2,8,8,128]{3,2,1,0:T(8,128)S(1)} collective-permute-done((f32[2,8,8,128]{3,2,1,0:T(8,128)S(1)}, f32[2,8,8,128]{3,2,1,0:T(8,128)S(1)}, u32[]{:S(2)}, u32[]{:S(2)}) %collective-permute-start.1) | collective-permute-done | bytes 65568 | tf_op jit(solution)/shard_map/ppermute | solution.py:308
  30.3 3.3 %collective-permute-start.2 = (f32[2,8,8,128]{3,2,1,0:T(8,128)}, f32[2,8,8,128]{3,2,1,0:T(8,128)S(1)}, u32[]{:S(2)}, u32[]{:S(2)}) collective-permute-start(f32[2,8,8,128]{3,2,1,0:T(8,128)} %hop_three.2), channel_id=1, source_target_pairs={{0,4},{1,5},{2,6},{3,7},{4,0},{5,1},{6,2},{7,3},{8,12},{9,13},{10,... | collective-permute-start | bytes 196616 | tf_op jit(solution)/shard_map/ppermute | solution.py:308
  33.5 3.1 %collective-permute-done.2.refs_4_ = f32[2,8,8,128]{3,2,1,0:T(8,128)S(1)} collective-permute-done((f32[2,8,8,128]{3,2,1,0:T(8,128)}, f32[2,8,8,128]{3,2,1,0:T(8,128)S(1)}, u32[]{:S(2)}, u32[]{:S(2)}) %collective-permute-start.2) | collective-permute-done | bytes 65568 | tf_op jit(solution)/shard_map/ppermute | solution.py:308
  37.2 1.6 %hop_four.2 = f32[1,8,8,128]{3,2,1,0:T(8,128)} custom-call(s32[16]{0:T(128)} %refs_0_.8, f32[1,8,8,128]{3,2,1,0:T(8,128)} %refs_1_.5, f32[1,8,8,128]{3,2,1,0:T(8,128)} %copy-done.21, f32[2,8,8,128]{3,2,1,0:T(8,128)} %copy-done.18, f32[2,8,8,128]{3,2,1,0:T(8,128)} %copy-done.23), custom_call_target="tpu_custom_call" | custom-call | flops 1024 | bytes 131072 | tf_op jit(solution)/shard_map/hop_four/pallas_call | solution.py:270
  38.8 6.9 %collective-permute-start.3 = (f32[1,8,8,128]{3,2,1,0:T(8,128)}, f32[1,8,8,128]{3,2,1,0:T(8,128)S(1)}, u32[]{:S(2)}, u32[]{:S(2)}) collective-permute-start(f32[1,8,8,128]{3,2,1,0:T(8,128)} %hop_four.2), channel_id=1, source_target_pairs={{0,8},{1,9},{2,10},{3,11},{4,12},{5,13},{6,14},{7,15},{8,0},{9,1},... | collective-permute-start | bytes 98312 | tf_op jit(solution)/shard_map/ppermute | solution.py:308
  45.7 2.1 %collective-permute-done.3.refs_5_ = f32[1,8,8,128]{3,2,1,0:T(8,128)S(1)} collective-permute-done((f32[1,8,8,128]{3,2,1,0:T(8,128)}, f32[1,8,8,128]{3,2,1,0:T(8,128)S(1)}, u32[]{:S(2)}, u32[]{:S(2)}) %collective-permute-start.3) | collective-permute-done | bytes 32800 | tf_op jit(solution)/shard_map/ppermute | solution.py:308
  48.4 1.6 %arrived.2 = f32[1,8,8,128]{3,2,1,0:T(8,128)} custom-call(s32[16]{0:T(128)} %refs_0_.8, f32[1,8,8,128]{3,2,1,0:T(8,128)} %refs_1_.5, f32[1,8,8,128]{3,2,1,0:T(8,128)} %copy-done.21, f32[2,8,8,128]{3,2,1,0:T(8,128)} %copy-done.18, f32[2,8,8,128]{3,2,1,0:T(8,128)} %copy-done.23, f32[1,8,8,128]{3,2,1,0:T(8,128)} %copy-done.25), custom_call_target="tpu_custom_call" | custom-call | flops 1024 | bytes 131072 | tf_op jit(solution)/shard_map/arrived/pallas_call | solution.py:270
  51.7 7.2 %all-to-all-start.1 = ((f32[16,8,8,128]{3,2,1,0:T(8,128)}), f32[16,8,8,128]{3,2,1,0:T(8,128)S(1)}, u32[]{:S(2)}, u32[]{:S(2)}) async-start(f32[16,8,8,128]{3,2,1,0:T(8,128)} %get-tuple-element.16), calls=%async_computation.1 | async-start | bytes 1048576 | tf_op jit(solution)/shard_map/all_to_all | solution.py:330
  60.8 3.6 %collective-permute-done.5.refs_3_ = f32[2,8,8,128]{3,2,1,0:T(8,128)S(1)} collective-permute-done((f32[2,8,8,128]{3,2,1,0:T(8,128)S(1)}, f32[2,8,8,128]{3,2,1,0:T(8,128)S(1)}, u32[]{:S(2)}, u32[]{:S(2)}) %collective-permute-start.5) | collective-permute-done | bytes 65568 | tf_op jit(solution)/shard_map/ppermute | solution.py:308
  65.1 1.6 %hop_three.3 = f32[2,8,8,128]{3,2,1,0:T(8,128)} custom-call(s32[16]{0:T(128)} %refs_0_.11, f32[1,8,8,128]{3,2,1,0:T(8,128)} %bitcast.9, f32[1,8,8,128]{3,2,1,0:T(8,128)} %copy-done.20, f32[2,8,8,128]{3,2,1,0:T(8,128)} %copy-done.17), custom_call_target="tpu_custom_call" | custom-call | flops 1024 | bytes 131072 | tf_op jit(solution)/shard_map/hop_three/pallas_call | solution.py:270
  66.7 1.9 %collective-permute-start.6 = (f32[2,8,8,128]{3,2,1,0:T(8,128)}, f32[2,8,8,128]{3,2,1,0:T(8,128)S(1)}, u32[]{:S(2)}, u32[]{:S(2)}) collective-permute-start(f32[2,8,8,128]{3,2,1,0:T(8,128)} %hop_three.3), channel_id=1, source_target_pairs={{0,4},{1,5},{2,6},{3,7},{4,0},{5,1},{6,2},{7,3},{8,12},{9,13},{10,... | collective-permute-start | bytes 196616 | tf_op jit(solution)/shard_map/ppermute | solution.py:308
  68.6 4.1 %collective-permute-done.6.refs_4_ = f32[2,8,8,128]{3,2,1,0:T(8,128)S(1)} collective-permute-done((f32[2,8,8,128]{3,2,1,0:T(8,128)}, f32[2,8,8,128]{3,2,1,0:T(8,128)S(1)}, u32[]{:S(2)}, u32[]{:S(2)}) %collective-permute-start.6) | collective-permute-done | bytes 65568 | tf_op jit(solution)/shard_map/ppermute | solution.py:308
  73.4 1.6 %hop_four.3 = f32[1,8,8,128]{3,2,1,0:T(8,128)} custom-call(s32[16]{0:T(128)} %refs_0_.11, f32[1,8,8,128]{3,2,1,0:T(8,128)} %bitcast.10, f32[1,8,8,128]{3,2,1,0:T(8,128)} %copy-done.20, f32[2,8,8,128]{3,2,1,0:T(8,128)} %copy-done.17, f32[2,8,8,128]{3,2,1,0:T(8,128)} %copy-done.22), custom_call_target="tpu_custom_call" | custom-call | flops 1024 | bytes 131072 | tf_op jit(solution)/shard_map/hop_four/pallas_call | solution.py:270
  74.9 5.8 %collective-permute-start.7 = (f32[1,8,8,128]{3,2,1,0:T(8,128)}, f32[1,8,8,128]{3,2,1,0:T(8,128)S(1)}, u32[]{:S(2)}, u32[]{:S(2)}) collective-permute-start(f32[1,8,8,128]{3,2,1,0:T(8,128)} %hop_four.3), channel_id=1, source_target_pairs={{0,8},{1,9},{2,10},{3,11},{4,12},{5,13},{6,14},{7,15},{8,0},{9,1},... | collective-permute-start | bytes 98312 | tf_op jit(solution)/shard_map/ppermute | solution.py:308
  80.7 1.6 %copy-done.9 = bf16[1024,1024]{1,0:T(8,128)(2,1)S(1)} copy-done((bf16[1024,1024]{1,0:T(8,128)(2,1)S(1)}, bf16[1024,1024]{1,0:T(8,128)(2,1)}, u32[]{:S(2)}) %copy-start.9) | copy-done | bytes 2097176
  86.0 8.8 %queries_inner.1 = (bf16[512,1024]{1,0:T(8,128)(2,1)S(1)}, f32[512,1024]{1,0:T(8,128)S(1)}) custom-call(bf16[512,1024]{1,0:T(8,128)(2,1)S(1)} %bitcast.14, bf16[1024,1024]{1,0:T(8,128)(2,1)S(1)} %copy-done.9, bf16[1024,512]{1,0:T(8,128)(2,1)S(1)} %copy-done.14, bf16[512,1024]{1,0:T(8,128)(2,1)S(1)} %copy-done.16, f32[8,512]{1,0:T(8,128)S(1)} %get-tuple-element.12.sums_ref), custom_call_target="tpu_custom_call" | custom-call | flops 1610612736 | bytes 8388608 | tf_op jit(solution)/shard_map/queries_inner/pallas_call | solution.py:150
  97.7 1.6 %arrived.3 = f32[1,8,8,128]{3,2,1,0:T(8,128)} custom-call(s32[16]{0:T(128)} %refs_0_.11, f32[1,8,8,128]{3,2,1,0:T(8,128)} %bitcast.11, f32[1,8,8,128]{3,2,1,0:T(8,128)} %copy-done.20, f32[2,8,8,128]{3,2,1,0:T(8,128)} %copy-done.17, f32[2,8,8,128]{3,2,1,0:T(8,128)} %copy-done.22, f32[1,8,8,128]{3,2,1,0:T(8,128)} %copy-done.24), custom_call_target="tpu_custom_call" | custom-call | flops 1024 | bytes 131072 | tf_op jit(solution)/shard_map/arrived/pallas_call | solution.py:270
  99.3 1.6 %copy-done.2 = f32[512,1024]{1,0:T(8,128)S(1)} copy-done((f32[512,1024]{1,0:T(8,128)S(1)}, f32[512,1024]{1,0:T(8,128)}, u32[]{:S(2)}) %copy-start.2) | copy-done | bytes 2097176
  102.1 5.5 %outer_whiten.1 = bf16[512,1024]{1,0:T(8,128)(2,1)} custom-call(s32[1]{0:T(128)S(6)} %copy.12.valid_ref, bf16[512,1024]{1,0:T(8,128)(2,1)S(1)} %copy-done.4, f32[512,1024]{1,0:T(8,128)S(1)} %copy-done.2, f32[16,8,8,128]{3,2,1,0:T(8,128)S(1)} %all-to-all-done.1.state_ref, f32[8,512]{1,0:T(8,128)S(1)} %get-tuple-element.12.sums_ref, bf16[1024,1024]{1,0:T(8,128)(2,1)S(1)} %bitcast.6), custom_call_target="tpu_custom_call" | custom-call | flops 1610612736 | bytes 8388608 | tf_op jit(solution)/shard_map/outer_whiten/pallas_call | solution.py:230
  (60 shorter events, 21.3 us)
Async XLA Ops:
  1.3 1.6 %copy-start.7 = (bf16[1024,1024]{1,0:T(8,128)(2,1)S(1)}, bf16[1024,1024]{1,0:T(8,128)(2,1)}, u32[]{:S(2)}) copy-start(bf16[1024,1024]{1,0:T(8,128)(2,1)} %w_key_ref.1) | copy-start | bytes 6291460
  2.9 1.6 %copy-start.8 = (bf16[1024,1024]{1,0:T(8,128)(2,1)S(1)}, bf16[1024,1024]{1,0:T(8,128)(2,1)}, u32[]{:S(2)}) copy-start(bf16[1024,1024]{1,0:T(8,128)(2,1)} %w_value_ref.1) | copy-start | bytes 6291460
  4.5 1.2 %copy-start.10 = (bf16[1,512,1024]{2,1,0:T(8,128)(2,1)S(1)}, bf16[1,512,1024]{2,1,0:T(8,128)(2,1)}, u32[]{:S(2)}) copy-start(bf16[1,512,1024]{2,1,0:T(8,128)(2,1)} %param.10) | copy-start | bytes 3145732
  6.4 16.0 %copy-start.19 = (f32[1,8,8,128]{3,2,1,0:T(8,128)S(1)}, f32[1,8,8,128]{3,2,1,0:T(8,128)}, u32[]{:S(2)}) copy-start(f32[1,8,8,128]{3,2,1,0:T(8,128)} %refs_1_.5) | copy-start | bytes 98308
  14.9 35.1 %all-to-all-start = ((f32[16,9,8,128]{3,2,1,0:T(8,128)}), f32[16,9,8,128]{3,2,1,0:T(8,128)S(1)}, u32[]{:S(2)}, u32[]{:S(2)}) async-start(f32[16,9,8,128]{3,2,1,0:T(8,128)} %get-tuple-element.15), calls=%async_computation | async-start | bytes 1179648 | tf_op jit(solution)/shard_map/all_to_all | solution.py:322
  22.4 1.3 %collective-permute-start = (f32[1,8,8,128]{3,2,1,0:T(8,128)S(1)}, f32[1,8,8,128]{3,2,1,0:T(8,128)S(1)}, u32[]{:S(2)}, u32[]{:S(2)}) collective-permute-start(f32[1,8,8,128]{3,2,1,0:T(8,128)S(1)} %copy-done.19), channel_id=1, source_target_pairs={{0,1},{1,0},{2,3},{3,2},{4,5},{5,4},{6,7},{7,6},{8,9},{9,8},{10,11... | collective-permute-start | bytes 98312 | tf_op jit(solution)/shard_map/ppermute | solution.py:308
  23.7 4.4 %copy-start.21 = (f32[1,8,8,128]{3,2,1,0:T(8,128)}, f32[1,8,8,128]{3,2,1,0:T(8,128)S(1)}, u32[]{:S(2)}) copy-start(f32[1,8,8,128]{3,2,1,0:T(8,128)S(1)} %collective-permute-done.refs_2_) | copy-start | bytes 98308
  23.7 4.4 %collective-permute-start.1 = (f32[2,8,8,128]{3,2,1,0:T(8,128)S(1)}, f32[2,8,8,128]{3,2,1,0:T(8,128)S(1)}, u32[]{:S(2)}, u32[]{:S(2)}) collective-permute-start(f32[2,8,8,128]{3,2,1,0:T(8,128)S(1)} %pad_maximum_fusion), channel_id=1, source_target_pairs={{0,2},{1,3},{2,0},{3,1},{4,6},{5,7},{6,4},{7,5},{8,10},{9,11},{10,... | collective-permute-start | bytes 196616 | tf_op jit(solution)/shard_map/ppermute | solution.py:308
  30.3 6.3 %collective-permute-start.2 = (f32[2,8,8,128]{3,2,1,0:T(8,128)}, f32[2,8,8,128]{3,2,1,0:T(8,128)S(1)}, u32[]{:S(2)}, u32[]{:S(2)}) collective-permute-start(f32[2,8,8,128]{3,2,1,0:T(8,128)} %hop_three.2), channel_id=1, source_target_pairs={{0,4},{1,5},{2,6},{3,7},{4,0},{5,1},{6,2},{7,3},{8,12},{9,13},{10,... | collective-permute-start | bytes 196616 | tf_op jit(solution)/shard_map/ppermute | solution.py:308
  38.8 9.0 %collective-permute-start.3 = (f32[1,8,8,128]{3,2,1,0:T(8,128)}, f32[1,8,8,128]{3,2,1,0:T(8,128)S(1)}, u32[]{:S(2)}, u32[]{:S(2)}) collective-permute-start(f32[1,8,8,128]{3,2,1,0:T(8,128)} %hop_four.2), channel_id=1, source_target_pairs={{0,8},{1,9},{2,10},{3,11},{4,12},{5,13},{6,14},{7,15},{8,0},{9,1},... | collective-permute-start | bytes 98312 | tf_op jit(solution)/shard_map/ppermute | solution.py:308
  51.7 12.8 %copy-start.5 = (f32[8,8,128]{2,1,0:T(8,128)}, f32[8,8,128]{2,1,0:T(8,128)S(1)}, u32[]{:S(2)}) copy-start(f32[8,8,128]{2,1,0:T(8,128)S(1)} %get-tuple-element.17) | copy-start | bytes 98308
  51.7 47.7 %all-to-all-start.1 = ((f32[16,8,8,128]{3,2,1,0:T(8,128)}), f32[16,8,8,128]{3,2,1,0:T(8,128)S(1)}, u32[]{:S(2)}, u32[]{:S(2)}) async-start(f32[16,8,8,128]{3,2,1,0:T(8,128)} %get-tuple-element.16), calls=%async_computation.1 | async-start | bytes 1048576 | tf_op jit(solution)/shard_map/all_to_all | solution.py:330
  58.9 1.2 %collective-permute-start.4 = (f32[1,8,8,128]{3,2,1,0:T(8,128)S(1)}, f32[1,8,8,128]{3,2,1,0:T(8,128)S(1)}, u32[]{:S(2)}, u32[]{:S(2)}) collective-permute-start(f32[1,8,8,128]{3,2,1,0:T(8,128)S(1)} %bitcast.7), channel_id=1, source_target_pairs={{0,1},{1,0},{2,3},{3,2},{4,5},{5,4},{6,7},{7,6},{8,9},{9,8},{10,11... | collective-permute-start | bytes 98312 | tf_op jit(solution)/shard_map/ppermute | solution.py:308
  60.1 4.4 %copy-start.20 = (f32[1,8,8,128]{3,2,1,0:T(8,128)}, f32[1,8,8,128]{3,2,1,0:T(8,128)S(1)}, u32[]{:S(2)}) copy-start(f32[1,8,8,128]{3,2,1,0:T(8,128)S(1)} %collective-permute-done.4.refs_2_) | copy-start | bytes 98308
  60.1 4.4 %collective-permute-start.5 = (f32[2,8,8,128]{3,2,1,0:T(8,128)S(1)}, f32[2,8,8,128]{3,2,1,0:T(8,128)S(1)}, u32[]{:S(2)}, u32[]{:S(2)}) collective-permute-start(f32[2,8,8,128]{3,2,1,0:T(8,128)S(1)} %pad_maximum_fusion.1), channel_id=1, source_target_pairs={{0,2},{1,3},{2,0},{3,1},{4,6},{5,7},{6,4},{7,5},{8,10},{9,11},{10,... | collective-permute-start | bytes 196616 | tf_op jit(solution)/shard_map/ppermute | solution.py:308
  66.7 6.1 %collective-permute-start.6 = (f32[2,8,8,128]{3,2,1,0:T(8,128)}, f32[2,8,8,128]{3,2,1,0:T(8,128)S(1)}, u32[]{:S(2)}, u32[]{:S(2)}) collective-permute-start(f32[2,8,8,128]{3,2,1,0:T(8,128)} %hop_three.3), channel_id=1, source_target_pairs={{0,4},{1,5},{2,6},{3,7},{4,0},{5,1},{6,2},{7,3},{8,12},{9,13},{10,... | collective-permute-start | bytes 196616 | tf_op jit(solution)/shard_map/ppermute | solution.py:308
  74.9 22.2 %collective-permute-start.7 = (f32[1,8,8,128]{3,2,1,0:T(8,128)}, f32[1,8,8,128]{3,2,1,0:T(8,128)S(1)}, u32[]{:S(2)}, u32[]{:S(2)}) collective-permute-start(f32[1,8,8,128]{3,2,1,0:T(8,128)} %hop_four.3), channel_id=1, source_target_pairs={{0,8},{1,9},{2,10},{3,11},{4,12},{5,13},{6,14},{7,15},{8,0},{9,1},... | collective-permute-start | bytes 98312 | tf_op jit(solution)/shard_map/ppermute | solution.py:308
  80.7 1.6 %copy-start.9 = (bf16[1024,1024]{1,0:T(8,128)(2,1)S(1)}, bf16[1024,1024]{1,0:T(8,128)(2,1)}, u32[]{:S(2)}) copy-start(bf16[1024,1024]{1,0:T(8,128)(2,1)} %w_query_ref.1) | copy-start | bytes 6291460
  82.3 1.2 %copy-start.11 = (bf16[1,512,1024]{2,1,0:T(8,128)(2,1)S(1)}, bf16[1,512,1024]{2,1,0:T(8,128)(2,1)}, u32[]{:S(2)}) copy-start(bf16[1,512,1024]{2,1,0:T(8,128)(2,1)} %param.10) | copy-start | bytes 3145732
  83.5 1.2 %copy-start.14 = (bf16[1024,512]{1,0:T(8,128)(2,1)S(1)}, bf16[1024,512]{1,0:T(8,128)(2,1)}, u32[]{:S(2)}) copy-start(bf16[1024,512]{1,0:T(8,128)(2,1)} %copy-done.13) | copy-start | bytes 3145732
  86.0 13.3 %copy-start = (bf16[1,1024,1024]{2,1,0:T(8,128)(2,1)S(1)}, bf16[1,1024,1024]{2,1,0:T(8,128)(2,1)}, u32[]{:S(2)}) copy-start(bf16[1,1024,1024]{2,1,0:T(8,128)(2,1)} %param.19) | copy-start | bytes 6291460
  94.8 1.4 %copy-start.1 = (f32[512,1024]{1,0:T(8,128)}, f32[512,1024]{1,0:T(8,128)S(1)}, u32[]{:S(2)}) copy-start(f32[512,1024]{1,0:T(8,128)S(1)} %get-tuple-element.14.inner_ref) | copy-start | bytes 6291460
  99.3 1.6 %copy-start.2 = (f32[512,1024]{1,0:T(8,128)S(1)}, f32[512,1024]{1,0:T(8,128)}, u32[]{:S(2)}) copy-start(f32[512,1024]{1,0:T(8,128)} %copy-done.1) | copy-start | bytes 6291460
  100.9 1.2 %copy-start.4 = (bf16[512,1024]{1,0:T(8,128)(2,1)S(1)}, bf16[512,1024]{1,0:T(8,128)(2,1)}, u32[]{:S(2)}) copy-start(bf16[512,1024]{1,0:T(8,128)(2,1)} %copy-done.3) | copy-start | bytes 3145732
  (12 other events, 9.3 us)

commit v2 on v0

v2 whole, which is shorter than its diff:
```python
import functools
import jax
import jax.numpy as jnp
from jax import lax
from jax.experimental import pallas as pl
from jax.experimental.pallas import tpu as pltpu
from jax.sharding import PartitionSpec as P

HEADS = 8
DIM = 128
STEPS = 512
WIDTH = 1024
PAIR = 2 * DIM
HALF = 256
SHARDS = 16
EPSILON = 1e-05
LOG2E = 1.4426950408889634
FAR = -1e30
MIB = 1024 * 1024
IN_HBM = pl.BlockSpec(memory_space=pltpu.HBM)
IN_VMEM = pl.BlockSpec(memory_space=pltpu.VMEM)
IN_SMEM = pl.BlockSpec(memory_space=pltpu.SMEM)
DMA = pltpu.SemaphoreType.DMA


def lanes_of(number, size=PAIR):
    return slice(number * size, (number + 1) * size)


def params(mib):
    return pltpu.CompilerParams(vmem_limit_bytes=mib * MIB)


def work(flops, nbytes):
    return pl.CostEstimate(flops=flops, bytes_accessed=nbytes, transcendentals=0)


def running_sum(rates):
    lane = lax.broadcasted_iota(jnp.int32, rates.shape, 1)
    shift = 1
    while shift < STEPS:
        moved = pltpu.roll(rates, shift, 1)
        rates = rates + jnp.where(lane >= shift, moved, 0.0)
        shift *= 2
    return rates


def split(state):
    high = state.astype(jnp.bfloat16)
    low = (state - high.astype(jnp.float32)).astype(jnp.bfloat16)
    return jnp.concatenate([high, low], 0)


def turned(sums):
    padding = jnp.zeros((DIM - HEADS, STEPS), jnp.float32)
    return jnp.concatenate([sums, padding], 0).T


def local_kernel(lengths_ref, tokens_hbm, w_query_hbm, w_key_hbm, w_value_hbm, decay_hbm,
                 total_hbm, mixed_hbm,
                 tokens_ref, w_query_ref, w_key_ref, w_value_ref, decay_ref,
                 keys_ref, values_ref, total_ref, mixed_ref, in_sems, out_sems):
    copies = []
    for at, (source, target) in enumerate((
            (decay_hbm, decay_ref), (tokens_hbm, tokens_ref), (w_key_hbm, w_key_ref),
            (w_value_hbm, w_value_ref), (w_query_hbm, w_query_ref))):
        copies.append(pltpu.make_async_copy(source, target, in_sems.at[at]))
        copies[at].start()
    outs = []

    def send(source, target):
        outs.append(pltpu.make_async_copy(source, target, out_sems.at[len(outs)]))
        outs[-1].start()

    valid = lengths_ref[0] - lax.axis_index("seq") * STEPS
    copies[0].wait()
    lane = lax.broadcasted_iota(jnp.int32, (HEADS, STEPS), 1)
    sums = running_sum(jnp.where(lane < valid, decay_ref[...] * LOG2E, 0.0))
    growth = jnp.broadcast_to(sums[:, STEPS - 1:], (HEADS, DIM))
    total_ref[:, HEADS] = jnp.broadcast_to(growth[None], (SHARDS, HEADS, DIM))
    tails = jnp.exp2(sums[:, STEPS - 1:] - sums)
    columns = turned(sums)
    alive = lax.broadcasted_iota(jnp.int32, (STEPS, PAIR), 0) < valid
    causal = (lax.broadcasted_iota(jnp.int32, (DIM, DIM), 0)
              >= lax.broadcasted_iota(jnp.int32, (DIM, DIM), 1))
    for copy in copies[1:4]:
        copy.wait()
    tokens = tokens_ref[...]
    for pair in range(4):
        lanes = lanes_of(pair)
        keys = jnp.dot(tokens, w_key_ref[:, lanes], preferred_element_type=jnp.float32)
        keys_t = jnp.where(alive, keys * DIM ** (-0.5), 0.0).astype(jnp.bfloat16).T
        values = jnp.dot(tokens, w_value_ref[:, lanes], preferred_element_type=jnp.float32)
        values = jnp.where(alive, values, 0.0).astype(jnp.bfloat16)
        keys_ref[lanes, :] = keys_t
        values_ref[:, lanes] = values
        for j in range(2):
            head = 2 * pair + j
            own = lanes_of(j, DIM)
            decayed = (keys_t[own].astype(jnp.float32) * tails[head:head + 1]).astype(jnp.bfloat16)
            total = jnp.dot(decayed, values[:, own], preferred_element_type=jnp.float32)
            total_ref[:, head] = total.reshape(SHARDS, 8, DIM)
    send(total_ref, total_hbm)
    copies[4].wait()
    for pair in range(4):
        lanes = lanes_of(pair)
        queries = jnp.dot(tokens, w_query_ref[:, lanes], preferred_element_type=jnp.float32).astype(jnp.bfloat16)
        for j in range(2):
            head = 2 * pair + j
            own = lanes_of(head, DIM)
            attend(causal, sums[head:head + 1], columns[:, head:head + 1], queries[:, lanes_of(j, DIM)],
                   keys_ref[own, :], values_ref[:, own], own, mixed_ref)
        if pair % 2 == 1:
            done = slice((pair - 1) * PAIR, (pair + 1) * PAIR)
            send(mixed_ref.at[:, :, done], mixed_hbm.at[:, :, done])
    for copy in outs:
        copy.wait()


def attend(causal, row, column, queries, keys_t, values, own, mixed_ref):
    first = slice(0, HALF)
    middle = row[:, HALF - 1:HALF]
    decayed = (keys_t[:, first].astype(jnp.float32) * jnp.exp2(middle - row[:, first])).astype(jnp.bfloat16)
    state = split(jnp.dot(decayed, values[first], preferred_element_type=jnp.float32))
    column = jnp.broadcast_to(column, (STEPS, DIM))
    mixed_ref[0, :, own] = (queries.astype(jnp.float32) * jnp.exp2(column)).astype(jnp.bfloat16)
    for c in range(2):
        rows = lanes_of(c)
        q = queries[rows]
        scores = jnp.dot(q, keys_t[:, rows], preferred_element_type=jnp.float32)
        strips = []
        for s in range(2):
            here = column[c * HALF + s * DIM:c * HALF + (s + 1) * DIM]
            parts = []
            for b in range(s + 1):
                gap = here - row[:, c * HALF + b * DIM:c * HALF + (b + 1) * DIM]
                if b == s:
                    gap = jnp.where(causal, gap, FAR)
                score = scores[s * DIM:(s + 1) * DIM, b * DIM:(b + 1) * DIM]
                parts.append((score * jnp.exp2(gap)).astype(jnp.bfloat16))
            if s == 0:
                parts.append(jnp.zeros((DIM, DIM), jnp.bfloat16))
            strips.append(jnp.concatenate(parts, 1))
        weights = jnp.concatenate(strips, 0)
        part = jnp.dot(weights, values[rows], preferred_element_type=jnp.float32)
        if c == 1:
            cross = jnp.dot(jnp.concatenate([q, q], 1), state, preferred_element_type=jnp.float32)
            part = part + cross * jnp.exp2(column[HALF:] - middle)
        part = part - jnp.mean(part, axis=1, keepdims=True)
        mixed_ref[1, rows, own] = part.astype(jnp.bfloat16)


def local_call(lengths, tokens, w_query, w_key, w_value, decay):
    return pl.pallas_call(
        local_kernel,
        in_specs=[IN_SMEM] + [IN_HBM] * 5,
        out_specs=[IN_HBM] * 2,
        out_shape=[
            jax.ShapeDtypeStruct((SHARDS, HEADS + 1, 8, DIM), jnp.float32),
            jax.ShapeDtypeStruct((2, STEPS, WIDTH), jnp.bfloat16),
        ],
        scratch_shapes=[
            pltpu.VMEM((STEPS, WIDTH), jnp.bfloat16),
            pltpu.VMEM((WIDTH, WIDTH), jnp.bfloat16),
            pltpu.VMEM((WIDTH, WIDTH), jnp.bfloat16),
            pltpu.VMEM((WIDTH, WIDTH), jnp.bfloat16),
            pltpu.VMEM((HEADS, STEPS), jnp.float32),
            pltpu.VMEM((WIDTH, STEPS), jnp.bfloat16),
            pltpu.VMEM((STEPS, WIDTH), jnp.bfloat16),
            pltpu.VMEM((SHARDS, HEADS + 1, 8, DIM), jnp.float32),
            pltpu.VMEM((2, STEPS, WIDTH), jnp.bfloat16),
            DMA((5,)),
            DMA((3,)),
        ],
        compiler_params=params(62),
        cost_estimate=work(2 * STEPS * WIDTH * WIDTH * 4, 10 * MIB),
        name="local_pass",
    )(lengths, tokens, w_query, w_key, w_value, decay)


def scan_kernel(sources_ref, received_ref, *refs):
    items = refs[:7]
    carried_hbm, closing_ref, start_ref, rows_ref, sems = refs[7:]
    number = landing(sources_ref[lax.axis_index("asset")])
    for k, item in enumerate(items):
        @pl.when(number == k)
        def _(item=item):
            start_ref[...] = item[...]
    states = [start_ref[head] for head in range(HEADS)]
    outs = []
    for shard in range(SHARDS):
        for head in range(HEADS):
            rows_ref[shard, head] = states[head]
            growth = jnp.exp2(received_ref[shard, HEADS, head:head + 1, :])
            states[head] = growth * states[head] + received_ref[shard, head]
        if shard % 4 == 3:
            done = slice(shard - 3, shard + 1)
            outs.append(pltpu.make_async_copy(rows_ref.at[done], carried_hbm.at[done], sems.at[shard // 4]))
            outs[-1].start()
    for head in range(HEADS):
        closing_ref[head] = states[head]
    for copy in outs:
        copy.wait()


def scan_call(sources, received, items):
    return pl.pallas_call(
        scan_kernel,
        in_specs=[IN_SMEM] + [IN_VMEM] * 8,
        out_specs=[IN_HBM, IN_VMEM],
        out_shape=[
            jax.ShapeDtypeStruct((SHARDS, HEADS, 8, DIM), jnp.float32),
            jax.ShapeDtypeStruct((HEADS, 8, DIM), jnp.float32),
        ],
        scratch_shapes=[
            pltpu.VMEM((HEADS, 8, DIM), jnp.float32),
            pltpu.VMEM((SHARDS, HEADS, 8, DIM), jnp.float32),
            DMA((4,)),
        ],
        compiler_params=params(8),
        cost_estimate=work(MIB, 2 * MIB),
        name="scan_rows",
    )(sources, received, *items)


STRIP = 512


def outer_kernel(lengths_ref, mixed_ref, state_ref, whiten_ref,
                 features_hbm, out_ref, out_sems):
    valid = lengths_ref[0] - lax.axis_index("seq") * STEPS
    states = []
    for head in range(HEADS):
        state = state_ref[:, head].reshape(DIM, DIM)
        states.append(split(state - jnp.mean(state, axis=1, keepdims=True)))
    same = (lax.broadcasted_iota(jnp.int32, (PAIR, PAIR), 0) // DIM
            == lax.broadcasted_iota(jnp.int32, (PAIR, PAIR), 1) // DIM)
    averaging = jnp.where(same, 1.0 / DIM, 0.0).astype(jnp.bfloat16)
    out_copies = []
    for strip in range(STEPS // STRIP):
        rows = lanes_of(strip, STRIP)
        alive = strip * STRIP + lax.broadcasted_iota(jnp.int32, (STRIP, PAIR), 0) < valid
        parts = []
        for pair in range(4):
            halves = []
            for head in (2 * pair, 2 * pair + 1):
                own = lanes_of(head, DIM)
                q = mixed_ref[0, rows, own]
                cross = jnp.dot(jnp.concatenate([q, q], 1), states[head], preferred_element_type=jnp.float32)
                halves.append(mixed_ref[1, rows, own].astype(jnp.float32) + cross)
            centered = jnp.concatenate(halves, 1)
            squares = (centered * centered).astype(jnp.bfloat16)
            spread = jnp.dot(squares, averaging, preferred_element_type=jnp.float32)
            scale = jnp.where(alive, lax.rsqrt(spread + EPSILON), 0.0)
            parts.append((centered * scale).astype(jnp.bfloat16))
        out_ref[rows, :] = jnp.dot(
            jnp.concatenate(parts, 1), whiten_ref[...], preferred_element_type=jnp.float32).astype(jnp.bfloat16)
        out_copies.append(pltpu.make_async_copy(
            out_ref.at[rows, :], features_hbm.at[rows, :], out_sems.at[strip]))
        out_copies[strip].start()
    for copy in out_copies:
        copy.wait()


def outer_call(lengths, mixed, state, whiten):
    return pl.pallas_call(
        outer_kernel,
        in_specs=[IN_SMEM] + [IN_VMEM] * 3,
        out_specs=IN_HBM,
        out_shape=jax.ShapeDtypeStruct((STEPS, WIDTH), jnp.bfloat16),
        scratch_shapes=[
            pltpu.VMEM((STEPS, WIDTH), jnp.bfloat16),
            DMA((STEPS // STRIP,)),
        ],
        compiler_params=params(16),
        cost_estimate=work(2 * STEPS * WIDTH * WIDTH * 3 // 2, 4 * MIB),
        name="outer_whiten",
    )(lengths, mixed, state, whiten)


def origin(targets_ref, slot):
    asset = jnp.int32(0)
    for k in range(1, SHARDS):
        asset = jnp.where(targets_ref[k] == slot, k, asset)
    return asset


def landing(source):
    me = lax.axis_index("asset")
    steps = (me ^ source) & 3
    return jnp.where(steps == 0, (me ^ source) >> 2, 3 + steps)


def near_kernel(inverted, route_ref, *refs):
    items, outs = refs[:4], refs[5:8]
    me = lax.axis_index("asset")
    for j, out in enumerate(outs, 1):
        slot = me ^ j
        source = origin(route_ref, slot) if inverted else route_ref[slot]
        number = ((me ^ source) >> 2) & 3
        for k, item in enumerate(items):
            @pl.when(number == k)
            def _(item=item, out=out):
                out[...] = item[...]


def near_call(inverted, route, items, passed):
    return pl.pallas_call(
        functools.partial(near_kernel, inverted),
        in_specs=[IN_SMEM] + [IN_VMEM] * 4 + [pl.BlockSpec(memory_space=pl.ANY)],
        out_specs=[IN_VMEM] * 3 + [pl.BlockSpec(memory_space=pl.ANY)],
        out_shape=[jax.ShapeDtypeStruct((HEADS, 8, DIM), jnp.float32)] * 3
        + [jax.ShapeDtypeStruct(passed.shape, passed.dtype)],
        input_output_aliases={5: 3},
        compiler_params=params(63),
        cost_estimate=work(1024, 2 ** 17),
        name="near_rows",
    )(route, *items, passed)


def kept_kernel(targets_ref, *refs):
    items, kept_hbm, sem = refs[:7], refs[7], refs[8]
    number = landing(origin(targets_ref, lax.axis_index("asset")))
    for k, item in enumerate(items):
        @pl.when(number == k)
        def _(item=item):
            copy = pltpu.make_async_copy(item, kept_hbm.at[0], sem)
            copy.start()
            copy.wait()


def kept_call(targets, items):
    return pl.pallas_call(
        kept_kernel,
        in_specs=[IN_SMEM] + [pl.BlockSpec(memory_space=pl.ANY)] * 7,
        out_specs=pl.BlockSpec(memory_space=pl.ANY),
        out_shape=jax.ShapeDtypeStruct((1, HEADS, 8, DIM), jnp.float32),
        scratch_shapes=[DMA],
        compiler_params=params(8),
        cost_estimate=work(1024, 2 ** 17),
        name="kept_rows",
    )(targets, *items)


def swap(value, bits):
    return lax.ppermute(value, "asset", [(k, k ^ bits) for k in range(SHARDS)])


def on_device(tokens, w_query, w_key, w_value, decay_log, lengths, sources, targets, stash, whiten):
    tokens, decay, whiten = tokens[0], decay_log[0], whiten[0]
    own = stash[0]
    items = [own] + [swap(own, 4 * k) for k in (1, 2, 3)]
    total, mixed = local_call(lengths, tokens, w_query, w_key, w_value, decay)
    *near, total = near_call(False, sources, items, total)
    items += [swap(item, k) for k, item in enumerate(near, 1)]
    received = lax.all_to_all(total, "seq", 0, 0, tiled=True)
    carried, closing = scan_call(sources, received, items)
    state = lax.all_to_all(carried, "seq", 0, 0, tiled=True)
    items = [closing] + [swap(closing, 4 * k) for k in (1, 2, 3)]
    features = outer_call(lengths, mixed, state, whiten)
    *near, features = near_call(True, targets, items, features)
    items += [swap(item, k) for k, item in enumerate(near, 1)]
    return (features[None], kept_call(targets, items))


def solution(mesh):
    return jax.shard_map(
        on_device,
        mesh=mesh,
        in_specs=(
            P("asset", "seq", None),
            P(),
            P(),
            P(),
            P("asset", None, "seq"),
            P("asset"),
            P(),
            P(),
            P("asset", None, "seq", None),
            P("asset", None, None),
        ),
        out_specs=(P("asset", "seq", None), P("asset", None, "seq", None)),
        check_vma=False,
    )
```

time: 288 us -> 81.1 us (0.28)
  blocking collectives: 103 us -> 0 us
  waiting for transfers between devices: 105 us -> 13.7 us
  starting transfers between devices: 0.08 us -> 33.4 us
  matrix products: 24.4 us -> 0 us
  Pallas kernels: 0 us -> 21.2 us
  other arithmetic: 20 us -> 0 us
  between operations: 18.4 us -> 1.63 us
  local copies, waits for them, and re-layouts: 15 us -> 10.3 us
    psum x1 -> x0, waiting for transfers between devices: 105 us -> none  [broadcast(): return lax.psum(kept, axis)]
    all_gather x3 -> x0, blocking collectives: 68.7 us -> none  [the longest x1 29.1 us: on_device(): gathered = lax.all_gather(stash, 'asset', axis=0, tiled=True)]
    unnamed x1 -> x0, blocking collectives: 34.5 us -> none
    dot_general x7 -> x0, matrix products: 24.4 us -> none  [the longest x1 5.58 us: on_device(): jnp.einsum('anchd,anhde->anche', query_float, block_state, precision=HIGH...]
    ppermute x0 -> x12, starting transfers between devices: none -> 23 us  [swap(): return lax.ppermute(value, 'asset', [(k, k ^ bits) for k in range(SHARDS)])]
    pallas_call x0 -> x6, Pallas kernels: none -> 21.2 us  [the longest x1 12.1 us: local_call(): pl.pallas_call(local_kernel, in_specs=[IN_SMEM] + [IN_HBM] * 5, out_specs...]
    all_to_all x0 -> x2, starting transfers between devices: none -> 10.3 us  [the longest x1 6.76 us: on_device(): received = lax.all_to_all(total, 'seq', 0, 0, tiled=True)]
    all_to_all x0 -> x2, waiting for transfers between devices: none -> 8.08 us  [the longest x1 4.56 us: on_device(): received = lax.all_to_all(total, 'seq', 0, 0, tiled=True)]
  transfers between devices with their start and end apart: 2 -> 14, of which waited for: 1 -> 6; matrix products, arithmetic and copies ran while one was open for 7% -> 0% of each run, Pallas kernels for 0% -> 19%
where the time goes in v2:
time: 81.1 us; the launch traced here: 80.2 us
  starting transfers between devices  33.4 us (41%)
  Pallas kernels  21.2 us (26%)
  waiting for transfers between devices  13.7 us (17%)
  local copies, waits for them, and re-layouts  10.3 us (13%)
  between operations  1.63 us (2%)
    ppermute x12, starting transfers between devices, swap(): return lax.ppermute(value, 'asset', [(k, k ^ bits) for k in range(SHARDS)])  23 us
    pallas_call x1, Pallas kernels, local_call(): pl.pallas_call(local_kernel, in_specs=[IN_SMEM] + [IN_HBM] * 5, out_specs...  12.1 us
    unnamed x38, local copies, waits for them, and re-layouts  10.3 us
    all_to_all x1, starting transfers between devices, on_device(): received = lax.all_to_all(total, 'seq', 0, 0, tiled=True)  6.76 us
    ppermute x12, waiting for transfers between devices, swap(): return lax.ppermute(value, 'asset', [(k, k ^ bits) for k in range(SHARDS)])  5.57 us
    all_to_all x1, waiting for transfers between devices, on_device(): received = lax.all_to_all(total, 'seq', 0, 0, tiled=True)  4.56 us
    all_to_all x1, starting transfers between devices, on_device(): state = lax.all_to_all(carried, 'seq', 0, 0, tiled=True)  3.59 us
    all_to_all x1, waiting for transfers between devices, on_device(): state = lax.all_to_all(carried, 'seq', 0, 0, tiled=True)  3.53 us
  transfers between devices with their start and end apart: 14, of which 6 were waited for; matrix products, arithmetic and copies ran while one was open for 0% of the time, Pallas kernels for 19%

profile of v2, /device:TPU:1, one launch (start us, length us, event | category | flops | bytes accessed | tf_op | source)
XLA Modules:
  0.0 80.2 jit_solution(2853140628854429732)
XLA Ops:
  0.6 6.9 %collective-permute-start.2 = (f32[8,8,128]{2,1,0:T(8,128)}, f32[8,8,128]{2,1,0:T(8,128)S(1)}, u32[]{:S(2)}, u32[]{:S(2)}) collective-permute-start(f32[8,8,128]{2,1,0:T(8,128)} %bitcast.5), channel_id=1, source_target_pairs={{0,12},{1,13},{2,14},{3,15},{4,8},{5,9},{6,10},{7,11},{8,4},{9,5},... | collective-permute-start | bytes 98312 | tf_op jit(solution)/shard_map/ppermute | solution.py:346
  7.6 1.0 %collective-permute-start.1 = (f32[8,8,128]{2,1,0:T(8,128)}, f32[8,8,128]{2,1,0:T(8,128)S(1)}, u32[]{:S(2)}, u32[]{:S(2)}) collective-permute-start(f32[8,8,128]{2,1,0:T(8,128)} %bitcast.6), channel_id=1, source_target_pairs={{0,8},{1,9},{2,10},{3,11},{4,12},{5,13},{6,14},{7,15},{8,0},{9,1},... | collective-permute-start | bytes 98312 | tf_op jit(solution)/shard_map/ppermute | solution.py:346
  8.6 1.2 %collective-permute-start = (f32[8,8,128]{2,1,0:T(8,128)}, f32[8,8,128]{2,1,0:T(8,128)S(1)}, u32[]{:S(2)}, u32[]{:S(2)}) collective-permute-start(f32[8,8,128]{2,1,0:T(8,128)} %bitcast.7), channel_id=1, source_target_pairs={{0,4},{1,5},{2,6},{3,7},{4,0},{5,1},{6,2},{7,3},{8,12},{9,13},{10,... | collective-permute-start | bytes 98312 | tf_op jit(solution)/shard_map/ppermute | solution.py:346
  10.4 12.1 %local_pass.1 = (f32[16,9,8,128]{3,2,1,0:T(8,128)}, bf16[2,512,1024]{2,1,0:T(8,128)(2,1)}) custom-call(s32[1]{0:T(128)S(6)} %copy.16.lengths_ref, bf16[512,1024]{1,0:T(8,128)(2,1)} %bitcast.12, bf16[1024,1024]{1,0:T(8,128)(2,1)} %w_query_hbm.1, bf16[1024,1024]{1,0:T(8,128)(2,1)} %w_key_hbm.1, bf16[1024,1024]{1,0:T(8,128)(2,1)} %w_value_hbm.1, f32[8,512]{1,0:T(8,128)} %bitcast.13), custom_call_target="tpu_custom_call" | custom-call | flops 4294967296 | bytes 10485760 | tf_op jit(solution)/shard_map/local_pass/pallas_call | solution.py:154
  23.2 1.5 %near_rows.2 = (f32[8,8,128]{2,1,0:T(8,128)}, f32[8,8,128]{2,1,0:T(8,128)}, f32[8,8,128]{2,1,0:T(8,128)}, f32[16,9,8,128]{3,2,1,0:T(8,128)}) custom-call(s32[16]{0:T(128)} %sources_ref.1, f32[8,8,128]{2,1,0:T(8,128)} %bitcast.8, f32[8,8,128]{2,1,0:T(8,128)} %copy-done.5, f32[8,8,128]{2,1,0:T(8,128)} %copy-done.3, ...), custom_call_target="tpu_custom_call", output_to_operand_aliasing={{3}: (5, {})} | custom-call | flops 1024 | bytes 131072 | tf_op jit(solution)/shard_map/near_rows/pallas_call | solution.py:308
  24.8 6.8 %all-to-all-start = ((f32[16,9,8,128]{3,2,1,0:T(8,128)}), f32[16,9,8,128]{3,2,1,0:T(8,128)S(1)}, u32[]{:S(2)}, u32[]{:S(2)}) async-start(f32[16,9,8,128]{3,2,1,0:T(8,128)} %get-tuple-element.15), calls=%async_computation | async-start | bytes 1179648 | tf_op jit(solution)/shard_map/all_to_all | solution.py:356
  31.6 1.6 %collective-permute-start.3 = (f32[8,8,128]{2,1,0:T(8,128)}, f32[8,8,128]{2,1,0:T(8,128)S(1)}, u32[]{:S(2)}, u32[]{:S(2)}) collective-permute-start(f32[8,8,128]{2,1,0:T(8,128)} %get-tuple-element.16), channel_id=1, source_target_pairs={{0,1},{1,0},{2,3},{3,2},{4,5},{5,4},{6,7},{7,6},{8,9},{9,8},{10,11... | collective-permute-start | bytes 98312 | tf_op jit(solution)/shard_map/ppermute | solution.py:346
  34.9 1.3 %collective-permute-done.4.refs_5_ = f32[8,8,128]{2,1,0:T(8,128)S(1)} collective-permute-done((f32[8,8,128]{2,1,0:T(8,128)}, f32[8,8,128]{2,1,0:T(8,128)S(1)}, u32[]{:S(2)}, u32[]{:S(2)}) %collective-permute-start.4) | collective-permute-done | bytes 32800 | tf_op jit(solution)/shard_map/ppermute | solution.py:346
  36.1 1.6 %collective-permute-done.5.refs_6_ = f32[8,8,128]{2,1,0:T(8,128)S(1)} collective-permute-done((f32[8,8,128]{2,1,0:T(8,128)}, f32[8,8,128]{2,1,0:T(8,128)S(1)}, u32[]{:S(2)}, u32[]{:S(2)}) %collective-permute-start.5) | collective-permute-done | bytes 32800 | tf_op jit(solution)/shard_map/ppermute | solution.py:346
  37.8 4.6 %all-to-all-done.received_ref = f32[16,9,8,128]{3,2,1,0:T(8,128)S(1)} async-done(((f32[16,9,8,128]{3,2,1,0:T(8,128)}), f32[16,9,8,128]{3,2,1,0:T(8,128)S(1)}, u32[]{:S(2)}, u32[]{:S(2)}) %all-to-all-start) | async-done | bytes 589856 | tf_op jit(solution)/shard_map/all_to_all | solution.py:356
  44.6 1.4 %scan_rows.1 = (f32[16,8,8,128]{3,2,1,0:T(8,128)}, f32[8,8,128]{2,1,0:T(8,128)S(1)}) custom-call(s32[16]{0:T(128)S(1)} %copy-done.16, f32[16,9,8,128]{3,2,1,0:T(8,128)S(1)} %all-to-all-done.received_ref, f32[8,8,128]{2,1,0:T(8,128)S(1)} %bitcast.9, f32[8,8,128]{2,1,0:T(8,128)S(1)} %copy-done.6, f32[8,8,128]{2,1,0:T(8,128)S(1)} %copy-done.4, ...), custom_call_target="tpu_custom_call" | custom-call | flops 1048576 | bytes 2097152 | tf_op jit(solution)/shard_map/scan_rows/pallas_call | solution.py:207
  46.1 3.6 %all-to-all-start.1 = ((f32[16,8,8,128]{3,2,1,0:T(8,128)}), f32[16,8,8,128]{3,2,1,0:T(8,128)S(1)}, u32[]{:S(2)}, u32[]{:S(2)}) async-start(f32[16,8,8,128]{3,2,1,0:T(8,128)} %get-tuple-element.21), calls=%async_computation.1 | async-start | bytes 1048576 | tf_op jit(solution)/shard_map/all_to_all | solution.py:358
  49.7 3.3 %collective-permute-start.8 = (f32[8,8,128]{2,1,0:T(8,128)S(1)}, f32[8,8,128]{2,1,0:T(8,128)S(1)}, u32[]{:S(2)}, u32[]{:S(2)}) collective-permute-start(f32[8,8,128]{2,1,0:T(8,128)S(1)} %get-tuple-element.19.refs_0_), channel_id=1, source_target_pairs={{0,12},{1,13},{2,14},{3,15},{4,8},{5,9},{6,10},{7,11},{8,4},{9,5},... | collective-permute-start | bytes 98312 | tf_op jit(solution)/shard_map/ppermute | solution.py:346
  53.0 1.2 %collective-permute-start.7 = (f32[8,8,128]{2,1,0:T(8,128)S(1)}, f32[8,8,128]{2,1,0:T(8,128)S(1)}, u32[]{:S(2)}, u32[]{:S(2)}) collective-permute-start(f32[8,8,128]{2,1,0:T(8,128)S(1)} %get-tuple-element.19.refs_0_), channel_id=1, source_target_pairs={{0,8},{1,9},{2,10},{3,11},{4,12},{5,13},{6,14},{7,15},{8,0},{9,1},... | collective-permute-start | bytes 98312 | tf_op jit(solution)/shard_map/ppermute | solution.py:346
  54.2 1.2 %collective-permute-start.6 = (f32[8,8,128]{2,1,0:T(8,128)S(1)}, f32[8,8,128]{2,1,0:T(8,128)S(1)}, u32[]{:S(2)}, u32[]{:S(2)}) collective-permute-start(f32[8,8,128]{2,1,0:T(8,128)S(1)} %get-tuple-element.19.refs_0_), channel_id=1, source_target_pairs={{0,4},{1,5},{2,6},{3,7},{4,0},{5,1},{6,2},{7,3},{8,12},{9,13},{10,... | collective-permute-start | bytes 98312 | tf_op jit(solution)/shard_map/ppermute | solution.py:346
  55.4 3.5 %all-to-all-done.1.state_ref = f32[16,8,8,128]{3,2,1,0:T(8,128)S(1)} async-done(((f32[16,8,8,128]{3,2,1,0:T(8,128)}), f32[16,8,8,128]{3,2,1,0:T(8,128)S(1)}, u32[]{:S(2)}, u32[]{:S(2)}) %all-to-all-start.1) | async-done | bytes 524320 | tf_op jit(solution)/shard_map/all_to_all | solution.py:358
  59.0 1.6 %copy-done.17 = bf16[1,1024,1024]{2,1,0:T(8,128)(2,1)S(1)} copy-done((bf16[1,1024,1024]{2,1,0:T(8,128)(2,1)S(1)}, bf16[1,1024,1024]{2,1,0:T(8,128)(2,1)}, u32[]{:S(2)}) %copy-start.17) | copy-done | bytes 2097176
  60.5 1.6 %copy-done.18 = bf16[2,512,1024]{2,1,0:T(8,128)(2,1)S(1)} copy-done((bf16[2,512,1024]{2,1,0:T(8,128)(2,1)S(1)}, bf16[2,512,1024]{2,1,0:T(8,128)(2,1)}, u32[]{:S(2)}) %copy-start.18) | copy-done | bytes 2097176
  62.1 3.4 %outer_whiten.1.refs_4_ = bf16[512,1024]{1,0:T(8,128)(2,1)} custom-call(s32[1]{0:T(128)S(6)} %copy.16.lengths_ref, bf16[2,512,1024]{2,1,0:T(8,128)(2,1)S(1)} %copy-done.18, f32[16,8,8,128]{3,2,1,0:T(8,128)S(1)} %all-to-all-done.1.state_ref, bf16[1024,1024]{1,0:T(8,128)(2,1)S(1)} %bitcast.10), custom_call_target="tpu_custom_call" | custom-call | flops 1610612736 | bytes 4194304 | tf_op jit(solution)/shard_map/outer_whiten/pallas_call | solution.py:266
  66.8 1.6 %near_rows.3 = (f32[8,8,128]{2,1,0:T(8,128)}, f32[8,8,128]{2,1,0:T(8,128)}, f32[8,8,128]{2,1,0:T(8,128)}, bf16[512,1024]{1,0:T(8,128)(2,1)}) custom-call(s32[16]{0:T(128)} %targets_ref.1, f32[8,8,128]{2,1,0:T(8,128)} %copy-done.7, f32[8,8,128]{2,1,0:T(8,128)} %copy-done.13, f32[8,8,128]{2,1,0:T(8,128)} %copy-done.11, ...), custom_call_target="tpu_custom_call", output_to_operand_aliasing={{3}: (5, {})} | custom-call | flops 1024 | bytes 131072 | tf_op jit(solution)/shard_map/near_rows/pallas_call | solution.py:308
  68.3 3.2 %collective-permute-start.9 = (f32[8,8,128]{2,1,0:T(8,128)}, f32[8,8,128]{2,1,0:T(8,128)S(1)}, u32[]{:S(2)}, u32[]{:S(2)}) collective-permute-start(f32[8,8,128]{2,1,0:T(8,128)} %get-tuple-element.23), channel_id=1, source_target_pairs={{0,1},{1,0},{2,3},{3,2},{4,5},{5,4},{6,7},{7,6},{8,9},{9,8},{10,11... | collective-permute-start | bytes 98312 | tf_op jit(solution)/shard_map/ppermute | solution.py:346
  73.1 1.3 %collective-permute-done.10.refs_5_ = f32[8,8,128]{2,1,0:T(8,128)S(1)} collective-permute-done((f32[8,8,128]{2,1,0:T(8,128)}, f32[8,8,128]{2,1,0:T(8,128)S(1)}, u32[]{:S(2)}, u32[]{:S(2)}) %collective-permute-start.10) | collective-permute-done | bytes 32800 | tf_op jit(solution)/shard_map/ppermute | solution.py:346
  74.5 1.3 %collective-permute-done.11.refs_6_ = f32[8,8,128]{2,1,0:T(8,128)S(1)} collective-permute-done((f32[8,8,128]{2,1,0:T(8,128)}, f32[8,8,128]{2,1,0:T(8,128)S(1)}, u32[]{:S(2)}, u32[]{:S(2)}) %collective-permute-start.11) | collective-permute-done | bytes 32800 | tf_op jit(solution)/shard_map/ppermute | solution.py:346
  78.8 1.2 %kept_rows.1 = f32[1,8,8,128]{3,2,1,0:T(8,128)} custom-call(s32[16]{0:T(128)S(1)} %copy-done.15, f32[8,8,128]{2,1,0:T(8,128)S(1)} %copy-done.8, f32[8,8,128]{2,1,0:T(8,128)S(1)} %copy-done.14, f32[8,8,128]{2,1,0:T(8,128)S(1)} %copy-done.12, f32[8,8,128]{2,1,0:T(8,128)S(1)} %copy-done.10, f32[8,8,128]{2,1,0:T(8,128)S(1)} %collective-permute-done.9.refs_4_, ...), custom_call_target="tpu_custom_call" | custom-call | flops 1024 | bytes 131072 | tf_op jit(solution)/shard_map/kept_rows/pallas_call | solution.py:333
  (48 shorter events, 10.5 us)
Async XLA Ops:
  0.6 22.0 %collective-permute-start.2 = (f32[8,8,128]{2,1,0:T(8,128)}, f32[8,8,128]{2,1,0:T(8,128)S(1)}, u32[]{:S(2)}, u32[]{:S(2)}) collective-permute-start(f32[8,8,128]{2,1,0:T(8,128)} %bitcast.5), channel_id=1, source_target_pairs={{0,12},{1,13},{2,14},{3,15},{4,8},{5,9},{6,10},{7,11},{8,4},{9,5},... | collective-permute-start | bytes 98312 | tf_op jit(solution)/shard_map/ppermute | solution.py:346
  7.6 15.0 %collective-permute-start.1 = (f32[8,8,128]{2,1,0:T(8,128)}, f32[8,8,128]{2,1,0:T(8,128)S(1)}, u32[]{:S(2)}, u32[]{:S(2)}) collective-permute-start(f32[8,8,128]{2,1,0:T(8,128)} %bitcast.6), channel_id=1, source_target_pairs={{0,8},{1,9},{2,10},{3,11},{4,12},{5,13},{6,14},{7,15},{8,0},{9,1},... | collective-permute-start | bytes 98312 | tf_op jit(solution)/shard_map/ppermute | solution.py:346
  8.6 14.1 %collective-permute-start = (f32[8,8,128]{2,1,0:T(8,128)}, f32[8,8,128]{2,1,0:T(8,128)S(1)}, u32[]{:S(2)}, u32[]{:S(2)}) collective-permute-start(f32[8,8,128]{2,1,0:T(8,128)} %bitcast.7), channel_id=1, source_target_pairs={{0,4},{1,5},{2,6},{3,7},{4,0},{5,1},{6,2},{7,3},{8,12},{9,13},{10,... | collective-permute-start | bytes 98312 | tf_op jit(solution)/shard_map/ppermute | solution.py:346
  10.4 31.9 %copy-start = (f32[1,8,8,128]{3,2,1,0:T(8,128)S(1)}, f32[1,8,8,128]{3,2,1,0:T(8,128)}, u32[]{:S(2)}) copy-start(f32[1,8,8,128]{3,2,1,0:T(8,128)} %param.18) | copy-start | bytes 98308
  10.4 31.9 %copy-start.16 = (s32[16]{0:T(128)S(1)}, s32[16]{0:T(128)}, u32[]{:S(2)}) copy-start(s32[16]{0:T(128)} %sources_ref.1) | copy-start | bytes 196
  24.8 17.6 %all-to-all-start = ((f32[16,9,8,128]{3,2,1,0:T(8,128)}), f32[16,9,8,128]{3,2,1,0:T(8,128)S(1)}, u32[]{:S(2)}, u32[]{:S(2)}) async-start(f32[16,9,8,128]{3,2,1,0:T(8,128)} %get-tuple-element.15), calls=%async_computation | async-start | bytes 1179648 | tf_op jit(solution)/shard_map/all_to_all | solution.py:356
  31.6 3.3 %collective-permute-start.3 = (f32[8,8,128]{2,1,0:T(8,128)}, f32[8,8,128]{2,1,0:T(8,128)S(1)}, u32[]{:S(2)}, u32[]{:S(2)}) collective-permute-start(f32[8,8,128]{2,1,0:T(8,128)} %get-tuple-element.16), channel_id=1, source_target_pairs={{0,1},{1,0},{2,3},{3,2},{4,5},{5,4},{6,7},{7,6},{8,9},{9,8},{10,11... | collective-permute-start | bytes 98312 | tf_op jit(solution)/shard_map/ppermute | solution.py:346
  33.2 3.0 %collective-permute-start.4 = (f32[8,8,128]{2,1,0:T(8,128)}, f32[8,8,128]{2,1,0:T(8,128)S(1)}, u32[]{:S(2)}, u32[]{:S(2)}) collective-permute-start(f32[8,8,128]{2,1,0:T(8,128)} %get-tuple-element.17), channel_id=1, source_target_pairs={{0,2},{1,3},{2,0},{3,1},{4,6},{5,7},{6,4},{7,5},{8,10},{9,11},{10,... | collective-permute-start | bytes 98312 | tf_op jit(solution)/shard_map/ppermute | solution.py:346
  33.9 3.9 %collective-permute-start.5 = (f32[8,8,128]{2,1,0:T(8,128)}, f32[8,8,128]{2,1,0:T(8,128)S(1)}, u32[]{:S(2)}, u32[]{:S(2)}) collective-permute-start(f32[8,8,128]{2,1,0:T(8,128)} %get-tuple-element.18), channel_id=1, source_target_pairs={{0,3},{1,2},{2,1},{3,0},{4,7},{5,6},{6,5},{7,4},{8,11},{9,10},{10,... | collective-permute-start | bytes 98312 | tf_op jit(solution)/shard_map/ppermute | solution.py:346
  42.4 0.8 copy-start.2
  43.1 0.8 copy-start.4
  43.9 0.8 copy-start.6
  46.1 19.4 %copy-start.7 = (f32[8,8,128]{2,1,0:T(8,128)}, f32[8,8,128]{2,1,0:T(8,128)S(1)}, u32[]{:S(2)}) copy-start(f32[8,8,128]{2,1,0:T(8,128)S(1)} %get-tuple-element.19.refs_0_) | copy-start | bytes 98308
  46.1 12.9 %all-to-all-start.1 = ((f32[16,8,8,128]{3,2,1,0:T(8,128)}), f32[16,8,8,128]{3,2,1,0:T(8,128)S(1)}, u32[]{:S(2)}, u32[]{:S(2)}) async-start(f32[16,8,8,128]{3,2,1,0:T(8,128)} %get-tuple-element.21), calls=%async_computation.1 | async-start | bytes 1048576 | tf_op jit(solution)/shard_map/all_to_all | solution.py:358
  49.7 15.9 %collective-permute-start.8 = (f32[8,8,128]{2,1,0:T(8,128)S(1)}, f32[8,8,128]{2,1,0:T(8,128)S(1)}, u32[]{:S(2)}, u32[]{:S(2)}) collective-permute-start(f32[8,8,128]{2,1,0:T(8,128)S(1)} %get-tuple-element.19.refs_0_), channel_id=1, source_target_pairs={{0,12},{1,13},{2,14},{3,15},{4,8},{5,9},{6,10},{7,11},{8,4},{9,5},... | collective-permute-start | bytes 98312 | tf_op jit(solution)/shard_map/ppermute | solution.py:346
  53.0 12.5 %collective-permute-start.7 = (f32[8,8,128]{2,1,0:T(8,128)S(1)}, f32[8,8,128]{2,1,0:T(8,128)S(1)}, u32[]{:S(2)}, u32[]{:S(2)}) collective-permute-start(f32[8,8,128]{2,1,0:T(8,128)S(1)} %get-tuple-element.19.refs_0_), channel_id=1, source_target_pairs={{0,8},{1,9},{2,10},{3,11},{4,12},{5,13},{6,14},{7,15},{8,0},{9,1},... | collective-permute-start | bytes 98312 | tf_op jit(solution)/shard_map/ppermute | solution.py:346
  54.2 11.3 %collective-permute-start.6 = (f32[8,8,128]{2,1,0:T(8,128)S(1)}, f32[8,8,128]{2,1,0:T(8,128)S(1)}, u32[]{:S(2)}, u32[]{:S(2)}) collective-permute-start(f32[8,8,128]{2,1,0:T(8,128)S(1)} %get-tuple-element.19.refs_0_), channel_id=1, source_target_pairs={{0,4},{1,5},{2,6},{3,7},{4,0},{5,1},{6,2},{7,3},{8,12},{9,13},{10,... | collective-permute-start | bytes 98312 | tf_op jit(solution)/shard_map/ppermute | solution.py:346
  58.9 1.6 %copy-start.17 = (bf16[1,1024,1024]{2,1,0:T(8,128)(2,1)S(1)}, bf16[1,1024,1024]{2,1,0:T(8,128)(2,1)}, u32[]{:S(2)}) copy-start(bf16[1,1024,1024]{2,1,0:T(8,128)(2,1)} %param.19) | copy-start | bytes 6291460
  60.5 1.6 %copy-start.18 = (bf16[2,512,1024]{2,1,0:T(8,128)(2,1)S(1)}, bf16[2,512,1024]{2,1,0:T(8,128)(2,1)}, u32[]{:S(2)}) copy-start(bf16[2,512,1024]{2,1,0:T(8,128)(2,1)} %get-tuple-element.20.mixed_ref) | copy-start | bytes 6291460
  62.1 13.7 %copy-start.15 = (s32[16]{0:T(128)S(1)}, s32[16]{0:T(128)}, u32[]{:S(2)}) copy-start(s32[16]{0:T(128)} %targets_ref.1) | copy-start | bytes 196
  68.3 4.8 %collective-permute-start.9 = (f32[8,8,128]{2,1,0:T(8,128)}, f32[8,8,128]{2,1,0:T(8,128)S(1)}, u32[]{:S(2)}, u32[]{:S(2)}) collective-permute-start(f32[8,8,128]{2,1,0:T(8,128)} %get-tuple-element.23), channel_id=1, source_target_pairs={{0,1},{1,0},{2,3},{3,2},{4,5},{5,4},{6,7},{7,6},{8,9},{9,8},{10,11... | collective-permute-start | bytes 98312 | tf_op jit(solution)/shard_map/ppermute | solution.py:346
  71.5 3.0 %collective-permute-start.10 = (f32[8,8,128]{2,1,0:T(8,128)}, f32[8,8,128]{2,1,0:T(8,128)S(1)}, u32[]{:S(2)}, u32[]{:S(2)}) collective-permute-start(f32[8,8,128]{2,1,0:T(8,128)} %get-tuple-element.24), channel_id=1, source_target_pairs={{0,2},{1,3},{2,0},{3,1},{4,6},{5,7},{6,4},{7,5},{8,10},{9,11},{10,... | collective-permute-start | bytes 98312 | tf_op jit(solution)/shard_map/ppermute | solution.py:346
  72.2 3.6 %collective-permute-start.11 = (f32[8,8,128]{2,1,0:T(8,128)}, f32[8,8,128]{2,1,0:T(8,128)S(1)}, u32[]{:S(2)}, u32[]{:S(2)}) collective-permute-start(f32[8,8,128]{2,1,0:T(8,128)} %get-tuple-element.25), channel_id=1, source_target_pairs={{0,3},{1,2},{2,1},{3,0},{4,7},{5,6},{6,5},{7,4},{8,11},{9,10},{10,... | collective-permute-start | bytes 98312 | tf_op jit(solution)/shard_map/ppermute | solution.py:346
  75.8 0.8 copy-start.8
  (9 other events, 5.9 us)

commit v3 on v2

--- a/solution.py
+++ b/solution.py
@@ -56,35 +56,37 @@
     return jnp.concatenate([sums, padding], 0).T
 
 
-def local_kernel(lengths_ref, tokens_hbm, w_query_hbm, w_key_hbm, w_value_hbm, decay_hbm,
-                 total_hbm, mixed_hbm,
-                 tokens_ref, w_query_ref, w_key_ref, w_value_ref, decay_ref,
-                 keys_ref, values_ref, total_ref, mixed_ref, in_sems, out_sems):
-    copies = []
-    for at, (source, target) in enumerate((
-            (decay_hbm, decay_ref), (tokens_hbm, tokens_ref), (w_key_hbm, w_key_ref),
-            (w_value_hbm, w_value_ref), (w_query_hbm, w_query_ref))):
-        copies.append(pltpu.make_async_copy(source, target, in_sems.at[at]))
-        copies[at].start()
-    outs = []
-
-    def send(source, target):
-        outs.append(pltpu.make_async_copy(source, target, out_sems.at[len(outs)]))
-        outs[-1].start()
-
+def place():
+    rank = lax.axis_index("seq")
+    return rank & 3, rank >> 2
+
+
+def fetch_kernel(stash_ref, own_ref):
+    own_ref[...] = stash_ref[0]
+
+
+def fetch_call(stash):
+    return pl.pallas_call(
+        fetch_kernel,
+        in_specs=[IN_VMEM],
+        out_specs=IN_VMEM,
+        out_shape=jax.ShapeDtypeStruct((HEADS, 8, DIM), jnp.float32),
+        compiler_params=params(8),
+        cost_estimate=pl.CostEstimate(flops=2 ** 36, bytes_accessed=2 ** 30, transcendentals=2 ** 30),
+        name="own_rows",
+    )(stash)
+
+
+def keys_kernel(lengths_ref, tokens_ref, w_key_ref, w_value_ref, decay_ref, *refs):
+    quarters = refs[:4]
+    keys_ref, values_ref, sums_ref, quarter_ref = refs[4:]
     valid = lengths_ref[0] - lax.axis_index("seq") * STEPS
-    copies[0].wait()
     lane = lax.broadcasted_iota(jnp.int32, (HEADS, STEPS), 1)
     sums = running_sum(jnp.where(lane < valid, decay_ref[...] * LOG2E, 0.0))
+    sums_ref[...] = sums
     growth = jnp.broadcast_to(sums[:, STEPS - 1:], (HEADS, DIM))
-    total_ref[:, HEADS] = jnp.broadcast_to(growth[None], (SHARDS, HEADS, DIM))
     tails = jnp.exp2(sums[:, STEPS - 1:] - sums)
-    columns = turned(sums)
     alive = lax.broadcasted_iota(jnp.int32, (STEPS, PAIR), 0) < valid
-    causal = (lax.broadcasted_iota(jnp.int32, (DIM, DIM), 0)
-              >= lax.broadcasted_iota(jnp.int32, (DIM, DIM), 1))
-    for copy in copies[1:4]:
-        copy.wait()
     tokens = tokens_ref[...]
     for pair in range(4):
         lanes = lanes_of(pair)
@@ -99,9 +101,37 @@
             own = lanes_of(j, DIM)
             decayed = (keys_t[own].astype(jnp.float32) * tails[head:head + 1]).astype(jnp.bfloat16)
             total = jnp.dot(decayed, values[:, own], preferred_element_type=jnp.float32)
-            total_ref[:, head] = total.reshape(SHARDS, 8, DIM)
-    send(total_ref, total_hbm)
-    copies[4].wait()
+            for block in range(SHARDS):
+                quarter_ref[block % 4, (block // 4) * HEADS + head] = total[block * 8:(block + 1) * 8]
+    x, _ = place()
+    for k, out in enumerate(quarters):
+        out[:32] = quarter_ref[x ^ k]
+        out[32] = growth
+
+
+def keys_call(lengths, tokens, w_key, w_value, decay):
+    return pl.pallas_call(
+        keys_kernel,
+        in_specs=[IN_SMEM] + [IN_VMEM] * 4,
+        out_specs=[IN_VMEM] * 7,
+        out_shape=[jax.ShapeDtypeStruct((33, 8, DIM), jnp.float32)] * 4 + [
+            jax.ShapeDtypeStruct((WIDTH, STEPS), jnp.bfloat16),
+            jax.ShapeDtypeStruct((STEPS, WIDTH), jnp.bfloat16),
+            jax.ShapeDtypeStruct((HEADS, STEPS), jnp.float32),
+        ],
+        scratch_shapes=[pltpu.VMEM((4, 32, 8, DIM), jnp.float32)],
+        compiler_params=params(16),
+        cost_estimate=work(2 * STEPS * WIDTH * WIDTH * 3, 16 * MIB),
+        name="keys_values",
+    )(lengths, tokens, w_key, w_value, decay)
+
+
+def inner_kernel(tokens_ref, w_query_ref, keys_ref, values_ref, sums_ref, after_ref, mixed_ref):
+    sums = sums_ref[...]
+    columns = turned(sums)
+    causal = (lax.broadcasted_iota(jnp.int32, (DIM, DIM), 0)
+              >= lax.broadcasted_iota(jnp.int32, (DIM, DIM), 1))
+    tokens = tokens_ref[...]
     for pair in range(4):
         lanes = lanes_of(pair)
         queries = jnp.dot(tokens, w_query_ref[:, lanes], preferred_element_type=jnp.float32).astype(jnp.bfloat16)
@@ -110,11 +140,18 @@
             own = lanes_of(head, DIM)
             attend(causal, sums[head:head + 1], columns[:, head:head + 1], queries[:, lanes_of(j, DIM)],
                    keys_ref[own, :], values_ref[:, own], own, mixed_ref)
-        if pair % 2 == 1:
-            done = slice((pair - 1) * PAIR, (pair + 1) * PAIR)
-            send(mixed_ref.at[:, :, done], mixed_hbm.at[:, :, done])
-    for copy in outs:
-        copy.wait()
+
+
+def inner_call(tokens, w_query, keys, values, sums, after):
+    return pl.pallas_call(
+        inner_kernel,
+        in_specs=[IN_VMEM] * 5 + [pl.BlockSpec(memory_space=pl.ANY)],
+        out_specs=IN_VMEM,
+        out_shape=jax.ShapeDtypeStruct((2, STEPS, WIDTH), jnp.bfloat16),
+        compiler_params=params(16),
+        cost_estimate=work(2 * STEPS * WIDTH * WIDTH * 3, 5 * MIB),
+        name="queries_inner",
+    )(tokens, w_query, keys, values, sums, after)
 
 
 def attend(causal, row, column, queries, keys_t, values, own, mixed_ref):
@@ -150,84 +187,95 @@
         mixed_ref[1, rows, own] = part.astype(jnp.bfloat16)
 
 
-def local_call(lengths, tokens, w_query, w_key, w_value, decay):
-    return pl.pallas_call(
-        local_kernel,
-        in_specs=[IN_SMEM] + [IN_HBM] * 5,
-        out_specs=[IN_HBM] * 2,
-        out_shape=[
-            jax.ShapeDtypeStruct((SHARDS, HEADS + 1, 8, DIM), jnp.float32),
-            jax.ShapeDtypeStruct((2, STEPS, WIDTH), jnp.bfloat16),
-        ],
-        scratch_shapes=[
-            pltpu.VMEM((STEPS, WIDTH), jnp.bfloat16),
-            pltpu.VMEM((WIDTH, WIDTH), jnp.bfloat16),
-            pltpu.VMEM((WIDTH, WIDTH), jnp.bfloat16),
-            pltpu.VMEM((WIDTH, WIDTH), jnp.bfloat16),
-            pltpu.VMEM((HEADS, STEPS), jnp.float32),
-            pltpu.VMEM((WIDTH, STEPS), jnp.bfloat16),
-            pltpu.VMEM((STEPS, WIDTH), jnp.bfloat16),
-            pltpu.VMEM((SHARDS, HEADS + 1, 8, DIM), jnp.float32),
-            pltpu.VMEM((2, STEPS, WIDTH), jnp.bfloat16),
-            DMA((5,)),
-            DMA((3,)),
-        ],
-        compiler_params=params(62),
-        cost_estimate=work(2 * STEPS * WIDTH * WIDTH * 4, 10 * MIB),
-        name="local_pass",
-    )(lengths, tokens, w_query, w_key, w_value, decay)
-
-
-def scan_kernel(sources_ref, received_ref, *refs):
-    items = refs[:7]
-    carried_hbm, closing_ref, start_ref, rows_ref, sems = refs[7:]
+def row_kernel(sources_ref, *refs):
+    quarters, items = refs[:4], refs[4:11]
+    ordered_ref, payload_ref = refs[11:]
+    x, _ = place()
     number = landing(sources_ref[lax.axis_index("asset")])
     for k, item in enumerate(items):
         @pl.when(number == k)
         def _(item=item):
-            start_ref[...] = item[...]
-    states = [start_ref[head] for head in range(HEADS)]
-    outs = []
-    for shard in range(SHARDS):
-        for head in range(HEADS):
-            rows_ref[shard, head] = states[head]
-            growth = jnp.exp2(received_ref[shard, HEADS, head:head + 1, :])
-            states[head] = growth * states[head] + received_ref[shard, head]
-        if shard % 4 == 3:
-            done = slice(shard - 3, shard + 1)
-            outs.append(pltpu.make_async_copy(rows_ref.at[done], carried_hbm.at[done], sems.at[shard // 4]))
-            outs[-1].start()
-    for head in range(HEADS):
-        closing_ref[head] = states[head]
-    for copy in outs:
-        copy.wait()
-
-
-def scan_call(sources, received, items):
-    return pl.pallas_call(
-        scan_kernel,
-        in_specs=[IN_SMEM] + [IN_VMEM] * 8,
-        out_specs=[IN_HBM, IN_VMEM],
+            payload_ref[33:41] = item[...]
+    for k, quarter in enumerate(quarters):
+        ordered_ref[x ^ k] = quarter[...]
+    for row in range(32):
+        head = row % HEADS
+        state = ordered_ref[0, row]
+        for shard in range(1, 4):
+            state = jnp.exp2(ordered_ref[shard, 32, head:head + 1]) * state + ordered_ref[shard, row]
+        payload_ref[row] = state
+    growth = ordered_ref[0, 32]
+    for shard in range(1, 4):
+        growth = growth + ordered_ref[shard, 32]
+    payload_ref[32] = growth
+
+
+def row_call(sources, quarters, items):
+    return pl.pallas_call(
+        row_kernel,
+        in_specs=[IN_SMEM] + [IN_VMEM] * 11,
+        out_specs=[IN_VMEM] * 2,
         out_shape=[
-            jax.ShapeDtypeStruct((SHARDS, HEADS, 8, DIM), jnp.float32),
-            jax.ShapeDtypeStruct((HEADS, 8, DIM), jnp.float32),
+            jax.ShapeDtypeStruct((4, 33, 8, DIM), jnp.float32),
+            jax.ShapeDtypeStruct((41, 8, DIM), jnp.float32),
         ],
+        compiler_params=params(8),
+        cost_estimate=work(MIB, 16 * MIB),
+        name="row_totals",
+    )(sources, *quarters, *items)
+
+
+def carry_kernel(*refs):
+    payloads, ordered_ref, carried = refs[:4], refs[4], refs[6:10]
+    closing_ref, rows_ref, carry_ref, final_ref = refs[10:]
+    x, y = place()
+    for m, payload in enumerate(payloads):
+        rows_ref[y ^ m] = payload[...]
+    for row in range(32):
+        head, block = row % HEADS, row // HEADS
+        state = rows_ref[block, 33 + head]
+        carry = state
+        for line in range(4):
+            carry = jnp.where(y == line, state, carry)
+            state = jnp.exp2(rows_ref[line, 32, head:head + 1]) * state + rows_ref[line, row]
+        final_ref[block, head] = state
+        carry_ref[0, row] = carry
+        for shard in range(3):
+            carry = jnp.exp2(ordered_ref[shard, 32, head:head + 1]) * carry + ordered_ref[shard, row]
+            carry_ref[shard + 1, row] = carry
+    for k, out in enumerate(carried):
+        out[...] = carry_ref[x ^ k]
+    closing_ref[...] = final_ref[y]
+
+
+def carry_call(payloads, ordered, after):
+    return pl.pallas_call(
+        carry_kernel,
+        in_specs=[IN_VMEM] * 5 + [pl.BlockSpec(memory_space=pl.ANY)],
+        out_specs=[IN_VMEM] * 5,
+        out_shape=[jax.ShapeDtypeStruct((32, 8, DIM), jnp.float32)] * 4
+        + [jax.ShapeDtypeStruct((HEADS, 8, DIM), jnp.float32)],
         scratch_shapes=[
-            pltpu.VMEM((HEADS, 8, DIM), jnp.float32),
-            pltpu.VMEM((SHARDS, HEADS, 8, DIM), jnp.float32),
-            DMA((4,)),
+            pltpu.VMEM((4, 41, 8, DIM), jnp.float32),
+            pltpu.VMEM((4, 32, 8, DIM), jnp.float32),
+            pltpu.VMEM((4, HEADS, 8, DIM), jnp.float32),
         ],
         compiler_params=params(8),
         cost_estimate=work(MIB, 2 * MIB),
-        name="scan_rows",
-    )(sources, received, *items)
+        name="carry_rows",
+    )(*payloads, ordered, after)
 
 
 STRIP = 512
 
 
-def outer_kernel(lengths_ref, mixed_ref, state_ref, whiten_ref,
-                 features_hbm, out_ref, out_sems):
+def outer_kernel(lengths_ref, mixed_ref, *refs):
+    quarters, whiten_ref, features_hbm, mark_ref, out_ref, state_ref, out_sems = refs[:4], *refs[4:]
+    mark_ref[...] = jnp.zeros((8, DIM), jnp.float32)
+    x, _ = place()
+    for k, quarter in enumerate(quarters):
+        for block in range(4):
+            state_ref[4 * block + (x ^ k)] = quarter[block * HEADS:(block + 1) * HEADS]
     valid = lengths_ref[0] - lax.axis_index("seq") * STEPS
     states = []
     for head in range(HEADS):
@@ -262,20 +310,24 @@
         copy.wait()
 
 
-def outer_call(lengths, mixed, state, whiten):
+def outer_call(lengths, mixed, quarters, whiten):
     return pl.pallas_call(
         outer_kernel,
-        in_specs=[IN_SMEM] + [IN_VMEM] * 3,
-        out_specs=IN_HBM,
-        out_shape=jax.ShapeDtypeStruct((STEPS, WIDTH), jnp.bfloat16),
+        in_specs=[IN_SMEM] + [IN_VMEM] * 6,
+        out_specs=[IN_HBM, IN_VMEM],
+        out_shape=[
+            jax.ShapeDtypeStruct((STEPS, WIDTH), jnp.bfloat16),
+            jax.ShapeDtypeStruct((8, DIM), jnp.float32),
+        ],
         scratch_shapes=[
             pltpu.VMEM((STEPS, WIDTH), jnp.bfloat16),
+            pltpu.VMEM((SHARDS, HEADS, 8, DIM), jnp.float32),
             DMA((STEPS // STRIP,)),
         ],
         compiler_params=params(16),
         cost_estimate=work(2 * STEPS * WIDTH * WIDTH * 3 // 2, 4 * MIB),
         name="outer_whiten",
-    )(lengths, mixed, state, whiten)
+    )(lengths, mixed, *quarters, whiten)
 
 
 def origin(targets_ref, slot):
@@ -292,7 +344,7 @@
 
 
 def near_kernel(inverted, route_ref, *refs):
-    items, outs = refs[:4], refs[5:8]
+    items, outs = refs[:4], refs[-3:]
     me = lax.axis_index("asset")
     for j, out in enumerate(outs, 1):
         slot = me ^ j
@@ -304,18 +356,16 @@
                 out[...] = item[...]
 
 
-def near_call(inverted, route, items, passed):
+def near_call(inverted, route, items, after=()):
     return pl.pallas_call(
         functools.partial(near_kernel, inverted),
-        in_specs=[IN_SMEM] + [IN_VMEM] * 4 + [pl.BlockSpec(memory_space=pl.ANY)],
-        out_specs=[IN_VMEM] * 3 + [pl.BlockSpec(memory_space=pl.ANY)],
-        out_shape=[jax.ShapeDtypeStruct((HEADS, 8, DIM), jnp.float32)] * 3
-        + [jax.ShapeDtypeStruct(passed.shape, passed.dtype)],
-        input_output_aliases={5: 3},
-        compiler_params=params(63),
-        cost_estimate=work(1024, 2 ** 17),
+        in_specs=[IN_SMEM] + [IN_VMEM] * 4 + [pl.BlockSpec(memory_space=pl.ANY)] * len(after),
+        out_specs=[IN_VMEM] * 3,
+        out_shape=[jax.ShapeDtypeStruct((HEADS, 8, DIM), jnp.float32)] * 3,
+        compiler_params=params(8),
+        cost_estimate=work(1024, 16 * MIB),
         name="near_rows",
-    )(route, *items, passed)
+    )(route, *items, *after)
 
 
 def kept_kernel(targets_ref, *refs):
@@ -342,23 +392,27 @@
     )(targets, *items)
 
 
-def swap(value, bits):
-    return lax.ppermute(value, "asset", [(k, k ^ bits) for k in range(SHARDS)])
+def swap(value, bits, axis="asset"):
+    return lax.ppermute(value, axis, [(k, k ^ bits) for k in range(SHARDS)])
 
 
 def on_device(tokens, w_query, w_key, w_value, decay_log, lengths, sources, targets, stash, whiten):
     tokens, decay, whiten = tokens[0], decay_log[0], whiten[0]
-    own = stash[0]
+    own = fetch_call(stash)
     items = [own] + [swap(own, 4 * k) for k in (1, 2, 3)]
-    total, mixed = local_call(lengths, tokens, w_query, w_key, w_value, decay)
-    *near, total = near_call(False, sources, items, total)
+    *quarters, keys, values, sums = keys_call(lengths, tokens, w_key, w_value, decay)
+    near = near_call(False, sources, items)
+    near, quarters = lax.optimization_barrier((near, quarters))
+    arrived = [quarters[0]] + [swap(quarters[k], k, "seq") for k in (1, 2, 3)]
     items += [swap(item, k) for k, item in enumerate(near, 1)]
-    received = lax.all_to_all(total, "seq", 0, 0, tiled=True)
-    carried, closing = scan_call(sources, received, items)
-    state = lax.all_to_all(carried, "seq", 0, 0, tiled=True)
+    ordered, payload = row_call(sources, arrived, items)
+    payloads = [payload] + [swap(payload, 4 * m, "seq") for m in (1, 2, 3)]
+    mixed = inner_call(tokens, w_query, keys, values, sums, payload)
+    *carried, closing = carry_call(payloads, ordered, mixed)
+    state = [carried[0]] + [swap(carried[k], k, "seq") for k in (1, 2, 3)]
     items = [closing] + [swap(closing, 4 * k) for k in (1, 2, 3)]
-    features = outer_call(lengths, mixed, state, whiten)
-    *near, features = near_call(True, targets, items, features)
+    features, mark = outer_call(lengths, mixed, state, whiten)
+    near = near_call(True, targets, items, (mark,))
     items += [swap(item, k) for k, item in enumerate(near, 1)]
     return (features[None], kept_call(targets, items))
 

time: 81.1 us -> 63.1 us (0.78)
  local copies, waits for them, and re-layouts: 10.3 us -> 0.79 us
  Pallas kernels: 21.2 us -> 15.4 us
  waiting for transfers between devices: 13.7 us -> 9.02 us
  starting transfers between devices: 33.4 us -> 36.1 us
    ppermute x12 -> x21, starting transfers between devices: 23 us -> 36.1 us  [swap(): return lax.ppermute(value, axis, [(k, k ^ bits) for k in range(SHARDS)])]
    all_to_all x2 -> x0, starting transfers between devices: 10.3 us -> none  [the longest x1 6.76 us: on_device(): received = lax.all_to_all(total, 'seq', 0, 0, tiled=True)]
    unnamed x38 -> x18, local copies, waits for them, and re-layouts: 10.3 us -> 0.79 us
    all_to_all x2 -> x0, waiting for transfers between devices: 8.08 us -> none  [the longest x1 4.56 us: on_device(): received = lax.all_to_all(total, 'seq', 0, 0, tiled=True)]
    pallas_call x3 -> x6, Pallas kernels: 16.9 us -> 12.9 us  [the longest x1 5.19 us: inner_call(): pl.pallas_call(inner_kernel, in_specs=[IN_VMEM] * 5 + [pl.BlockSpec(memor...]
    ppermute x12 -> x21, waiting for transfers between devices: 5.57 us -> 9.02 us  [swap(): return lax.ppermute(value, axis, [(k, k ^ bits) for k in range(SHARDS)])]
    pallas_call x2, Pallas kernels: 3.09 us -> 1.26 us  [near_call(): pl.pallas_call(functools.partial(near_kernel, inverted), in_specs=[IN_SME...]
  transfers between devices with their start and end apart: 14 -> 21, of which waited for: 6 -> 8; matrix products, arithmetic and copies ran while one was open for 0% -> 0% of each run, Pallas kernels for 19% -> 19%
where the time goes in v3:
time: 63.1 us; the launch traced here: 62.9 us
  starting transfers between devices  36.1 us (57%)
  Pallas kernels  15.4 us (24%)
  waiting for transfers between devices  9.02 us (14%)
  between operations  1.62 us (3%)
  local copies, waits for them, and re-layouts  0.79 us (1%)
    ppermute x21, starting transfers between devices, swap(): return lax.ppermute(value, axis, [(k, k ^ bits) for k in range(SHARDS)])  36.1 us
    ppermute x21, waiting for transfers between devices, swap(): return lax.ppermute(value, axis, [(k, k ^ bits) for k in range(SHARDS)])  9.02 us
    pallas_call x1, Pallas kernels, inner_call(): pl.pallas_call(inner_kernel, in_specs=[IN_VMEM] * 5 + [pl.BlockSpec(memor...  5.19 us
    pallas_call x1, Pallas kernels, outer_call(): pl.pallas_call(outer_kernel, in_specs=[IN_SMEM] + [IN_VMEM] * 6, out_spec...  3.45 us
    pallas_call x1, Pallas kernels, keys_call(): pl.pallas_call(keys_kernel, in_specs=[IN_SMEM] + [IN_VMEM] * 4, out_specs...  3.33 us
    pallas_call x2, Pallas kernels, near_call(): pl.pallas_call(functools.partial(near_kernel, inverted), in_specs=[IN_SME...  1.26 us
  transfers between devices with their start and end apart: 21, of which 8 were waited for; matrix products, arithmetic and copies ran while one was open for 0% of the time, Pallas kernels for 19%

profile of v3, /device:TPU:1, one launch (start us, length us, event | category | flops | bytes accessed | tf_op | source)
XLA Modules:
  0.0 62.9 jit_solution(11651381534619448213)
XLA Ops:
  1.4 6.9 %collective-permute-start.2 = (f32[8,8,128]{2,1,0:T(8,128)S(1)}, f32[8,8,128]{2,1,0:T(8,128)S(1)}, u32[]{:S(2)}, u32[]{:S(2)}) collective-permute-start(f32[8,8,128]{2,1,0:T(8,128)S(1)} %own_rows.1.refs_0_.refs_4_), channel_id=1, source_target_pairs={{0,12},{1,13},{2,14},{3,15},{4,8},{5,9},{6,10},{7,11},{8,4},{9,5},... | collective-permute-start | bytes 98312 | tf_op jit(solution)/shard_map/ppermute | solution.py:396
  8.3 1.0 %collective-permute-start.1 = (f32[8,8,128]{2,1,0:T(8,128)S(1)}, f32[8,8,128]{2,1,0:T(8,128)S(1)}, u32[]{:S(2)}, u32[]{:S(2)}) collective-permute-start(f32[8,8,128]{2,1,0:T(8,128)S(1)} %own_rows.1.refs_0_.refs_4_), channel_id=1, source_target_pairs={{0,8},{1,9},{2,10},{3,11},{4,12},{5,13},{6,14},{7,15},{8,0},{9,1},... | collective-permute-start | bytes 98312 | tf_op jit(solution)/shard_map/ppermute | solution.py:396
  9.3 1.2 %collective-permute-start = (f32[8,8,128]{2,1,0:T(8,128)S(1)}, f32[8,8,128]{2,1,0:T(8,128)S(1)}, u32[]{:S(2)}, u32[]{:S(2)}) collective-permute-start(f32[8,8,128]{2,1,0:T(8,128)S(1)} %own_rows.1.refs_0_.refs_4_), channel_id=1, source_target_pairs={{0,4},{1,5},{2,6},{3,7},{4,0},{5,1},{6,2},{7,3},{8,12},{9,13},{10,... | collective-permute-start | bytes 98312 | tf_op jit(solution)/shard_map/ppermute | solution.py:396
  11.2 3.3 %keys_values.1 = (f32[33,8,128]{2,1,0:T(8,128)S(1)}, f32[33,8,128]{2,1,0:T(8,128)S(1)}, f32[33,8,128]{2,1,0:T(8,128)S(1)}, f32[33,8,128]{2,1,0:T(8,128)S(1)}, bf...) custom-call(s32[1]{0:T(128)S(6)} %copy.12.lengths_ref, ...), custom_call_target="tpu_custom_call" | custom-call | flops 3221225472 | bytes 16777216 | tf_op jit(solution)/shard_map/keys_values/pallas_call | solution.py:113
  15.9 1.3 %collective-permute-start.3 = (f32[33,8,128]{2,1,0:T(8,128)S(1)}, f32[33,8,128]{2,1,0:T(8,128)S(1)}, u32[]{:S(2)}, u32[]{:S(2)}) collective-permute-start(f32[33,8,128]{2,1,0:T(8,128)S(1)} %get-tuple-element.42), channel_id=1, source_target_pairs={{0,16},{16,0},{32,48},{48,32},{64,80},{80,64},{96,112},{112,96},{1... | collective-permute-start | bytes 405512 | tf_op jit(solution)/shard_map/ppermute | solution.py:396
  17.2 2.5 %collective-permute-start.4 = (f32[33,8,128]{2,1,0:T(8,128)S(1)}, f32[33,8,128]{2,1,0:T(8,128)S(1)}, u32[]{:S(2)}, u32[]{:S(2)}) collective-permute-start(f32[33,8,128]{2,1,0:T(8,128)S(1)} %get-tuple-element.43), channel_id=1, source_target_pairs={{0,32},{16,48},{32,0},{48,16},{64,96},{80,112},{96,64},{112,80},{1... | collective-permute-start | bytes 405512 | tf_op jit(solution)/shard_map/ppermute | solution.py:396
  19.8 3.1 %collective-permute-start.6 = (f32[8,8,128]{2,1,0:T(8,128)S(1)}, f32[8,8,128]{2,1,0:T(8,128)S(1)}, u32[]{:S(2)}, u32[]{:S(2)}) collective-permute-start(f32[8,8,128]{2,1,0:T(8,128)S(1)} %get-tuple-element.45), channel_id=1, source_target_pairs={{0,1},{1,0},{2,3},{3,2},{4,5},{5,4},{6,7},{7,6},{8,9},{9,8},{10,11... | collective-permute-start | bytes 98312 | tf_op jit(solution)/shard_map/ppermute | solution.py:396
  23.8 1.0 %collective-permute-start.8 = (f32[8,8,128]{2,1,0:T(8,128)S(1)}, f32[8,8,128]{2,1,0:T(8,128)S(1)}, u32[]{:S(2)}, u32[]{:S(2)}) collective-permute-start(f32[8,8,128]{2,1,0:T(8,128)S(1)} %get-tuple-element.47), channel_id=1, source_target_pairs={{0,3},{1,2},{2,1},{3,0},{4,7},{5,6},{6,5},{7,4},{8,11},{9,10},{10,... | collective-permute-start | bytes 98312 | tf_op jit(solution)/shard_map/ppermute | solution.py:396
  24.8 1.2 %collective-permute-done.7.refs_9_ = f32[8,8,128]{2,1,0:T(8,128)S(1)} collective-permute-done((f32[8,8,128]{2,1,0:T(8,128)S(1)}, f32[8,8,128]{2,1,0:T(8,128)S(1)}, u32[]{:S(2)}, u32[]{:S(2)}) %collective-permute-start.7) | collective-permute-done | bytes 32800 | tf_op jit(solution)/shard_map/ppermute | solution.py:396
  26.0 1.4 %collective-permute-done.8.refs_10_ = f32[8,8,128]{2,1,0:T(8,128)S(1)} collective-permute-done((f32[8,8,128]{2,1,0:T(8,128)S(1)}, f32[8,8,128]{2,1,0:T(8,128)S(1)}, u32[]{:S(2)}, u32[]{:S(2)}) %collective-permute-start.8) | collective-permute-done | bytes 32800 | tf_op jit(solution)/shard_map/ppermute | solution.py:396
  28.1 2.8 %collective-permute-start.11 = (f32[41,8,128]{2,1,0:T(8,128)S(1)}, f32[41,8,128]{2,1,0:T(8,128)S(1)}, u32[]{:S(2)}, u32[]{:S(2)}) collective-permute-start(f32[41,8,128]{2,1,0:T(8,128)S(1)} %get-tuple-element.48.after_ref.refs_0_), channel_id=1, source_target_pairs={{0,192},{16,208},{32,224},{48,240},{64,128},{80,144},{96,160},{112... | collective-permute-start | bytes 503816 | tf_op jit(solution)/shard_map/ppermute | solution.py:396
  31.6 5.2 %queries_inner.1.refs_5_.mixed_ref = bf16[2,512,1024]{2,1,0:T(8,128)(2,1)S(1)} custom-call(bf16[512,1024]{1,0:T(8,128)(2,1)S(1)} %bitcast.6, bf16[1024,1024]{1,0:T(8,128)(2,1)S(1)} %copy-done.4, bf16[1024,512]{1,0:T(8,128)(2,1)S(1)} %get-tuple-element.31.keys_ref, bf16[512,1024]{1,0:T(8,128)(2,1)S(1)} %get-tuple-element.32.values_ref, ...), custom_call_target="tpu_custom_call" | custom-call | flops 3221225472 | bytes 5242880 | tf_op jit(solution)/shard_map/queries_inner/pallas_call | solution.py:146
  36.8 1.1 %collective-permute-done.11.refs_3_ = f32[41,8,128]{2,1,0:T(8,128)S(1)} collective-permute-done((f32[41,8,128]{2,1,0:T(8,128)S(1)}, f32[41,8,128]{2,1,0:T(8,128)S(1)}, u32[]{:S(2)}, u32[]{:S(2)}) %collective-permute-start.11) | collective-permute-done | bytes 167968 | tf_op jit(solution)/shard_map/ppermute | solution.py:396
  38.8 4.1 %collective-permute-start.13 = (f32[32,8,128]{2,1,0:T(8,128)S(1)}, f32[32,8,128]{2,1,0:T(8,128)S(1)}, u32[]{:S(2)}, u32[]{:S(2)}) collective-permute-start(f32[32,8,128]{2,1,0:T(8,128)S(1)} %get-tuple-element.52), channel_id=1, source_target_pairs={{0,32},{16,48},{32,0},{48,16},{64,96},{80,112},{96,64},{112,80},{1... | collective-permute-start | bytes 393224 | tf_op jit(solution)/shard_map/ppermute | solution.py:396
  42.9 2.3 %collective-permute-start.17 = (f32[8,8,128]{2,1,0:T(8,128)S(1)}, f32[8,8,128]{2,1,0:T(8,128)S(1)}, u32[]{:S(2)}, u32[]{:S(2)}) collective-permute-start(f32[8,8,128]{2,1,0:T(8,128)S(1)} %get-tuple-element.55.refs_0_), channel_id=1, source_target_pairs={{0,12},{1,13},{2,14},{3,15},{4,8},{5,9},{6,10},{7,11},{8,4},{9,5},... | collective-permute-start | bytes 98312 | tf_op jit(solution)/shard_map/ppermute | solution.py:396
  45.2 2.2 %collective-permute-start.16 = (f32[8,8,128]{2,1,0:T(8,128)S(1)}, f32[8,8,128]{2,1,0:T(8,128)S(1)}, u32[]{:S(2)}, u32[]{:S(2)}) collective-permute-start(f32[8,8,128]{2,1,0:T(8,128)S(1)} %get-tuple-element.55.refs_0_), channel_id=1, source_target_pairs={{0,8},{1,9},{2,10},{3,11},{4,12},{5,13},{6,14},{7,15},{8,0},{9,1},... | collective-permute-start | bytes 98312 | tf_op jit(solution)/shard_map/ppermute | solution.py:396
  47.4 1.2 %collective-permute-start.15 = (f32[8,8,128]{2,1,0:T(8,128)S(1)}, f32[8,8,128]{2,1,0:T(8,128)S(1)}, u32[]{:S(2)}, u32[]{:S(2)}) collective-permute-start(f32[8,8,128]{2,1,0:T(8,128)S(1)} %get-tuple-element.55.refs_0_), channel_id=1, source_target_pairs={{0,4},{1,5},{2,6},{3,7},{4,0},{5,1},{6,2},{7,3},{8,12},{9,13},{10,... | collective-permute-start | bytes 98312 | tf_op jit(solution)/shard_map/ppermute | solution.py:396
  48.6 1.9 %collective-permute-done.14.refs_3_ = f32[32,8,128]{2,1,0:T(8,128)S(1)} collective-permute-done((f32[32,8,128]{2,1,0:T(8,128)S(1)}, f32[32,8,128]{2,1,0:T(8,128)S(1)}, u32[]{:S(2)}, u32[]{:S(2)}) %collective-permute-start.14) | collective-permute-done | bytes 131104 | tf_op jit(solution)/shard_map/ppermute | solution.py:396
  50.4 3.5 %outer_whiten.1 = (bf16[512,1024]{1,0:T(8,128)(2,1)}, f32[8,128]{1,0:T(8,128)S(1)}) custom-call(s32[1]{0:T(128)S(6)} %copy.12.lengths_ref, bf16[2,512,1024]{2,1,0:T(8,128)(2,1)S(1)} %queries_inner.1.refs_5_.mixed_ref, f32[32,8,128]{2,1,0:T(8,128)S(1)} %get-tuple-element.50.refs_0_, f32[32,8,128]{2,1,0:T(8,128)S(1)} %collective-permute-done.12.refs_1_, ...), custom_call_target="tpu_custom_call" | custom-call | flops 1610612736 | bytes 4194304 | tf_op jit(solution)/shard_map/outer_whiten/pallas_call | solution.py:314
  54.6 2.8 %collective-permute-start.18 = (f32[8,8,128]{2,1,0:T(8,128)S(1)}, f32[8,8,128]{2,1,0:T(8,128)S(1)}, u32[]{:S(2)}, u32[]{:S(2)}) collective-permute-start(f32[8,8,128]{2,1,0:T(8,128)S(1)} %get-tuple-element.57), channel_id=1, source_target_pairs={{0,1},{1,0},{2,3},{3,2},{4,5},{5,4},{6,7},{7,6},{8,9},{9,8},{10,11... | collective-permute-start | bytes 98312 | tf_op jit(solution)/shard_map/ppermute | solution.py:396
  58.2 1.0 %collective-permute-start.20 = (f32[8,8,128]{2,1,0:T(8,128)S(1)}, f32[8,8,128]{2,1,0:T(8,128)S(1)}, u32[]{:S(2)}, u32[]{:S(2)}) collective-permute-start(f32[8,8,128]{2,1,0:T(8,128)S(1)} %get-tuple-element.59), channel_id=1, source_target_pairs={{0,3},{1,2},{2,1},{3,0},{4,7},{5,6},{6,5},{7,4},{8,11},{9,10},{10,... | collective-permute-start | bytes 98312 | tf_op jit(solution)/shard_map/ppermute | solution.py:396
  59.2 1.0 %collective-permute-done.19.refs_5_ = f32[8,8,128]{2,1,0:T(8,128)S(1)} collective-permute-done((f32[8,8,128]{2,1,0:T(8,128)S(1)}, f32[8,8,128]{2,1,0:T(8,128)S(1)}, u32[]{:S(2)}, u32[]{:S(2)}) %collective-permute-start.19) | collective-permute-done | bytes 32800 | tf_op jit(solution)/shard_map/ppermute | solution.py:396
  60.2 1.3 %collective-permute-done.20.refs_6_ = f32[8,8,128]{2,1,0:T(8,128)S(1)} collective-permute-done((f32[8,8,128]{2,1,0:T(8,128)S(1)}, f32[8,8,128]{2,1,0:T(8,128)S(1)}, u32[]{:S(2)}, u32[]{:S(2)}) %collective-permute-start.20) | collective-permute-done | bytes 32800 | tf_op jit(solution)/shard_map/ppermute | solution.py:396
  61.6 1.2 %kept_rows.1 = f32[1,8,8,128]{3,2,1,0:T(8,128)} custom-call(s32[16]{0:T(128)S(1)} %copy-done, f32[8,8,128]{2,1,0:T(8,128)S(1)} %get-tuple-element.55.refs_0_, f32[8,8,128]{2,1,0:T(8,128)S(1)} %collective-permute-done.15.refs_1_, f32[8,8,128]{2,1,0:T(8,128)S(1)} %collective-permute-done.16.refs_2_, f32[8,8,128]{2,1,0:T(8,128)S(1)} %collective-permute-done.17.refs_3_, ...), custom_call_target="tpu_custom_call" | custom-call | flops 1024 | bytes 131072 | tf_op jit(solution)/shard_map/kept_rows/pallas_call | solution.py:383
  (45 shorter events, 6.8 us)
Async XLA Ops:
  1.4 9.8 %copy-start.8 = (f32[1,8,512]{2,1,0:T(8,128)S(1)}, f32[1,8,512]{2,1,0:T(8,128)}, u32[]{:S(2)}) copy-start(f32[1,8,512]{2,1,0:T(8,128)} %param.14) | copy-start | bytes 49156
  1.4 13.2 %collective-permute-start.2 = (f32[8,8,128]{2,1,0:T(8,128)S(1)}, f32[8,8,128]{2,1,0:T(8,128)S(1)}, u32[]{:S(2)}, u32[]{:S(2)}) collective-permute-start(f32[8,8,128]{2,1,0:T(8,128)S(1)} %own_rows.1.refs_0_.refs_4_), channel_id=1, source_target_pairs={{0,12},{1,13},{2,14},{3,15},{4,8},{5,9},{6,10},{7,11},{8,4},{9,5},... | collective-permute-start | bytes 98312 | tf_op jit(solution)/shard_map/ppermute | solution.py:396
  8.3 6.9 %collective-permute-start.1 = (f32[8,8,128]{2,1,0:T(8,128)S(1)}, f32[8,8,128]{2,1,0:T(8,128)S(1)}, u32[]{:S(2)}, u32[]{:S(2)}) collective-permute-start(f32[8,8,128]{2,1,0:T(8,128)S(1)} %own_rows.1.refs_0_.refs_4_), channel_id=1, source_target_pairs={{0,8},{1,9},{2,10},{3,11},{4,12},{5,13},{6,14},{7,15},{8,0},{9,1},... | collective-permute-start | bytes 98312 | tf_op jit(solution)/shard_map/ppermute | solution.py:396
  9.3 5.9 %collective-permute-start = (f32[8,8,128]{2,1,0:T(8,128)S(1)}, f32[8,8,128]{2,1,0:T(8,128)S(1)}, u32[]{:S(2)}, u32[]{:S(2)}) collective-permute-start(f32[8,8,128]{2,1,0:T(8,128)S(1)} %own_rows.1.refs_0_.refs_4_), channel_id=1, source_target_pairs={{0,4},{1,5},{2,6},{3,7},{4,0},{5,1},{6,2},{7,3},{8,12},{9,13},{10,... | collective-permute-start | bytes 98312 | tf_op jit(solution)/shard_map/ppermute | solution.py:396
  11.2 20.4 %copy-start.4 = (bf16[1024,1024]{1,0:T(8,128)(2,1)S(1)}, bf16[1024,1024]{1,0:T(8,128)(2,1)}, u32[]{:S(2)}) copy-start(bf16[1024,1024]{1,0:T(8,128)(2,1)} %w_query_ref.1) | copy-start | bytes 6291460
  15.9 11.6 %collective-permute-start.3 = (f32[33,8,128]{2,1,0:T(8,128)S(1)}, f32[33,8,128]{2,1,0:T(8,128)S(1)}, u32[]{:S(2)}, u32[]{:S(2)}) collective-permute-start(f32[33,8,128]{2,1,0:T(8,128)S(1)} %get-tuple-element.42), channel_id=1, source_target_pairs={{0,16},{16,0},{32,48},{48,32},{64,80},{80,64},{96,112},{112,96},{1... | collective-permute-start | bytes 405512 | tf_op jit(solution)/shard_map/ppermute | solution.py:396
  17.2 10.3 %collective-permute-start.4 = (f32[33,8,128]{2,1,0:T(8,128)S(1)}, f32[33,8,128]{2,1,0:T(8,128)S(1)}, u32[]{:S(2)}, u32[]{:S(2)}) collective-permute-start(f32[33,8,128]{2,1,0:T(8,128)S(1)} %get-tuple-element.43), channel_id=1, source_target_pairs={{0,32},{16,48},{32,0},{48,16},{64,96},{80,112},{96,64},{112,80},{1... | collective-permute-start | bytes 405512 | tf_op jit(solution)/shard_map/ppermute | solution.py:396
  19.6 7.8 %collective-permute-start.5 = (f32[33,8,128]{2,1,0:T(8,128)S(1)}, f32[33,8,128]{2,1,0:T(8,128)S(1)}, u32[]{:S(2)}, u32[]{:S(2)}) collective-permute-start(f32[33,8,128]{2,1,0:T(8,128)S(1)} %get-tuple-element.44), channel_id=1, source_target_pairs={{0,48},{16,32},{32,16},{48,0},{64,112},{80,96},{96,80},{112,64},{1... | collective-permute-start | bytes 405512 | tf_op jit(solution)/shard_map/ppermute | solution.py:396
  19.8 4.0 %collective-permute-start.6 = (f32[8,8,128]{2,1,0:T(8,128)S(1)}, f32[8,8,128]{2,1,0:T(8,128)S(1)}, u32[]{:S(2)}, u32[]{:S(2)}) collective-permute-start(f32[8,8,128]{2,1,0:T(8,128)S(1)} %get-tuple-element.45), channel_id=1, source_target_pairs={{0,1},{1,0},{2,3},{3,2},{4,5},{5,4},{6,7},{7,6},{8,9},{9,8},{10,11... | collective-permute-start | bytes 98312 | tf_op jit(solution)/shard_map/ppermute | solution.py:396
  22.9 3.1 %collective-permute-start.7 = (f32[8,8,128]{2,1,0:T(8,128)S(1)}, f32[8,8,128]{2,1,0:T(8,128)S(1)}, u32[]{:S(2)}, u32[]{:S(2)}) collective-permute-start(f32[8,8,128]{2,1,0:T(8,128)S(1)} %get-tuple-element.46), channel_id=1, source_target_pairs={{0,2},{1,3},{2,0},{3,1},{4,6},{5,7},{6,4},{7,5},{8,10},{9,11},{10,... | collective-permute-start | bytes 98312 | tf_op jit(solution)/shard_map/ppermute | solution.py:396
  23.8 3.6 %collective-permute-start.8 = (f32[8,8,128]{2,1,0:T(8,128)S(1)}, f32[8,8,128]{2,1,0:T(8,128)S(1)}, u32[]{:S(2)}, u32[]{:S(2)}) collective-permute-start(f32[8,8,128]{2,1,0:T(8,128)S(1)} %get-tuple-element.47), channel_id=1, source_target_pairs={{0,3},{1,2},{2,1},{3,0},{4,7},{5,6},{6,5},{7,4},{8,11},{9,10},{10,... | collective-permute-start | bytes 98312 | tf_op jit(solution)/shard_map/ppermute | solution.py:396
  28.1 9.8 %collective-permute-start.11 = (f32[41,8,128]{2,1,0:T(8,128)S(1)}, f32[41,8,128]{2,1,0:T(8,128)S(1)}, u32[]{:S(2)}, u32[]{:S(2)}) collective-permute-start(f32[41,8,128]{2,1,0:T(8,128)S(1)} %get-tuple-element.48.after_ref.refs_0_), channel_id=1, source_target_pairs={{0,192},{16,208},{32,224},{48,240},{64,128},{80,144},{96,160},{112... | collective-permute-start | bytes 503816 | tf_op jit(solution)/shard_map/ppermute | solution.py:396
  30.9 7.0 %collective-permute-start.10 = (f32[41,8,128]{2,1,0:T(8,128)S(1)}, f32[41,8,128]{2,1,0:T(8,128)S(1)}, u32[]{:S(2)}, u32[]{:S(2)}) collective-permute-start(f32[41,8,128]{2,1,0:T(8,128)S(1)} %get-tuple-element.48.after_ref.refs_0_), channel_id=1, source_target_pairs={{0,128},{16,144},{32,160},{48,176},{64,192},{80,208},{96,224},{112... | collective-permute-start | bytes 503816 | tf_op jit(solution)/shard_map/ppermute | solution.py:396
  31.3 7.0 %collective-permute-start.9 = (f32[41,8,128]{2,1,0:T(8,128)S(1)}, f32[41,8,128]{2,1,0:T(8,128)S(1)}, u32[]{:S(2)}, u32[]{:S(2)}) collective-permute-start(f32[41,8,128]{2,1,0:T(8,128)S(1)} %get-tuple-element.48.after_ref.refs_0_), channel_id=1, source_target_pairs={{0,64},{16,80},{32,96},{48,112},{64,0},{80,16},{96,32},{112,48},{1... | collective-permute-start | bytes 503816 | tf_op jit(solution)/shard_map/ppermute | solution.py:396
  36.8 13.6 %copy-start.5 = (bf16[1,1024,1024]{2,1,0:T(8,128)(2,1)S(1)}, bf16[1,1024,1024]{2,1,0:T(8,128)(2,1)}, u32[]{:S(2)}) copy-start(bf16[1,1024,1024]{2,1,0:T(8,128)(2,1)} %param.19) | copy-start | bytes 6291460
  38.5 8.9 %collective-permute-start.12 = (f32[32,8,128]{2,1,0:T(8,128)S(1)}, f32[32,8,128]{2,1,0:T(8,128)S(1)}, u32[]{:S(2)}, u32[]{:S(2)}) collective-permute-start(f32[32,8,128]{2,1,0:T(8,128)S(1)} %get-tuple-element.51), channel_id=1, source_target_pairs={{0,16},{16,0},{32,48},{48,32},{64,80},{80,64},{96,112},{112,96},{1... | collective-permute-start | bytes 393224 | tf_op jit(solution)/shard_map/ppermute | solution.py:396
  38.8 9.7 %collective-permute-start.13 = (f32[32,8,128]{2,1,0:T(8,128)S(1)}, f32[32,8,128]{2,1,0:T(8,128)S(1)}, u32[]{:S(2)}, u32[]{:S(2)}) collective-permute-start(f32[32,8,128]{2,1,0:T(8,128)S(1)} %get-tuple-element.52), channel_id=1, source_target_pairs={{0,32},{16,48},{32,0},{48,16},{64,96},{80,112},{96,64},{112,80},{1... | collective-permute-start | bytes 393224 | tf_op jit(solution)/shard_map/ppermute | solution.py:396
  42.9 7.5 %collective-permute-start.14 = (f32[32,8,128]{2,1,0:T(8,128)S(1)}, f32[32,8,128]{2,1,0:T(8,128)S(1)}, u32[]{:S(2)}, u32[]{:S(2)}) collective-permute-start(f32[32,8,128]{2,1,0:T(8,128)S(1)} %get-tuple-element.53), channel_id=1, source_target_pairs={{0,48},{16,32},{32,16},{48,0},{64,112},{80,96},{96,80},{112,64},{1... | collective-permute-start | bytes 393224 | tf_op jit(solution)/shard_map/ppermute | solution.py:396
  42.9 11.0 %collective-permute-start.17 = (f32[8,8,128]{2,1,0:T(8,128)S(1)}, f32[8,8,128]{2,1,0:T(8,128)S(1)}, u32[]{:S(2)}, u32[]{:S(2)}) collective-permute-start(f32[8,8,128]{2,1,0:T(8,128)S(1)} %get-tuple-element.55.refs_0_), channel_id=1, source_target_pairs={{0,12},{1,13},{2,14},{3,15},{4,8},{5,9},{6,10},{7,11},{8,4},{9,5},... | collective-permute-start | bytes 98312 | tf_op jit(solution)/shard_map/ppermute | solution.py:396
  45.2 8.7 %collective-permute-start.16 = (f32[8,8,128]{2,1,0:T(8,128)S(1)}, f32[8,8,128]{2,1,0:T(8,128)S(1)}, u32[]{:S(2)}, u32[]{:S(2)}) collective-permute-start(f32[8,8,128]{2,1,0:T(8,128)S(1)} %get-tuple-element.55.refs_0_), channel_id=1, source_target_pairs={{0,8},{1,9},{2,10},{3,11},{4,12},{5,13},{6,14},{7,15},{8,0},{9,1},... | collective-permute-start | bytes 98312 | tf_op jit(solution)/shard_map/ppermute | solution.py:396
  47.4 6.5 %collective-permute-start.15 = (f32[8,8,128]{2,1,0:T(8,128)S(1)}, f32[8,8,128]{2,1,0:T(8,128)S(1)}, u32[]{:S(2)}, u32[]{:S(2)}) collective-permute-start(f32[8,8,128]{2,1,0:T(8,128)S(1)} %get-tuple-element.55.refs_0_), channel_id=1, source_target_pairs={{0,4},{1,5},{2,6},{3,7},{4,0},{5,1},{6,2},{7,3},{8,12},{9,13},{10,... | collective-permute-start | bytes 98312 | tf_op jit(solution)/shard_map/ppermute | solution.py:396
  54.6 4.6 %collective-permute-start.18 = (f32[8,8,128]{2,1,0:T(8,128)S(1)}, f32[8,8,128]{2,1,0:T(8,128)S(1)}, u32[]{:S(2)}, u32[]{:S(2)}) collective-permute-start(f32[8,8,128]{2,1,0:T(8,128)S(1)} %get-tuple-element.57), channel_id=1, source_target_pairs={{0,1},{1,0},{2,3},{3,2},{4,5},{5,4},{6,7},{7,6},{8,9},{9,8},{10,11... | collective-permute-start | bytes 98312 | tf_op jit(solution)/shard_map/ppermute | solution.py:396
  57.4 2.8 %collective-permute-start.19 = (f32[8,8,128]{2,1,0:T(8,128)S(1)}, f32[8,8,128]{2,1,0:T(8,128)S(1)}, u32[]{:S(2)}, u32[]{:S(2)}) collective-permute-start(f32[8,8,128]{2,1,0:T(8,128)S(1)} %get-tuple-element.58), channel_id=1, source_target_pairs={{0,2},{1,3},{2,0},{3,1},{4,6},{5,7},{6,4},{7,5},{8,10},{9,11},{10,... | collective-permute-start | bytes 98312 | tf_op jit(solution)/shard_map/ppermute | solution.py:396
  58.2 3.4 %collective-permute-start.20 = (f32[8,8,128]{2,1,0:T(8,128)S(1)}, f32[8,8,128]{2,1,0:T(8,128)S(1)}, u32[]{:S(2)}, u32[]{:S(2)}) collective-permute-start(f32[8,8,128]{2,1,0:T(8,128)S(1)} %get-tuple-element.59), channel_id=1, source_target_pairs={{0,3},{1,2},{2,1},{3,0},{4,7},{5,6},{6,5},{7,4},{8,11},{9,10},{10,... | collective-permute-start | bytes 98312 | tf_op jit(solution)/shard_map/ppermute | solution.py:396
  (6 other events, 37.7 us)

commit v4 on v3

--- a/solution.py
+++ b/solution.py
@@ -61,20 +61,19 @@
     return rank & 3, rank >> 2
 
 
-def fetch_kernel(stash_ref, own_ref):
-    own_ref[...] = stash_ref[0]
-
-
-def fetch_call(stash):
-    return pl.pallas_call(
-        fetch_kernel,
-        in_specs=[IN_VMEM],
+def mark_kernel(mark_ref):
+    mark_ref[...] = jnp.zeros((8, DIM), jnp.float32)
+
+
+def mark_call():
+    return pl.pallas_call(
+        mark_kernel,
         out_specs=IN_VMEM,
-        out_shape=jax.ShapeDtypeStruct((HEADS, 8, DIM), jnp.float32),
+        out_shape=jax.ShapeDtypeStruct((8, DIM), jnp.float32),
         compiler_params=params(8),
         cost_estimate=pl.CostEstimate(flops=2 ** 36, bytes_accessed=2 ** 30, transcendentals=2 ** 30),
-        name="own_rows",
-    )(stash)
+        name="mark",
+    )()
 
 
 def keys_kernel(lengths_ref, tokens_ref, w_key_ref, w_value_ref, decay_ref, *refs):
@@ -191,7 +190,7 @@
     quarters, items = refs[:4], refs[4:11]
     ordered_ref, payload_ref = refs[11:]
     x, _ = place()
-    number = landing(sources_ref[lax.axis_index("asset")])
+    number = landing(lookup(sources_ref, lax.axis_index("asset"), False))
     for k, item in enumerate(items):
         @pl.when(number == k)
         def _(item=item):
@@ -213,7 +212,7 @@
 def row_call(sources, quarters, items):
     return pl.pallas_call(
         row_kernel,
-        in_specs=[IN_SMEM] + [IN_VMEM] * 11,
+        in_specs=[IN_VMEM] * 12,
         out_specs=[IN_VMEM] * 2,
         out_shape=[
             jax.ShapeDtypeStruct((4, 33, 8, DIM), jnp.float32),
@@ -266,75 +265,77 @@
     )(*payloads, ordered, after)
 
 
-STRIP = 512
-
-
-def outer_kernel(lengths_ref, mixed_ref, *refs):
-    quarters, whiten_ref, features_hbm, mark_ref, out_ref, state_ref, out_sems = refs[:4], *refs[4:]
-    mark_ref[...] = jnp.zeros((8, DIM), jnp.float32)
+def norm_kernel(lengths_ref, mixed_ref, *refs):
+    quarters, normed_ref, state_ref = refs[:4], *refs[4:]
     x, _ = place()
     for k, quarter in enumerate(quarters):
         for block in range(4):
             state_ref[4 * block + (x ^ k)] = quarter[block * HEADS:(block + 1) * HEADS]
     valid = lengths_ref[0] - lax.axis_index("seq") * STEPS
-    states = []
-    for head in range(HEADS):
-        state = state_ref[:, head].reshape(DIM, DIM)
-        states.append(split(state - jnp.mean(state, axis=1, keepdims=True)))
     same = (lax.broadcasted_iota(jnp.int32, (PAIR, PAIR), 0) // DIM
             == lax.broadcasted_iota(jnp.int32, (PAIR, PAIR), 1) // DIM)
     averaging = jnp.where(same, 1.0 / DIM, 0.0).astype(jnp.bfloat16)
-    out_copies = []
-    for strip in range(STEPS // STRIP):
-        rows = lanes_of(strip, STRIP)
-        alive = strip * STRIP + lax.broadcasted_iota(jnp.int32, (STRIP, PAIR), 0) < valid
-        parts = []
-        for pair in range(4):
-            halves = []
-            for head in (2 * pair, 2 * pair + 1):
-                own = lanes_of(head, DIM)
-                q = mixed_ref[0, rows, own]
-                cross = jnp.dot(jnp.concatenate([q, q], 1), states[head], preferred_element_type=jnp.float32)
-                halves.append(mixed_ref[1, rows, own].astype(jnp.float32) + cross)
-            centered = jnp.concatenate(halves, 1)
-            squares = (centered * centered).astype(jnp.bfloat16)
-            spread = jnp.dot(squares, averaging, preferred_element_type=jnp.float32)
-            scale = jnp.where(alive, lax.rsqrt(spread + EPSILON), 0.0)
-            parts.append((centered * scale).astype(jnp.bfloat16))
-        out_ref[rows, :] = jnp.dot(
-            jnp.concatenate(parts, 1), whiten_ref[...], preferred_element_type=jnp.float32).astype(jnp.bfloat16)
-        out_copies.append(pltpu.make_async_copy(
-            out_ref.at[rows, :], features_hbm.at[rows, :], out_sems.at[strip]))
-        out_copies[strip].start()
-    for copy in out_copies:
+    alive = lax.broadcasted_iota(jnp.int32, (STEPS, PAIR), 0) < valid
+    for pair in range(4):
+        halves = []
+        for head in (2 * pair, 2 * pair + 1):
+            own = lanes_of(head, DIM)
+            state = state_ref[:, head].reshape(DIM, DIM)
+            state = split(state - jnp.mean(state, axis=1, keepdims=True))
+            q = mixed_ref[0, :, own]
+            cross = jnp.dot(jnp.concatenate([q, q], 1), state, preferred_element_type=jnp.float32)
+            halves.append(mixed_ref[1, :, own].astype(jnp.float32) + cross)
+        centered = jnp.concatenate(halves, 1)
+        squares = (centered * centered).astype(jnp.bfloat16)
+        spread = jnp.dot(squares, averaging, preferred_element_type=jnp.float32)
+        scale = jnp.where(alive, lax.rsqrt(spread + EPSILON), 0.0)
+        normed_ref[:, lanes_of(pair)] = (centered * scale).astype(jnp.bfloat16)
+
+
+def norm_call(lengths, mixed, quarters):
+    return pl.pallas_call(
+        norm_kernel,
+        in_specs=[IN_SMEM] + [IN_VMEM] * 5,
+        out_specs=IN_VMEM,
+        out_shape=jax.ShapeDtypeStruct((STEPS, WIDTH), jnp.bfloat16),
+        scratch_shapes=[pltpu.VMEM((SHARDS, HEADS, 8, DIM), jnp.float32)],
+        compiler_params=params(12),
+        cost_estimate=work(2 * STEPS * WIDTH * WIDTH * 2, 4 * MIB),
+        name="cross_norm",
+    )(lengths, mixed, *quarters)
+
+
+def whiten_kernel(normed_ref, whiten_ref, after_ref, features_hbm, out_ref, out_sems):
+    copies = []
+    for part in range(2):
+        lanes = lanes_of(part, 512)
+        out_ref[:, lanes] = jnp.dot(
+            normed_ref[...], whiten_ref[:, lanes], preferred_element_type=jnp.float32).astype(jnp.bfloat16)
+        copies.append(pltpu.make_async_copy(out_ref.at[:, lanes], features_hbm.at[:, lanes], out_sems.at[part]))
+        copies[part].start()
+    for copy in copies:
         copy.wait()
 
 
-def outer_call(lengths, mixed, quarters, whiten):
-    return pl.pallas_call(
-        outer_kernel,
-        in_specs=[IN_SMEM] + [IN_VMEM] * 6,
-        out_specs=[IN_HBM, IN_VMEM],
-        out_shape=[
-            jax.ShapeDtypeStruct((STEPS, WIDTH), jnp.bfloat16),
-            jax.ShapeDtypeStruct((8, DIM), jnp.float32),
-        ],
-        scratch_shapes=[
-            pltpu.VMEM((STEPS, WIDTH), jnp.bfloat16),
-            pltpu.VMEM((SHARDS, HEADS, 8, DIM), jnp.float32),
-            DMA((STEPS // STRIP,)),
-        ],
-        compiler_params=params(16),
-        cost_estimate=work(2 * STEPS * WIDTH * WIDTH * 3 // 2, 4 * MIB),
-        name="outer_whiten",
-    )(lengths, mixed, *quarters, whiten)
-
-
-def origin(targets_ref, slot):
-    asset = jnp.int32(0)
-    for k in range(1, SHARDS):
-        asset = jnp.where(targets_ref[k] == slot, k, asset)
-    return asset
+def whiten_call(normed, whiten, after):
+    return pl.pallas_call(
+        whiten_kernel,
+        in_specs=[IN_VMEM] * 2 + [pl.BlockSpec(memory_space=pl.ANY)],
+        out_specs=IN_HBM,
+        out_shape=jax.ShapeDtypeStruct((STEPS, WIDTH), jnp.bfloat16),
+        scratch_shapes=[pltpu.VMEM((STEPS, WIDTH), jnp.bfloat16), DMA((2,))],
+        compiler_params=params(12),
+        cost_estimate=work(2 * STEPS * WIDTH * WIDTH * 2, 4 * MIB),
+        name="whiten_rows",
+    )(normed, whiten, after)
+
+
+def lookup(route_ref, slot, inverted):
+    route = route_ref[...].astype(jnp.float32)
+    lane = lax.broadcasted_iota(jnp.int32, route.shape, 1).astype(jnp.float32)
+    slot = slot.astype(jnp.float32)
+    found = jnp.where(route == slot, lane, 0.0) if inverted else jnp.where(lane == slot, route, 0.0)
+    return jnp.sum(found).astype(jnp.int32)
 
 
 def landing(source):
@@ -348,7 +349,7 @@
     me = lax.axis_index("asset")
     for j, out in enumerate(outs, 1):
         slot = me ^ j
-        source = origin(route_ref, slot) if inverted else route_ref[slot]
+        source = lookup(route_ref, slot, inverted)
         number = ((me ^ source) >> 2) & 3
         for k, item in enumerate(items):
             @pl.when(number == k)
@@ -359,7 +360,7 @@
 def near_call(inverted, route, items, after=()):
     return pl.pallas_call(
         functools.partial(near_kernel, inverted),
-        in_specs=[IN_SMEM] + [IN_VMEM] * 4 + [pl.BlockSpec(memory_space=pl.ANY)] * len(after),
+        in_specs=[IN_VMEM] * 5 + [pl.BlockSpec(memory_space=pl.ANY)] * len(after),
         out_specs=[IN_VMEM] * 3,
         out_shape=[jax.ShapeDtypeStruct((HEADS, 8, DIM), jnp.float32)] * 3,
         compiler_params=params(8),
@@ -370,7 +371,7 @@
 
 def kept_kernel(targets_ref, *refs):
     items, kept_hbm, sem = refs[:7], refs[7], refs[8]
-    number = landing(origin(targets_ref, lax.axis_index("asset")))
+    number = landing(lookup(targets_ref, lax.axis_index("asset"), True))
     for k, item in enumerate(items):
         @pl.when(number == k)
         def _(item=item):
@@ -382,7 +383,7 @@
 def kept_call(targets, items):
     return pl.pallas_call(
         kept_kernel,
-        in_specs=[IN_SMEM] + [pl.BlockSpec(memory_space=pl.ANY)] * 7,
+        in_specs=[IN_VMEM] + [pl.BlockSpec(memory_space=pl.ANY)] * 7,
         out_specs=pl.BlockSpec(memory_space=pl.ANY),
         out_shape=jax.ShapeDtypeStruct((1, HEADS, 8, DIM), jnp.float32),
         scratch_shapes=[DMA],
@@ -398,22 +399,28 @@
 
 def on_device(tokens, w_query, w_key, w_value, decay_log, lengths, sources, targets, stash, whiten):
     tokens, decay, whiten = tokens[0], decay_log[0], whiten[0]
-    own = fetch_call(stash)
+    sources, targets = sources[None], targets[None]
+    stash, mark = lax.optimization_barrier((stash, mark_call()))
+    own = stash[0]
     items = [own] + [swap(own, 4 * k) for k in (1, 2, 3)]
     *quarters, keys, values, sums = keys_call(lengths, tokens, w_key, w_value, decay)
-    near = near_call(False, sources, items)
+    near = near_call(False, sources, items, (mark,))
     near, quarters = lax.optimization_barrier((near, quarters))
-    arrived = [quarters[0]] + [swap(quarters[k], k, "seq") for k in (1, 2, 3)]
+    moved = {k: swap(quarters[k], k, "seq") for k in (2, 1, 3)}
+    arrived = [quarters[0]] + [moved[k] for k in (1, 2, 3)]
     items += [swap(item, k) for k, item in enumerate(near, 1)]
     ordered, payload = row_call(sources, arrived, items)
-    payloads = [payload] + [swap(payload, 4 * m, "seq") for m in (1, 2, 3)]
+    moved = {m: swap(payload, 4 * m, "seq") for m in (1, 3, 2)}
+    payloads = [payload] + [moved[m] for m in (1, 2, 3)]
     mixed = inner_call(tokens, w_query, keys, values, sums, payload)
     *carried, closing = carry_call(payloads, ordered, mixed)
-    state = [carried[0]] + [swap(carried[k], k, "seq") for k in (1, 2, 3)]
+    moved = {k: swap(carried[k], k, "seq") for k in (2, 1, 3)}
+    state = [carried[0]] + [moved[k] for k in (1, 2, 3)]
     items = [closing] + [swap(closing, 4 * k) for k in (1, 2, 3)]
-    features, mark = outer_call(lengths, mixed, state, whiten)
-    near = near_call(True, targets, items, (mark,))
+    normed = norm_call(lengths, mixed, state)
+    near = near_call(True, targets, items, (normed,))
     items += [swap(item, k) for k, item in enumerate(near, 1)]
+    features = whiten_call(normed, whiten, near[0])
     return (features[None], kept_call(targets, items))
 
 

time: 63.1 us -> 61.6 us (0.976)
  waiting for transfers between devices: 9.02 us -> 7.17 us
  starting transfers between devices: 36.1 us -> 37.9 us
  Pallas kernels: 15.4 us -> 14.1 us
    ppermute x21, waiting for transfers between devices: 9.02 us -> 7.17 us  [swap(): return lax.ppermute(value, axis, [(k, k ^ bits) for k in range(SHARDS)])]
    ppermute x21, starting transfers between devices: 36.1 us -> 37.9 us  [swap(): return lax.ppermute(value, axis, [(k, k ^ bits) for k in range(SHARDS)])]
    pallas_call x6 -> x7, Pallas kernels: 6.59 us -> 5.29 us  [the longest x1 2.06 us: whiten_call(): pl.pallas_call(whiten_kernel, in_specs=[IN_VMEM] * 2 + [pl.BlockSpec(memo...]
where the time goes in v4:
time: 61.6 us; the launch traced here: 61.5 us
  starting transfers between devices  37.9 us (62%)
  Pallas kernels  14.1 us (23%)
  waiting for transfers between devices  7.17 us (12%)
  between operations  1.63 us (3%)
  local copies, waits for them, and re-layouts  0.74 us (1%)
    ppermute x21, starting transfers between devices, swap(): return lax.ppermute(value, axis, [(k, k ^ bits) for k in range(SHARDS)])  37.9 us
    ppermute x21, waiting for transfers between devices, swap(): return lax.ppermute(value, axis, [(k, k ^ bits) for k in range(SHARDS)])  7.17 us
    pallas_call x1, Pallas kernels, inner_call(): pl.pallas_call(inner_kernel, in_specs=[IN_VMEM] * 5 + [pl.BlockSpec(memor...  5.19 us
    pallas_call x1, Pallas kernels, keys_call(): pl.pallas_call(keys_kernel, in_specs=[IN_SMEM] + [IN_VMEM] * 4, out_specs...  3.33 us
    pallas_call x1, Pallas kernels, whiten_call(): pl.pallas_call(whiten_kernel, in_specs=[IN_VMEM] * 2 + [pl.BlockSpec(memo...  2.06 us
    pallas_call x1, Pallas kernels, norm_call(): pl.pallas_call(norm_kernel, in_specs=[IN_SMEM] + [IN_VMEM] * 5, out_specs...  1.37 us
  transfers between devices with their start and end apart: 21, of which 8 were waited for; matrix products, arithmetic and copies ran while one was open for 0% of the time, Pallas kernels for 19%

profile of v4, /device:TPU:1, one launch (start us, length us, event | category | flops | bytes accessed | tf_op | source)
XLA Modules:
  0.0 61.5 jit_solution(5228783851520576942)
XLA Ops:
  1.4 6.8 %collective-permute-start.2 = (f32[8,8,128]{2,1,0:T(8,128)S(1)}, f32[8,8,128]{2,1,0:T(8,128)S(1)}, u32[]{:S(2)}, u32[]{:S(2)}) collective-permute-start(f32[8,8,128]{2,1,0:T(8,128)S(1)} %bitcast.7), channel_id=1, source_target_pairs={{0,12},{1,13},{2,14},{3,15},{4,8},{5,9},{6,10},{7,11},{8,4},{9,5},... | collective-permute-start | bytes 98312 | tf_op jit(solution)/shard_map/ppermute | solution.py:397
  8.2 0.9 %collective-permute-start.1 = (f32[8,8,128]{2,1,0:T(8,128)S(1)}, f32[8,8,128]{2,1,0:T(8,128)S(1)}, u32[]{:S(2)}, u32[]{:S(2)}) collective-permute-start(f32[8,8,128]{2,1,0:T(8,128)S(1)} %bitcast.8), channel_id=1, source_target_pairs={{0,8},{1,9},{2,10},{3,11},{4,12},{5,13},{6,14},{7,15},{8,0},{9,1},... | collective-permute-start | bytes 98312 | tf_op jit(solution)/shard_map/ppermute | solution.py:397
  9.1 1.2 %collective-permute-start = (f32[8,8,128]{2,1,0:T(8,128)S(1)}, f32[8,8,128]{2,1,0:T(8,128)S(1)}, u32[]{:S(2)}, u32[]{:S(2)}) collective-permute-start(f32[8,8,128]{2,1,0:T(8,128)S(1)} %bitcast.9), channel_id=1, source_target_pairs={{0,4},{1,5},{2,6},{3,7},{4,0},{5,1},{6,2},{7,3},{8,12},{9,13},{10,... | collective-permute-start | bytes 98312 | tf_op jit(solution)/shard_map/ppermute | solution.py:397
  11.0 3.3 %keys_values.1 = (f32[33,8,128]{2,1,0:T(8,128)S(1)}, f32[33,8,128]{2,1,0:T(8,128)S(1)}, f32[33,8,128]{2,1,0:T(8,128)S(1)}, f32[33,8,128]{2,1,0:T(8,128)S(1)}, bf...) custom-call(s32[1]{0:T(128)S(6)} %copy.12.lengths_ref, ...), custom_call_target="tpu_custom_call" | custom-call | flops 3221225472 | bytes 16777216 | tf_op jit(solution)/shard_map/keys_values/pallas_call | solution.py:112
  15.5 1.3 %collective-permute-start.3 = (f32[33,8,128]{2,1,0:T(8,128)S(1)}, f32[33,8,128]{2,1,0:T(8,128)S(1)}, u32[]{:S(2)}, u32[]{:S(2)}) collective-permute-start(f32[33,8,128]{2,1,0:T(8,128)S(1)} %get-tuple-element.44), channel_id=1, source_target_pairs={{0,16},{16,0},{32,48},{48,32},{64,80},{80,64},{96,112},{112,96},{1... | collective-permute-start | bytes 405512 | tf_op jit(solution)/shard_map/ppermute | solution.py:397
  16.8 2.5 %collective-permute-start.4 = (f32[33,8,128]{2,1,0:T(8,128)S(1)}, f32[33,8,128]{2,1,0:T(8,128)S(1)}, u32[]{:S(2)}, u32[]{:S(2)}) collective-permute-start(f32[33,8,128]{2,1,0:T(8,128)S(1)} %get-tuple-element.45), channel_id=1, source_target_pairs={{0,32},{16,48},{32,0},{48,16},{64,96},{80,112},{96,64},{112,80},{1... | collective-permute-start | bytes 405512 | tf_op jit(solution)/shard_map/ppermute | solution.py:397
  19.5 3.1 %collective-permute-start.6 = (f32[8,8,128]{2,1,0:T(8,128)S(1)}, f32[8,8,128]{2,1,0:T(8,128)S(1)}, u32[]{:S(2)}, u32[]{:S(2)}) collective-permute-start(f32[8,8,128]{2,1,0:T(8,128)S(1)} %get-tuple-element.47), channel_id=1, source_target_pairs={{0,1},{1,0},{2,3},{3,2},{4,5},{5,4},{6,7},{7,6},{8,9},{9,8},{10,11... | collective-permute-start | bytes 98312 | tf_op jit(solution)/shard_map/ppermute | solution.py:397
  22.6 0.8 %collective-permute-start.7 = (f32[8,8,128]{2,1,0:T(8,128)S(1)}, f32[8,8,128]{2,1,0:T(8,128)S(1)}, u32[]{:S(2)}, u32[]{:S(2)}) collective-permute-start(f32[8,8,128]{2,1,0:T(8,128)S(1)} %get-tuple-element.48), channel_id=1, source_target_pairs={{0,2},{1,3},{2,0},{3,1},{4,6},{5,7},{6,4},{7,5},{8,10},{9,11},{10,... | collective-permute-start | bytes 98312 | tf_op jit(solution)/shard_map/ppermute | solution.py:397
  23.5 1.1 %collective-permute-start.8 = (f32[8,8,128]{2,1,0:T(8,128)S(1)}, f32[8,8,128]{2,1,0:T(8,128)S(1)}, u32[]{:S(2)}, u32[]{:S(2)}) collective-permute-start(f32[8,8,128]{2,1,0:T(8,128)S(1)} %get-tuple-element.49), channel_id=1, source_target_pairs={{0,3},{1,2},{2,1},{3,0},{4,7},{5,6},{6,5},{7,4},{8,11},{9,10},{10,... | collective-permute-start | bytes 98312 | tf_op jit(solution)/shard_map/ppermute | solution.py:397
  24.5 1.1 %collective-permute-done.7.refs_9_ = f32[8,8,128]{2,1,0:T(8,128)S(1)} collective-permute-done((f32[8,8,128]{2,1,0:T(8,128)S(1)}, f32[8,8,128]{2,1,0:T(8,128)S(1)}, u32[]{:S(2)}, u32[]{:S(2)}) %collective-permute-start.7) | collective-permute-done | bytes 32800 | tf_op jit(solution)/shard_map/ppermute | solution.py:397
  25.7 1.4 %collective-permute-done.8.refs_10_ = f32[8,8,128]{2,1,0:T(8,128)S(1)} collective-permute-done((f32[8,8,128]{2,1,0:T(8,128)S(1)}, f32[8,8,128]{2,1,0:T(8,128)S(1)}, u32[]{:S(2)}, u32[]{:S(2)}) %collective-permute-start.8) | collective-permute-done | bytes 32800 | tf_op jit(solution)/shard_map/ppermute | solution.py:397
  27.4 2.8 %collective-permute-start.11 = (f32[41,8,128]{2,1,0:T(8,128)S(1)}, f32[41,8,128]{2,1,0:T(8,128)S(1)}, u32[]{:S(2)}, u32[]{:S(2)}) collective-permute-start(f32[41,8,128]{2,1,0:T(8,128)S(1)} %get-tuple-element.50.after_ref.refs_0_), channel_id=1, source_target_pairs={{0,192},{16,208},{32,224},{48,240},{64,128},{80,144},{96,160},{112... | collective-permute-start | bytes 503816 | tf_op jit(solution)/shard_map/ppermute | solution.py:397
  30.9 5.2 %queries_inner.1.refs_5_.mixed_ref = bf16[2,512,1024]{2,1,0:T(8,128)(2,1)S(1)} custom-call(bf16[512,1024]{1,0:T(8,128)(2,1)S(1)} %bitcast.18, bf16[1024,1024]{1,0:T(8,128)(2,1)S(1)} %copy-done.5, bf16[1024,512]{1,0:T(8,128)(2,1)S(1)} %get-tuple-element.31.keys_ref, bf16[512,1024]{1,0:T(8,128)(2,1)S(1)} %get-tuple-element.32.values_ref, ...), custom_call_target="tpu_custom_call" | custom-call | flops 3221225472 | bytes 5242880 | tf_op jit(solution)/shard_map/queries_inner/pallas_call | solution.py:145
  36.1 1.1 %collective-permute-done.11.refs_3_ = f32[41,8,128]{2,1,0:T(8,128)S(1)} collective-permute-done((f32[41,8,128]{2,1,0:T(8,128)S(1)}, f32[41,8,128]{2,1,0:T(8,128)S(1)}, u32[]{:S(2)}, u32[]{:S(2)}) %collective-permute-start.11) | collective-permute-done | bytes 167968 | tf_op jit(solution)/shard_map/ppermute | solution.py:397
  38.1 4.0 %collective-permute-start.13 = (f32[32,8,128]{2,1,0:T(8,128)S(1)}, f32[32,8,128]{2,1,0:T(8,128)S(1)}, u32[]{:S(2)}, u32[]{:S(2)}) collective-permute-start(f32[32,8,128]{2,1,0:T(8,128)S(1)} %get-tuple-element.54), channel_id=1, source_target_pairs={{0,32},{16,48},{32,0},{48,16},{64,96},{80,112},{96,64},{112,80},{1... | collective-permute-start | bytes 393224 | tf_op jit(solution)/shard_map/ppermute | solution.py:397
  42.1 2.3 %collective-permute-start.17 = (f32[8,8,128]{2,1,0:T(8,128)S(1)}, f32[8,8,128]{2,1,0:T(8,128)S(1)}, u32[]{:S(2)}, u32[]{:S(2)}) collective-permute-start(f32[8,8,128]{2,1,0:T(8,128)S(1)} %get-tuple-element.56.refs_0_), channel_id=1, source_target_pairs={{0,12},{1,13},{2,14},{3,15},{4,8},{5,9},{6,10},{7,11},{8,4},{9,5},... | collective-permute-start | bytes 98312 | tf_op jit(solution)/shard_map/ppermute | solution.py:397
  44.5 2.1 %collective-permute-start.16 = (f32[8,8,128]{2,1,0:T(8,128)S(1)}, f32[8,8,128]{2,1,0:T(8,128)S(1)}, u32[]{:S(2)}, u32[]{:S(2)}) collective-permute-start(f32[8,8,128]{2,1,0:T(8,128)S(1)} %get-tuple-element.56.refs_0_), channel_id=1, source_target_pairs={{0,8},{1,9},{2,10},{3,11},{4,12},{5,13},{6,14},{7,15},{8,0},{9,1},... | collective-permute-start | bytes 98312 | tf_op jit(solution)/shard_map/ppermute | solution.py:397
  46.6 1.2 %collective-permute-start.15 = (f32[8,8,128]{2,1,0:T(8,128)S(1)}, f32[8,8,128]{2,1,0:T(8,128)S(1)}, u32[]{:S(2)}, u32[]{:S(2)}) collective-permute-start(f32[8,8,128]{2,1,0:T(8,128)S(1)} %get-tuple-element.56.refs_0_), channel_id=1, source_target_pairs={{0,4},{1,5},{2,6},{3,7},{4,0},{5,1},{6,2},{7,3},{8,12},{9,13},{10,... | collective-permute-start | bytes 98312 | tf_op jit(solution)/shard_map/ppermute | solution.py:397
  47.8 1.9 %collective-permute-done.14.refs_3_ = f32[32,8,128]{2,1,0:T(8,128)S(1)} collective-permute-done((f32[32,8,128]{2,1,0:T(8,128)S(1)}, f32[32,8,128]{2,1,0:T(8,128)S(1)}, u32[]{:S(2)}, u32[]{:S(2)}) %collective-permute-start.14) | collective-permute-done | bytes 131104 | tf_op jit(solution)/shard_map/ppermute | solution.py:397
  49.7 1.4 %cross_norm.1.refs_4_.normed_ref = bf16[512,1024]{1,0:T(8,128)(2,1)S(1)} custom-call(s32[1]{0:T(128)S(6)} %copy.12.lengths_ref, bf16[2,512,1024]{2,1,0:T(8,128)(2,1)S(1)} %queries_inner.1.refs_5_.mixed_ref, f32[32,8,128]{2,1,0:T(8,128)S(1)} %get-tuple-element.52.refs_0_, f32[32,8,128]{2,1,0:T(8,128)S(1)} %collective-permute-done.12.refs_1_, ...), custom_call_target="tpu_custom_call" | custom-call | flops 2147483648 | bytes 4194304 | tf_op jit(solution)/shard_map/cross_norm/pallas_call | solution.py:296
  51.6 1.1 %collective-permute-start.19 = (f32[8,8,128]{2,1,0:T(8,128)S(1)}, f32[8,8,128]{2,1,0:T(8,128)S(1)}, u32[]{:S(2)}, u32[]{:S(2)}) collective-permute-start(f32[8,8,128]{2,1,0:T(8,128)S(1)} %get-tuple-element.58), channel_id=1, source_target_pairs={{0,2},{1,3},{2,0},{3,1},{4,6},{5,7},{6,4},{7,5},{8,10},{9,11},{10,... | collective-permute-start | bytes 98312 | tf_op jit(solution)/shard_map/ppermute | solution.py:397
  52.7 5.4 %collective-permute-start.20 = (f32[8,8,128]{2,1,0:T(8,128)S(1)}, f32[8,8,128]{2,1,0:T(8,128)S(1)}, u32[]{:S(2)}, u32[]{:S(2)}) collective-permute-start(f32[8,8,128]{2,1,0:T(8,128)S(1)} %get-tuple-element.59), channel_id=1, source_target_pairs={{0,3},{1,2},{2,1},{3,0},{4,7},{5,6},{6,5},{7,4},{8,11},{9,10},{10,... | collective-permute-start | bytes 98312 | tf_op jit(solution)/shard_map/ppermute | solution.py:397
  58.1 2.1 %whiten_rows.1 = bf16[512,1024]{1,0:T(8,128)(2,1)} custom-call(bf16[512,1024]{1,0:T(8,128)(2,1)S(1)} %cross_norm.1.refs_4_.normed_ref, bf16[1024,1024]{1,0:T(8,128)(2,1)S(1)} %bitcast.16, f32[8,8,128]{2,1,0:T(8,128)S(1)} %get-tuple-element.57.after_ref), custom_call_target="tpu_custom_call" | custom-call | flops 2147483648 | bytes 4194304 | tf_op jit(solution)/shard_map/whiten_rows/pallas_call | solution.py:321
  60.6 0.8 %kept_rows.1 = f32[1,8,8,128]{3,2,1,0:T(8,128)} custom-call(s32[1,16]{1,0:T(1,128)S(1)} %bitcast.13, f32[8,8,128]{2,1,0:T(8,128)S(1)} %get-tuple-element.56.refs_0_, f32[8,8,128]{2,1,0:T(8,128)S(1)} %collective-permute-done.15.refs_1_, f32[8,8,128]{2,1,0:T(8,128)S(1)} %collective-permute-done.16.refs_2_, f32[8,8,128]{2,1,0:T(8,128)S(1)} %collective-permute-done.17.refs_3_, ...), custom_call_target="tpu_custom_call" | custom-call | flops 1024 | bytes 131072 | tf_op jit(solution)/shard_map/kept_rows/pallas_call | solution.py:384
  (46 shorter events, 4.9 us)
Async XLA Ops:
  0.6 10.3 %copy-start.3 = (bf16[1024,1024]{1,0:T(8,128)(2,1)S(1)}, bf16[1024,1024]{1,0:T(8,128)(2,1)}, u32[]{:S(2)}) copy-start(bf16[1024,1024]{1,0:T(8,128)(2,1)} %w_key_ref.1) | copy-start | bytes 6291460
  0.7 10.3 %copy-start.4 = (bf16[1024,1024]{1,0:T(8,128)(2,1)S(1)}, bf16[1024,1024]{1,0:T(8,128)(2,1)}, u32[]{:S(2)}) copy-start(bf16[1024,1024]{1,0:T(8,128)(2,1)} %w_value_ref.1) | copy-start | bytes 6291460
  1.4 13.0 %collective-permute-start.2 = (f32[8,8,128]{2,1,0:T(8,128)S(1)}, f32[8,8,128]{2,1,0:T(8,128)S(1)}, u32[]{:S(2)}, u32[]{:S(2)}) collective-permute-start(f32[8,8,128]{2,1,0:T(8,128)S(1)} %bitcast.7), channel_id=1, source_target_pairs={{0,12},{1,13},{2,14},{3,15},{4,8},{5,9},{6,10},{7,11},{8,4},{9,5},... | collective-permute-start | bytes 98312 | tf_op jit(solution)/shard_map/ppermute | solution.py:397
  8.2 6.8 %collective-permute-start.1 = (f32[8,8,128]{2,1,0:T(8,128)S(1)}, f32[8,8,128]{2,1,0:T(8,128)S(1)}, u32[]{:S(2)}, u32[]{:S(2)}) collective-permute-start(f32[8,8,128]{2,1,0:T(8,128)S(1)} %bitcast.8), channel_id=1, source_target_pairs={{0,8},{1,9},{2,10},{3,11},{4,12},{5,13},{6,14},{7,15},{8,0},{9,1},... | collective-permute-start | bytes 98312 | tf_op jit(solution)/shard_map/ppermute | solution.py:397
  9.1 6.0 %collective-permute-start = (f32[8,8,128]{2,1,0:T(8,128)S(1)}, f32[8,8,128]{2,1,0:T(8,128)S(1)}, u32[]{:S(2)}, u32[]{:S(2)}) collective-permute-start(f32[8,8,128]{2,1,0:T(8,128)S(1)} %bitcast.9), channel_id=1, source_target_pairs={{0,4},{1,5},{2,6},{3,7},{4,0},{5,1},{6,2},{7,3},{8,12},{9,13},{10,... | collective-permute-start | bytes 98312 | tf_op jit(solution)/shard_map/ppermute | solution.py:397
  11.0 19.8 %copy-start.5 = (bf16[1024,1024]{1,0:T(8,128)(2,1)S(1)}, bf16[1024,1024]{1,0:T(8,128)(2,1)}, u32[]{:S(2)}) copy-start(bf16[1024,1024]{1,0:T(8,128)(2,1)} %w_query_ref.1) | copy-start | bytes 6291460
  15.5 11.6 %collective-permute-start.3 = (f32[33,8,128]{2,1,0:T(8,128)S(1)}, f32[33,8,128]{2,1,0:T(8,128)S(1)}, u32[]{:S(2)}, u32[]{:S(2)}) collective-permute-start(f32[33,8,128]{2,1,0:T(8,128)S(1)} %get-tuple-element.44), channel_id=1, source_target_pairs={{0,16},{16,0},{32,48},{48,32},{64,80},{80,64},{96,112},{112,96},{1... | collective-permute-start | bytes 405512 | tf_op jit(solution)/shard_map/ppermute | solution.py:397
  16.8 10.3 %collective-permute-start.4 = (f32[33,8,128]{2,1,0:T(8,128)S(1)}, f32[33,8,128]{2,1,0:T(8,128)S(1)}, u32[]{:S(2)}, u32[]{:S(2)}) collective-permute-start(f32[33,8,128]{2,1,0:T(8,128)S(1)} %get-tuple-element.45), channel_id=1, source_target_pairs={{0,32},{16,48},{32,0},{48,16},{64,96},{80,112},{96,64},{112,80},{1... | collective-permute-start | bytes 405512 | tf_op jit(solution)/shard_map/ppermute | solution.py:397
  19.3 7.8 %collective-permute-start.5 = (f32[33,8,128]{2,1,0:T(8,128)S(1)}, f32[33,8,128]{2,1,0:T(8,128)S(1)}, u32[]{:S(2)}, u32[]{:S(2)}) collective-permute-start(f32[33,8,128]{2,1,0:T(8,128)S(1)} %get-tuple-element.46), channel_id=1, source_target_pairs={{0,48},{16,32},{32,16},{48,0},{64,112},{80,96},{96,80},{112,64},{1... | collective-permute-start | bytes 405512 | tf_op jit(solution)/shard_map/ppermute | solution.py:397
  19.5 4.0 %collective-permute-start.6 = (f32[8,8,128]{2,1,0:T(8,128)S(1)}, f32[8,8,128]{2,1,0:T(8,128)S(1)}, u32[]{:S(2)}, u32[]{:S(2)}) collective-permute-start(f32[8,8,128]{2,1,0:T(8,128)S(1)} %get-tuple-element.47), channel_id=1, source_target_pairs={{0,1},{1,0},{2,3},{3,2},{4,5},{5,4},{6,7},{7,6},{8,9},{9,8},{10,11... | collective-permute-start | bytes 98312 | tf_op jit(solution)/shard_map/ppermute | solution.py:397
  22.6 3.1 %collective-permute-start.7 = (f32[8,8,128]{2,1,0:T(8,128)S(1)}, f32[8,8,128]{2,1,0:T(8,128)S(1)}, u32[]{:S(2)}, u32[]{:S(2)}) collective-permute-start(f32[8,8,128]{2,1,0:T(8,128)S(1)} %get-tuple-element.48), channel_id=1, source_target_pairs={{0,2},{1,3},{2,0},{3,1},{4,6},{5,7},{6,4},{7,5},{8,10},{9,11},{10,... | collective-permute-start | bytes 98312 | tf_op jit(solution)/shard_map/ppermute | solution.py:397
  23.5 3.6 %collective-permute-start.8 = (f32[8,8,128]{2,1,0:T(8,128)S(1)}, f32[8,8,128]{2,1,0:T(8,128)S(1)}, u32[]{:S(2)}, u32[]{:S(2)}) collective-permute-start(f32[8,8,128]{2,1,0:T(8,128)S(1)} %get-tuple-element.49), channel_id=1, source_target_pairs={{0,3},{1,2},{2,1},{3,0},{4,7},{5,6},{6,5},{7,4},{8,11},{9,10},{10,... | collective-permute-start | bytes 98312 | tf_op jit(solution)/shard_map/ppermute | solution.py:397
  27.4 9.8 %collective-permute-start.11 = (f32[41,8,128]{2,1,0:T(8,128)S(1)}, f32[41,8,128]{2,1,0:T(8,128)S(1)}, u32[]{:S(2)}, u32[]{:S(2)}) collective-permute-start(f32[41,8,128]{2,1,0:T(8,128)S(1)} %get-tuple-element.50.after_ref.refs_0_), channel_id=1, source_target_pairs={{0,192},{16,208},{32,224},{48,240},{64,128},{80,144},{96,160},{112... | collective-permute-start | bytes 503816 | tf_op jit(solution)/shard_map/ppermute | solution.py:397
  30.2 7.0 %collective-permute-start.10 = (f32[41,8,128]{2,1,0:T(8,128)S(1)}, f32[41,8,128]{2,1,0:T(8,128)S(1)}, u32[]{:S(2)}, u32[]{:S(2)}) collective-permute-start(f32[41,8,128]{2,1,0:T(8,128)S(1)} %get-tuple-element.50.after_ref.refs_0_), channel_id=1, source_target_pairs={{0,128},{16,144},{32,160},{48,176},{64,192},{80,208},{96,224},{112... | collective-permute-start | bytes 503816 | tf_op jit(solution)/shard_map/ppermute | solution.py:397
  30.5 7.0 %collective-permute-start.9 = (f32[41,8,128]{2,1,0:T(8,128)S(1)}, f32[41,8,128]{2,1,0:T(8,128)S(1)}, u32[]{:S(2)}, u32[]{:S(2)}) collective-permute-start(f32[41,8,128]{2,1,0:T(8,128)S(1)} %get-tuple-element.50.after_ref.refs_0_), channel_id=1, source_target_pairs={{0,64},{16,80},{32,96},{48,112},{64,0},{80,16},{96,32},{112,48},{1... | collective-permute-start | bytes 503816 | tf_op jit(solution)/shard_map/ppermute | solution.py:397
  37.8 8.8 %collective-permute-start.12 = (f32[32,8,128]{2,1,0:T(8,128)S(1)}, f32[32,8,128]{2,1,0:T(8,128)S(1)}, u32[]{:S(2)}, u32[]{:S(2)}) collective-permute-start(f32[32,8,128]{2,1,0:T(8,128)S(1)} %get-tuple-element.53), channel_id=1, source_target_pairs={{0,16},{16,0},{32,48},{48,32},{64,80},{80,64},{96,112},{112,96},{1... | collective-permute-start | bytes 393224 | tf_op jit(solution)/shard_map/ppermute | solution.py:397
  38.1 9.7 %collective-permute-start.13 = (f32[32,8,128]{2,1,0:T(8,128)S(1)}, f32[32,8,128]{2,1,0:T(8,128)S(1)}, u32[]{:S(2)}, u32[]{:S(2)}) collective-permute-start(f32[32,8,128]{2,1,0:T(8,128)S(1)} %get-tuple-element.54), channel_id=1, source_target_pairs={{0,32},{16,48},{32,0},{48,16},{64,96},{80,112},{96,64},{112,80},{1... | collective-permute-start | bytes 393224 | tf_op jit(solution)/shard_map/ppermute | solution.py:397
  42.1 7.5 %collective-permute-start.14 = (f32[32,8,128]{2,1,0:T(8,128)S(1)}, f32[32,8,128]{2,1,0:T(8,128)S(1)}, u32[]{:S(2)}, u32[]{:S(2)}) collective-permute-start(f32[32,8,128]{2,1,0:T(8,128)S(1)} %get-tuple-element.55), channel_id=1, source_target_pairs={{0,48},{16,32},{32,16},{48,0},{64,112},{80,96},{96,80},{112,64},{1... | collective-permute-start | bytes 393224 | tf_op jit(solution)/shard_map/ppermute | solution.py:397
  42.1 8.9 %collective-permute-start.17 = (f32[8,8,128]{2,1,0:T(8,128)S(1)}, f32[8,8,128]{2,1,0:T(8,128)S(1)}, u32[]{:S(2)}, u32[]{:S(2)}) collective-permute-start(f32[8,8,128]{2,1,0:T(8,128)S(1)} %get-tuple-element.56.refs_0_), channel_id=1, source_target_pairs={{0,12},{1,13},{2,14},{3,15},{4,8},{5,9},{6,10},{7,11},{8,4},{9,5},... | collective-permute-start | bytes 98312 | tf_op jit(solution)/shard_map/ppermute | solution.py:397
  44.5 6.7 %collective-permute-start.16 = (f32[8,8,128]{2,1,0:T(8,128)S(1)}, f32[8,8,128]{2,1,0:T(8,128)S(1)}, u32[]{:S(2)}, u32[]{:S(2)}) collective-permute-start(f32[8,8,128]{2,1,0:T(8,128)S(1)} %get-tuple-element.56.refs_0_), channel_id=1, source_target_pairs={{0,8},{1,9},{2,10},{3,11},{4,12},{5,13},{6,14},{7,15},{8,0},{9,1},... | collective-permute-start | bytes 98312 | tf_op jit(solution)/shard_map/ppermute | solution.py:397
  46.6 4.6 %collective-permute-start.15 = (f32[8,8,128]{2,1,0:T(8,128)S(1)}, f32[8,8,128]{2,1,0:T(8,128)S(1)}, u32[]{:S(2)}, u32[]{:S(2)}) collective-permute-start(f32[8,8,128]{2,1,0:T(8,128)S(1)} %get-tuple-element.56.refs_0_), channel_id=1, source_target_pairs={{0,4},{1,5},{2,6},{3,7},{4,0},{5,1},{6,2},{7,3},{8,12},{9,13},{10,... | collective-permute-start | bytes 98312 | tf_op jit(solution)/shard_map/ppermute | solution.py:397
  51.6 8.6 %collective-permute-start.19 = (f32[8,8,128]{2,1,0:T(8,128)S(1)}, f32[8,8,128]{2,1,0:T(8,128)S(1)}, u32[]{:S(2)}, u32[]{:S(2)}) collective-permute-start(f32[8,8,128]{2,1,0:T(8,128)S(1)} %get-tuple-element.58), channel_id=1, source_target_pairs={{0,2},{1,3},{2,0},{3,1},{4,6},{5,7},{6,4},{7,5},{8,10},{9,11},{10,... | collective-permute-start | bytes 98312 | tf_op jit(solution)/shard_map/ppermute | solution.py:397
  52.7 7.9 %collective-permute-start.20 = (f32[8,8,128]{2,1,0:T(8,128)S(1)}, f32[8,8,128]{2,1,0:T(8,128)S(1)}, u32[]{:S(2)}, u32[]{:S(2)}) collective-permute-start(f32[8,8,128]{2,1,0:T(8,128)S(1)} %get-tuple-element.59), channel_id=1, source_target_pairs={{0,3},{1,2},{2,1},{3,0},{4,7},{5,6},{6,5},{7,4},{8,11},{9,10},{10,... | collective-permute-start | bytes 98312 | tf_op jit(solution)/shard_map/ppermute | solution.py:397
  58.1 2.5 %collective-permute-start.18 = (f32[8,8,128]{2,1,0:T(8,128)S(1)}, f32[8,8,128]{2,1,0:T(8,128)S(1)}, u32[]{:S(2)}, u32[]{:S(2)}) collective-permute-start(f32[8,8,128]{2,1,0:T(8,128)S(1)} %get-tuple-element.57.after_ref), channel_id=1, source_target_pairs={{0,1},{1,0},{2,3},{3,2},{4,5},{5,4},{6,7},{7,6},{8,9},{9,8},{10,11... | collective-permute-start | bytes 98312 | tf_op jit(solution)/shard_map/ppermute | solution.py:397
  (6 other events, 35.4 us)

commit v5 on v4

--- a/solution.py
+++ b/solution.py
@@ -17,6 +17,9 @@
 LOG2E = 1.4426950408889634
 FAR = -1e30
 MIB = 1024 * 1024
+ROW_ORDER = (0, 2, 1, 3)
+LINE_ORDER = (0, 1, 3, 2)
+FAR_ORDER = (0, 1, 3, 2, 4, 5, 6)
 IN_HBM = pl.BlockSpec(memory_space=pltpu.HBM)
 IN_VMEM = pl.BlockSpec(memory_space=pltpu.VMEM)
 IN_SMEM = pl.BlockSpec(memory_space=pltpu.SMEM)
@@ -191,11 +194,11 @@
     ordered_ref, payload_ref = refs[11:]
     x, _ = place()
     number = landing(lookup(sources_ref, lax.axis_index("asset"), False))
-    for k, item in enumerate(items):
+    for k, item in zip(FAR_ORDER, items):
         @pl.when(number == k)
         def _(item=item):
             payload_ref[33:41] = item[...]
-    for k, quarter in enumerate(quarters):
+    for k, quarter in zip(ROW_ORDER, quarters):
         ordered_ref[x ^ k] = quarter[...]
     for row in range(32):
         head = row % HEADS
@@ -228,7 +231,7 @@
     payloads, ordered_ref, carried = refs[:4], refs[4], refs[6:10]
     closing_ref, rows_ref, carry_ref, final_ref = refs[10:]
     x, y = place()
-    for m, payload in enumerate(payloads):
+    for m, payload in zip(LINE_ORDER, payloads):
         rows_ref[y ^ m] = payload[...]
     for row in range(32):
         head, block = row % HEADS, row // HEADS
@@ -268,7 +271,7 @@
 def norm_kernel(lengths_ref, mixed_ref, *refs):
     quarters, normed_ref, state_ref = refs[:4], *refs[4:]
     x, _ = place()
-    for k, quarter in enumerate(quarters):
+    for k, quarter in zip(ROW_ORDER, quarters):
         for block in range(4):
             state_ref[4 * block + (x ^ k)] = quarter[block * HEADS:(block + 1) * HEADS]
     valid = lengths_ref[0] - lax.axis_index("seq") * STEPS
@@ -351,7 +354,7 @@
         slot = me ^ j
         source = lookup(route_ref, slot, inverted)
         number = ((me ^ source) >> 2) & 3
-        for k, item in enumerate(items):
+        for k, item in zip(FAR_ORDER, items):
             @pl.when(number == k)
             def _(item=item, out=out):
                 out[...] = item[...]
@@ -372,7 +375,7 @@
 def kept_kernel(targets_ref, *refs):
     items, kept_hbm, sem = refs[:7], refs[7], refs[8]
     number = landing(lookup(targets_ref, lax.axis_index("asset"), True))
-    for k, item in enumerate(items):
+    for k, item in zip(FAR_ORDER, items):
         @pl.when(number == k)
         def _(item=item):
             copy = pltpu.make_async_copy(item, kept_hbm.at[0], sem)
@@ -402,21 +405,18 @@
     sources, targets = sources[None], targets[None]
     stash, mark = lax.optimization_barrier((stash, mark_call()))
     own = stash[0]
-    items = [own] + [swap(own, 4 * k) for k in (1, 2, 3)]
+    items = [own] + [swap(own, 4 * k) for k in FAR_ORDER[1:4]]
     *quarters, keys, values, sums = keys_call(lengths, tokens, w_key, w_value, decay)
     near = near_call(False, sources, items, (mark,))
     near, quarters = lax.optimization_barrier((near, quarters))
-    moved = {k: swap(quarters[k], k, "seq") for k in (2, 1, 3)}
-    arrived = [quarters[0]] + [moved[k] for k in (1, 2, 3)]
+    arrived = [quarters[0]] + [swap(quarters[k], k, "seq") for k in ROW_ORDER[1:]]
     items += [swap(item, k) for k, item in enumerate(near, 1)]
     ordered, payload = row_call(sources, arrived, items)
-    moved = {m: swap(payload, 4 * m, "seq") for m in (1, 3, 2)}
-    payloads = [payload] + [moved[m] for m in (1, 2, 3)]
+    payloads = [payload] + [swap(payload, 4 * m, "seq") for m in LINE_ORDER[1:]]
     mixed = inner_call(tokens, w_query, keys, values, sums, payload)
     *carried, closing = carry_call(payloads, ordered, mixed)
-    moved = {k: swap(carried[k], k, "seq") for k in (2, 1, 3)}
-    state = [carried[0]] + [moved[k] for k in (1, 2, 3)]
-    items = [closing] + [swap(closing, 4 * k) for k in (1, 2, 3)]
+    state = [carried[0]] + [swap(carried[k], k, "seq") for k in ROW_ORDER[1:]]
+    items = [closing] + [swap(closing, 4 * k) for k in FAR_ORDER[1:4]]
     normed = norm_call(lengths, mixed, state)
     near = near_call(True, targets, items, (normed,))
     items += [swap(item, k) for k, item in enumerate(near, 1)]

time: 61.6 us -> 58.6 us (0.951)
  starting transfers between devices: 37.9 us -> 34.4 us
    ppermute x21, starting transfers between devices: 37.9 us -> 34.4 us  [swap(): return lax.ppermute(value, axis, [(k, k ^ bits) for k in range(SHARDS)])]
  transfers between devices with their start and end apart: 21 -> 21, of which waited for: 8 -> 7; matrix products, arithmetic and copies ran while one was open for 0% -> 0% of each run, Pallas kernels for 19% -> 20%
where the time goes in v5:
time: 58.6 us; the launch traced here: 58.5 us
  starting transfers between devices  34.4 us (59%)
  Pallas kernels  14.1 us (24%)
  waiting for transfers between devices  7.63 us (13%)
  between operations  1.66 us (3%)
  local copies, waits for them, and re-layouts  0.74 us (1%)
    ppermute x21, starting transfers between devices, swap(): return lax.ppermute(value, axis, [(k, k ^ bits) for k in range(SHARDS)])  34.4 us
    ppermute x21, waiting for transfers between devices, swap(): return lax.ppermute(value, axis, [(k, k ^ bits) for k in range(SHARDS)])  7.63 us
    pallas_call x1, Pallas kernels, inner_call(): pl.pallas_call(inner_kernel, in_specs=[IN_VMEM] * 5 + [pl.BlockSpec(memor...  5.19 us
    pallas_call x1, Pallas kernels, keys_call(): pl.pallas_call(keys_kernel, in_specs=[IN_SMEM] + [IN_VMEM] * 4, out_specs...  3.33 us
    pallas_call x1, Pallas kernels, whiten_call(): pl.pallas_call(whiten_kernel, in_specs=[IN_VMEM] * 2 + [pl.BlockSpec(memo...  2.06 us
    pallas_call x1, Pallas kernels, norm_call(): pl.pallas_call(norm_kernel, in_specs=[IN_SMEM] + [IN_VMEM] * 5, out_specs...  1.37 us
  transfers between devices with their start and end apart: 21, of which 7 were waited for; matrix products, arithmetic and copies ran while one was open for 0% of the time, Pallas kernels for 20%

profile of v5, /device:TPU:1, one launch (start us, length us, event | category | flops | bytes accessed | tf_op | source)
XLA Modules:
  0.0 58.5 jit_solution(7840594776485436206)
XLA Ops:
  0.7 0.7 %copy-done = f32[1,8,8,128]{3,2,1,0:T(8,128)S(1)} copy-done((f32[1,8,8,128]{3,2,1,0:T(8,128)S(1)}, f32[1,8,8,128]{3,2,1,0:T(8,128)}, u32[]{:S(2)}) %copy-start) | copy-done | bytes 32792
  1.4 7.7 %collective-permute-start.2 = (f32[8,8,128]{2,1,0:T(8,128)S(1)}, f32[8,8,128]{2,1,0:T(8,128)S(1)}, u32[]{:S(2)}, u32[]{:S(2)}) collective-permute-start(f32[8,8,128]{2,1,0:T(8,128)S(1)} %bitcast.7), channel_id=1, source_target_pairs={{0,8},{1,9},{2,10},{3,11},{4,12},{5,13},{6,14},{7,15},{8,0},{9,1},... | collective-permute-start | bytes 98312 | tf_op jit(solution)/shard_map/ppermute | solution.py:400
  9.1 1.2 %collective-permute-start = (f32[8,8,128]{2,1,0:T(8,128)S(1)}, f32[8,8,128]{2,1,0:T(8,128)S(1)}, u32[]{:S(2)}, u32[]{:S(2)}) collective-permute-start(f32[8,8,128]{2,1,0:T(8,128)S(1)} %bitcast.9), channel_id=1, source_target_pairs={{0,4},{1,5},{2,6},{3,7},{4,0},{5,1},{6,2},{7,3},{8,12},{9,13},{10,... | collective-permute-start | bytes 98312 | tf_op jit(solution)/shard_map/ppermute | solution.py:400
  11.0 3.3 %keys_values.1 = (f32[33,8,128]{2,1,0:T(8,128)S(1)}, f32[33,8,128]{2,1,0:T(8,128)S(1)}, f32[33,8,128]{2,1,0:T(8,128)S(1)}, f32[33,8,128]{2,1,0:T(8,128)S(1)}, bf...) custom-call(s32[1]{0:T(128)S(6)} %copy.12.lengths_ref, ...), custom_call_target="tpu_custom_call" | custom-call | flops 3221225472 | bytes 16777216 | tf_op jit(solution)/shard_map/keys_values/pallas_call | solution.py:115
  14.9 2.8 %collective-permute-start.3 = (f32[33,8,128]{2,1,0:T(8,128)S(1)}, f32[33,8,128]{2,1,0:T(8,128)S(1)}, u32[]{:S(2)}, u32[]{:S(2)}) collective-permute-start(f32[33,8,128]{2,1,0:T(8,128)S(1)} %get-tuple-element.44), channel_id=1, source_target_pairs={{0,32},{16,48},{32,0},{48,16},{64,96},{80,112},{96,64},{112,80},{1... | collective-permute-start | bytes 405512 | tf_op jit(solution)/shard_map/ppermute | solution.py:400
  18.0 0.6 collective-permute-start.5
  18.6 2.6 %collective-permute-start.6 = (f32[8,8,128]{2,1,0:T(8,128)S(1)}, f32[8,8,128]{2,1,0:T(8,128)S(1)}, u32[]{:S(2)}, u32[]{:S(2)}) collective-permute-start(f32[8,8,128]{2,1,0:T(8,128)S(1)} %get-tuple-element.47), channel_id=1, source_target_pairs={{0,1},{1,0},{2,3},{3,2},{4,5},{5,4},{6,7},{7,6},{8,9},{9,8},{10,11... | collective-permute-start | bytes 98312 | tf_op jit(solution)/shard_map/ppermute | solution.py:400
  22.0 0.8 %collective-permute-start.8 = (f32[8,8,128]{2,1,0:T(8,128)S(1)}, f32[8,8,128]{2,1,0:T(8,128)S(1)}, u32[]{:S(2)}, u32[]{:S(2)}) collective-permute-start(f32[8,8,128]{2,1,0:T(8,128)S(1)} %get-tuple-element.49), channel_id=1, source_target_pairs={{0,3},{1,2},{2,1},{3,0},{4,7},{5,6},{6,5},{7,4},{8,11},{9,10},{10,... | collective-permute-start | bytes 98312 | tf_op jit(solution)/shard_map/ppermute | solution.py:400
  22.8 1.4 %collective-permute-done.7.refs_9_ = f32[8,8,128]{2,1,0:T(8,128)S(1)} collective-permute-done((f32[8,8,128]{2,1,0:T(8,128)S(1)}, f32[8,8,128]{2,1,0:T(8,128)S(1)}, u32[]{:S(2)}, u32[]{:S(2)}) %collective-permute-start.7) | collective-permute-done | bytes 32800 | tf_op jit(solution)/shard_map/ppermute | solution.py:400
  24.2 1.4 %collective-permute-done.8.refs_10_ = f32[8,8,128]{2,1,0:T(8,128)S(1)} collective-permute-done((f32[8,8,128]{2,1,0:T(8,128)S(1)}, f32[8,8,128]{2,1,0:T(8,128)S(1)}, u32[]{:S(2)}, u32[]{:S(2)}) %collective-permute-start.8) | collective-permute-done | bytes 32800 | tf_op jit(solution)/shard_map/ppermute | solution.py:400
  25.9 3.0 %collective-permute-start.11 = (f32[41,8,128]{2,1,0:T(8,128)S(1)}, f32[41,8,128]{2,1,0:T(8,128)S(1)}, u32[]{:S(2)}, u32[]{:S(2)}) collective-permute-start(f32[41,8,128]{2,1,0:T(8,128)S(1)} %get-tuple-element.50.after_ref.refs_0_), channel_id=1, source_target_pairs={{0,128},{16,144},{32,160},{48,176},{64,192},{80,208},{96,224},{112... | collective-permute-start | bytes 503816 | tf_op jit(solution)/shard_map/ppermute | solution.py:400
  28.9 0.8 %collective-permute-start.10 = (f32[41,8,128]{2,1,0:T(8,128)S(1)}, f32[41,8,128]{2,1,0:T(8,128)S(1)}, u32[]{:S(2)}, u32[]{:S(2)}) collective-permute-start(f32[41,8,128]{2,1,0:T(8,128)S(1)} %get-tuple-element.50.after_ref.refs_0_), channel_id=1, source_target_pairs={{0,192},{16,208},{32,224},{48,240},{64,128},{80,144},{96,160},{112... | collective-permute-start | bytes 503816 | tf_op jit(solution)/shard_map/ppermute | solution.py:400
  29.7 5.2 %queries_inner.1.refs_5_.mixed_ref = bf16[2,512,1024]{2,1,0:T(8,128)(2,1)S(1)} custom-call(bf16[512,1024]{1,0:T(8,128)(2,1)S(1)} %bitcast.18, bf16[1024,1024]{1,0:T(8,128)(2,1)S(1)} %copy-done.5, bf16[1024,512]{1,0:T(8,128)(2,1)S(1)} %get-tuple-element.31.keys_ref, bf16[512,1024]{1,0:T(8,128)(2,1)S(1)} %get-tuple-element.32.values_ref, ...), custom_call_target="tpu_custom_call" | custom-call | flops 3221225472 | bytes 5242880 | tf_op jit(solution)/shard_map/queries_inner/pallas_call | solution.py:148
  34.9 1.5 %collective-permute-done.10.refs_2_ = f32[41,8,128]{2,1,0:T(8,128)S(1)} collective-permute-done((f32[41,8,128]{2,1,0:T(8,128)S(1)}, f32[41,8,128]{2,1,0:T(8,128)S(1)}, u32[]{:S(2)}, u32[]{:S(2)}) %collective-permute-start.10) | collective-permute-done | bytes 167968 | tf_op jit(solution)/shard_map/ppermute | solution.py:400
  36.7 3.3 %collective-permute-start.12 = (f32[32,8,128]{2,1,0:T(8,128)S(1)}, f32[32,8,128]{2,1,0:T(8,128)S(1)}, u32[]{:S(2)}, u32[]{:S(2)}) collective-permute-start(f32[32,8,128]{2,1,0:T(8,128)S(1)} %get-tuple-element.53), channel_id=1, source_target_pairs={{0,32},{16,48},{32,0},{48,16},{64,96},{80,112},{96,64},{112,80},{1... | collective-permute-start | bytes 393224 | tf_op jit(solution)/shard_map/ppermute | solution.py:400
  40.4 0.5 collective-permute-start.14
  40.9 4.2 %collective-permute-start.17 = (f32[8,8,128]{2,1,0:T(8,128)S(1)}, f32[8,8,128]{2,1,0:T(8,128)S(1)}, u32[]{:S(2)}, u32[]{:S(2)}) collective-permute-start(f32[8,8,128]{2,1,0:T(8,128)S(1)} %get-tuple-element.56.refs_0_), channel_id=1, source_target_pairs={{0,8},{1,9},{2,10},{3,11},{4,12},{5,13},{6,14},{7,15},{8,0},{9,1},... | collective-permute-start | bytes 98312 | tf_op jit(solution)/shard_map/ppermute | solution.py:400
  45.3 1.3 %collective-permute-start.15 = (f32[8,8,128]{2,1,0:T(8,128)S(1)}, f32[8,8,128]{2,1,0:T(8,128)S(1)}, u32[]{:S(2)}, u32[]{:S(2)}) collective-permute-start(f32[8,8,128]{2,1,0:T(8,128)S(1)} %get-tuple-element.56.refs_0_), channel_id=1, source_target_pairs={{0,4},{1,5},{2,6},{3,7},{4,0},{5,1},{6,2},{7,3},{8,12},{9,13},{10,... | collective-permute-start | bytes 98312 | tf_op jit(solution)/shard_map/ppermute | solution.py:400
  46.7 1.4 %cross_norm.1.refs_4_.normed_ref = bf16[512,1024]{1,0:T(8,128)(2,1)S(1)} custom-call(s32[1]{0:T(128)S(6)} %copy.12.lengths_ref, bf16[2,512,1024]{2,1,0:T(8,128)(2,1)S(1)} %queries_inner.1.refs_5_.mixed_ref, f32[32,8,128]{2,1,0:T(8,128)S(1)} %get-tuple-element.52.refs_0_, f32[32,8,128]{2,1,0:T(8,128)S(1)} %collective-permute-done.12.refs_1_, ...), custom_call_target="tpu_custom_call" | custom-call | flops 2147483648 | bytes 4194304 | tf_op jit(solution)/shard_map/cross_norm/pallas_call | solution.py:299
  48.1 2.1 %collective-permute-done.16.refs_2_ = f32[8,8,128]{2,1,0:T(8,128)S(1)} collective-permute-done((f32[8,8,128]{2,1,0:T(8,128)S(1)}, f32[8,8,128]{2,1,0:T(8,128)S(1)}, u32[]{:S(2)}, u32[]{:S(2)}) %collective-permute-start.16) | collective-permute-done | bytes 32800 | tf_op jit(solution)/shard_map/ppermute | solution.py:400
  50.6 0.6 collective-permute-start.19
  51.2 3.8 %collective-permute-start.20 = (f32[8,8,128]{2,1,0:T(8,128)S(1)}, f32[8,8,128]{2,1,0:T(8,128)S(1)}, u32[]{:S(2)}, u32[]{:S(2)}) collective-permute-start(f32[8,8,128]{2,1,0:T(8,128)S(1)} %get-tuple-element.59), channel_id=1, source_target_pairs={{0,3},{1,2},{2,1},{3,0},{4,7},{5,6},{6,5},{7,4},{8,11},{9,10},{10,... | collective-permute-start | bytes 98312 | tf_op jit(solution)/shard_map/ppermute | solution.py:400
  55.0 2.1 %whiten_rows.1 = bf16[512,1024]{1,0:T(8,128)(2,1)} custom-call(bf16[512,1024]{1,0:T(8,128)(2,1)S(1)} %cross_norm.1.refs_4_.normed_ref, bf16[1024,1024]{1,0:T(8,128)(2,1)S(1)} %bitcast.16, f32[8,8,128]{2,1,0:T(8,128)S(1)} %get-tuple-element.57.after_ref), custom_call_target="tpu_custom_call" | custom-call | flops 2147483648 | bytes 4194304 | tf_op jit(solution)/shard_map/whiten_rows/pallas_call | solution.py:324
  57.6 0.8 %kept_rows.1 = f32[1,8,8,128]{3,2,1,0:T(8,128)} custom-call(s32[1,16]{1,0:T(1,128)S(1)} %bitcast.13, f32[8,8,128]{2,1,0:T(8,128)S(1)} %get-tuple-element.56.refs_0_, f32[8,8,128]{2,1,0:T(8,128)S(1)} %collective-permute-done.15.refs_1_, f32[8,8,128]{2,1,0:T(8,128)S(1)} %collective-permute-done.16.refs_2_, f32[8,8,128]{2,1,0:T(8,128)S(1)} %collective-permute-done.17.refs_3_, ...), custom_call_target="tpu_custom_call" | custom-call | flops 1024 | bytes 131072 | tf_op jit(solution)/shard_map/kept_rows/pallas_call | solution.py:387
  (46 shorter events, 3.7 us)
Async XLA Ops:
  0.6 10.3 %copy-start.3 = (bf16[1024,1024]{1,0:T(8,128)(2,1)S(1)}, bf16[1024,1024]{1,0:T(8,128)(2,1)}, u32[]{:S(2)}) copy-start(bf16[1024,1024]{1,0:T(8,128)(2,1)} %w_key_ref.1) | copy-start | bytes 6291460
  0.7 10.3 %copy-start.4 = (bf16[1024,1024]{1,0:T(8,128)(2,1)S(1)}, bf16[1024,1024]{1,0:T(8,128)(2,1)}, u32[]{:S(2)}) copy-start(bf16[1024,1024]{1,0:T(8,128)(2,1)} %w_value_ref.1) | copy-start | bytes 6291460
  1.4 13.0 %collective-permute-start.2 = (f32[8,8,128]{2,1,0:T(8,128)S(1)}, f32[8,8,128]{2,1,0:T(8,128)S(1)}, u32[]{:S(2)}, u32[]{:S(2)}) collective-permute-start(f32[8,8,128]{2,1,0:T(8,128)S(1)} %bitcast.7), channel_id=1, source_target_pairs={{0,8},{1,9},{2,10},{3,11},{4,12},{5,13},{6,14},{7,15},{8,0},{9,1},... | collective-permute-start | bytes 98312 | tf_op jit(solution)/shard_map/ppermute | solution.py:400
  9.1 5.3 %collective-permute-start.1 = (f32[8,8,128]{2,1,0:T(8,128)S(1)}, f32[8,8,128]{2,1,0:T(8,128)S(1)}, u32[]{:S(2)}, u32[]{:S(2)}) collective-permute-start(f32[8,8,128]{2,1,0:T(8,128)S(1)} %bitcast.8), channel_id=1, source_target_pairs={{0,12},{1,13},{2,14},{3,15},{4,8},{5,9},{6,10},{7,11},{8,4},{9,5},... | collective-permute-start | bytes 98312 | tf_op jit(solution)/shard_map/ppermute | solution.py:400
  9.1 5.3 %collective-permute-start = (f32[8,8,128]{2,1,0:T(8,128)S(1)}, f32[8,8,128]{2,1,0:T(8,128)S(1)}, u32[]{:S(2)}, u32[]{:S(2)}) collective-permute-start(f32[8,8,128]{2,1,0:T(8,128)S(1)} %bitcast.9), channel_id=1, source_target_pairs={{0,4},{1,5},{2,6},{3,7},{4,0},{5,1},{6,2},{7,3},{8,12},{9,13},{10,... | collective-permute-start | bytes 98312 | tf_op jit(solution)/shard_map/ppermute | solution.py:400
  11.0 18.7 %copy-start.5 = (bf16[1024,1024]{1,0:T(8,128)(2,1)S(1)}, bf16[1024,1024]{1,0:T(8,128)(2,1)}, u32[]{:S(2)}) copy-start(bf16[1024,1024]{1,0:T(8,128)(2,1)} %w_query_ref.1) | copy-start | bytes 6291460
  14.9 10.8 %collective-permute-start.3 = (f32[33,8,128]{2,1,0:T(8,128)S(1)}, f32[33,8,128]{2,1,0:T(8,128)S(1)}, u32[]{:S(2)}, u32[]{:S(2)}) collective-permute-start(f32[33,8,128]{2,1,0:T(8,128)S(1)} %get-tuple-element.44), channel_id=1, source_target_pairs={{0,32},{16,48},{32,0},{48,16},{64,96},{80,112},{96,64},{112,80},{1... | collective-permute-start | bytes 405512 | tf_op jit(solution)/shard_map/ppermute | solution.py:400
  17.7 8.0 %collective-permute-start.4 = (f32[33,8,128]{2,1,0:T(8,128)S(1)}, f32[33,8,128]{2,1,0:T(8,128)S(1)}, u32[]{:S(2)}, u32[]{:S(2)}) collective-permute-start(f32[33,8,128]{2,1,0:T(8,128)S(1)} %get-tuple-element.45), channel_id=1, source_target_pairs={{0,16},{16,0},{32,48},{48,32},{64,80},{80,64},{96,112},{112,96},{1... | collective-permute-start | bytes 405512 | tf_op jit(solution)/shard_map/ppermute | solution.py:400
  18.0 7.7 %collective-permute-start.5 = (f32[33,8,128]{2,1,0:T(8,128)S(1)}, f32[33,8,128]{2,1,0:T(8,128)S(1)}, u32[]{:S(2)}, u32[]{:S(2)}) collective-permute-start(f32[33,8,128]{2,1,0:T(8,128)S(1)} %get-tuple-element.46), channel_id=1, source_target_pairs={{0,48},{16,32},{32,16},{48,0},{64,112},{80,96},{96,80},{112,64},{1... | collective-permute-start | bytes 405512 | tf_op jit(solution)/shard_map/ppermute | solution.py:400
  18.6 3.5 %collective-permute-start.6 = (f32[8,8,128]{2,1,0:T(8,128)S(1)}, f32[8,8,128]{2,1,0:T(8,128)S(1)}, u32[]{:S(2)}, u32[]{:S(2)}) collective-permute-start(f32[8,8,128]{2,1,0:T(8,128)S(1)} %get-tuple-element.47), channel_id=1, source_target_pairs={{0,1},{1,0},{2,3},{3,2},{4,5},{5,4},{6,7},{7,6},{8,9},{9,8},{10,11... | collective-permute-start | bytes 98312 | tf_op jit(solution)/shard_map/ppermute | solution.py:400
  21.2 3.1 %collective-permute-start.7 = (f32[8,8,128]{2,1,0:T(8,128)S(1)}, f32[8,8,128]{2,1,0:T(8,128)S(1)}, u32[]{:S(2)}, u32[]{:S(2)}) collective-permute-start(f32[8,8,128]{2,1,0:T(8,128)S(1)} %get-tuple-element.48), channel_id=1, source_target_pairs={{0,2},{1,3},{2,0},{3,1},{4,6},{5,7},{6,4},{7,5},{8,10},{9,11},{10,... | collective-permute-start | bytes 98312 | tf_op jit(solution)/shard_map/ppermute | solution.py:400
  22.0 3.6 %collective-permute-start.8 = (f32[8,8,128]{2,1,0:T(8,128)S(1)}, f32[8,8,128]{2,1,0:T(8,128)S(1)}, u32[]{:S(2)}, u32[]{:S(2)}) collective-permute-start(f32[8,8,128]{2,1,0:T(8,128)S(1)} %get-tuple-element.49), channel_id=1, source_target_pairs={{0,3},{1,2},{2,1},{3,0},{4,7},{5,6},{6,5},{7,4},{8,11},{9,10},{10,... | collective-permute-start | bytes 98312 | tf_op jit(solution)/shard_map/ppermute | solution.py:400
  25.9 9.0 %collective-permute-start.11 = (f32[41,8,128]{2,1,0:T(8,128)S(1)}, f32[41,8,128]{2,1,0:T(8,128)S(1)}, u32[]{:S(2)}, u32[]{:S(2)}) collective-permute-start(f32[41,8,128]{2,1,0:T(8,128)S(1)} %get-tuple-element.50.after_ref.refs_0_), channel_id=1, source_target_pairs={{0,128},{16,144},{32,160},{48,176},{64,192},{80,208},{96,224},{112... | collective-permute-start | bytes 503816 | tf_op jit(solution)/shard_map/ppermute | solution.py:400
  28.9 7.5 %collective-permute-start.10 = (f32[41,8,128]{2,1,0:T(8,128)S(1)}, f32[41,8,128]{2,1,0:T(8,128)S(1)}, u32[]{:S(2)}, u32[]{:S(2)}) collective-permute-start(f32[41,8,128]{2,1,0:T(8,128)S(1)} %get-tuple-element.50.after_ref.refs_0_), channel_id=1, source_target_pairs={{0,192},{16,208},{32,224},{48,240},{64,128},{80,144},{96,160},{112... | collective-permute-start | bytes 503816 | tf_op jit(solution)/shard_map/ppermute | solution.py:400
  29.7 6.7 %collective-permute-start.9 = (f32[41,8,128]{2,1,0:T(8,128)S(1)}, f32[41,8,128]{2,1,0:T(8,128)S(1)}, u32[]{:S(2)}, u32[]{:S(2)}) collective-permute-start(f32[41,8,128]{2,1,0:T(8,128)S(1)} %get-tuple-element.50.after_ref.refs_0_), channel_id=1, source_target_pairs={{0,64},{16,80},{32,96},{48,112},{64,0},{80,16},{96,32},{112,48},{1... | collective-permute-start | bytes 503816 | tf_op jit(solution)/shard_map/ppermute | solution.py:400
  36.7 8.6 %collective-permute-start.12 = (f32[32,8,128]{2,1,0:T(8,128)S(1)}, f32[32,8,128]{2,1,0:T(8,128)S(1)}, u32[]{:S(2)}, u32[]{:S(2)}) collective-permute-start(f32[32,8,128]{2,1,0:T(8,128)S(1)} %get-tuple-element.53), channel_id=1, source_target_pairs={{0,32},{16,48},{32,0},{48,16},{64,96},{80,112},{96,64},{112,80},{1... | collective-permute-start | bytes 393224 | tf_op jit(solution)/shard_map/ppermute | solution.py:400
  40.0 6.5 %collective-permute-start.13 = (f32[32,8,128]{2,1,0:T(8,128)S(1)}, f32[32,8,128]{2,1,0:T(8,128)S(1)}, u32[]{:S(2)}, u32[]{:S(2)}) collective-permute-start(f32[32,8,128]{2,1,0:T(8,128)S(1)} %get-tuple-element.54), channel_id=1, source_target_pairs={{0,16},{16,0},{32,48},{48,32},{64,80},{80,64},{96,112},{112,96},{1... | collective-permute-start | bytes 393224 | tf_op jit(solution)/shard_map/ppermute | solution.py:400
  40.4 6.3 %collective-permute-start.14 = (f32[32,8,128]{2,1,0:T(8,128)S(1)}, f32[32,8,128]{2,1,0:T(8,128)S(1)}, u32[]{:S(2)}, u32[]{:S(2)}) collective-permute-start(f32[32,8,128]{2,1,0:T(8,128)S(1)} %get-tuple-element.55), channel_id=1, source_target_pairs={{0,48},{16,32},{32,16},{48,0},{64,112},{80,96},{96,80},{112,64},{1... | collective-permute-start | bytes 393224 | tf_op jit(solution)/shard_map/ppermute | solution.py:400
  40.9 7.1 %collective-permute-start.17 = (f32[8,8,128]{2,1,0:T(8,128)S(1)}, f32[8,8,128]{2,1,0:T(8,128)S(1)}, u32[]{:S(2)}, u32[]{:S(2)}) collective-permute-start(f32[8,8,128]{2,1,0:T(8,128)S(1)} %get-tuple-element.56.refs_0_), channel_id=1, source_target_pairs={{0,8},{1,9},{2,10},{3,11},{4,12},{5,13},{6,14},{7,15},{8,0},{9,1},... | collective-permute-start | bytes 98312 | tf_op jit(solution)/shard_map/ppermute | solution.py:400
  45.1 5.1 %collective-permute-start.16 = (f32[8,8,128]{2,1,0:T(8,128)S(1)}, f32[8,8,128]{2,1,0:T(8,128)S(1)}, u32[]{:S(2)}, u32[]{:S(2)}) collective-permute-start(f32[8,8,128]{2,1,0:T(8,128)S(1)} %get-tuple-element.56.refs_0_), channel_id=1, source_target_pairs={{0,12},{1,13},{2,14},{3,15},{4,8},{5,9},{6,10},{7,11},{8,4},{9,5},... | collective-permute-start | bytes 98312 | tf_op jit(solution)/shard_map/ppermute | solution.py:400
  45.3 4.9 %collective-permute-start.15 = (f32[8,8,128]{2,1,0:T(8,128)S(1)}, f32[8,8,128]{2,1,0:T(8,128)S(1)}, u32[]{:S(2)}, u32[]{:S(2)}) collective-permute-start(f32[8,8,128]{2,1,0:T(8,128)S(1)} %get-tuple-element.56.refs_0_), channel_id=1, source_target_pairs={{0,4},{1,5},{2,6},{3,7},{4,0},{5,1},{6,2},{7,3},{8,12},{9,13},{10,... | collective-permute-start | bytes 98312 | tf_op jit(solution)/shard_map/ppermute | solution.py:400
  50.6 6.5 %collective-permute-start.19 = (f32[8,8,128]{2,1,0:T(8,128)S(1)}, f32[8,8,128]{2,1,0:T(8,128)S(1)}, u32[]{:S(2)}, u32[]{:S(2)}) collective-permute-start(f32[8,8,128]{2,1,0:T(8,128)S(1)} %get-tuple-element.58), channel_id=1, source_target_pairs={{0,2},{1,3},{2,0},{3,1},{4,6},{5,7},{6,4},{7,5},{8,10},{9,11},{10,... | collective-permute-start | bytes 98312 | tf_op jit(solution)/shard_map/ppermute | solution.py:400
  51.2 6.4 %collective-permute-start.20 = (f32[8,8,128]{2,1,0:T(8,128)S(1)}, f32[8,8,128]{2,1,0:T(8,128)S(1)}, u32[]{:S(2)}, u32[]{:S(2)}) collective-permute-start(f32[8,8,128]{2,1,0:T(8,128)S(1)} %get-tuple-element.59), channel_id=1, source_target_pairs={{0,3},{1,2},{2,1},{3,0},{4,7},{5,6},{6,5},{7,4},{8,11},{9,10},{10,... | collective-permute-start | bytes 98312 | tf_op jit(solution)/shard_map/ppermute | solution.py:400
  55.0 2.6 %collective-permute-start.18 = (f32[8,8,128]{2,1,0:T(8,128)S(1)}, f32[8,8,128]{2,1,0:T(8,128)S(1)}, u32[]{:S(2)}, u32[]{:S(2)}) collective-permute-start(f32[8,8,128]{2,1,0:T(8,128)S(1)} %get-tuple-element.57.after_ref), channel_id=1, source_target_pairs={{0,1},{1,0},{2,3},{3,2},{4,5},{5,4},{6,7},{7,6},{8,9},{9,8},{10,11... | collective-permute-start | bytes 98312 | tf_op jit(solution)/shard_map/ppermute | solution.py:400
  (6 other events, 36.7 us)

commit v6 on v5

--- a/solution.py
+++ b/solution.py
@@ -18,8 +18,9 @@
 FAR = -1e30
 MIB = 1024 * 1024
 ROW_ORDER = (0, 2, 1, 3)
-LINE_ORDER = (0, 1, 3, 2)
+LINE_ORDER = (0, 3, 1, 2)
 FAR_ORDER = (0, 1, 3, 2, 4, 5, 6)
+START_ORDER = (0, 1, 3, 2, 6, 5, 4)
 IN_HBM = pl.BlockSpec(memory_space=pltpu.HBM)
 IN_VMEM = pl.BlockSpec(memory_space=pltpu.VMEM)
 IN_SMEM = pl.BlockSpec(memory_space=pltpu.SMEM)
@@ -194,7 +195,7 @@
     ordered_ref, payload_ref = refs[11:]
     x, _ = place()
     number = landing(lookup(sources_ref, lax.axis_index("asset"), False))
-    for k, item in zip(FAR_ORDER, items):
+    for k, item in zip(START_ORDER, items):
         @pl.when(number == k)
         def _(item=item):
             payload_ref[33:41] = item[...]
@@ -410,7 +411,7 @@
     near = near_call(False, sources, items, (mark,))
     near, quarters = lax.optimization_barrier((near, quarters))
     arrived = [quarters[0]] + [swap(quarters[k], k, "seq") for k in ROW_ORDER[1:]]
-    items += [swap(item, k) for k, item in enumerate(near, 1)]
+    items += [swap(near[k - 1], k) for k in (3, 2, 1)]
     ordered, payload = row_call(sources, arrived, items)
     payloads = [payload] + [swap(payload, 4 * m, "seq") for m in LINE_ORDER[1:]]
     mixed = inner_call(tokens, w_query, keys, values, sums, payload)

time: 58.6 us -> 58.6 us (level)
  waiting for transfers between devices: 7.63 us -> 5.61 us
  starting transfers between devices: 34.4 us -> 36.4 us
    ppermute x21, starting transfers between devices: 34.4 us -> 36.4 us  [swap(): return lax.ppermute(value, axis, [(k, k ^ bits) for k in range(SHARDS)])]
    ppermute x21, waiting for transfers between devices: 7.63 us -> 5.61 us  [swap(): return lax.ppermute(value, axis, [(k, k ^ bits) for k in range(SHARDS)])]
  transfers between devices with their start and end apart: 21 -> 21, of which waited for: 7 -> 8; matrix products, arithmetic and copies ran while one was open for 0% -> 0% of each run, Pallas kernels for 20% -> 20%
where the time goes in v6:
time: 58.6 us; the launch traced here: 58.5 us
  starting transfers between devices  36.4 us (62%)
  Pallas kernels  14.1 us (24%)
  waiting for transfers between devices  5.61 us (10%)
  between operations  1.66 us (3%)
  local copies, waits for them, and re-layouts  0.74 us (1%)
    ppermute x21, starting transfers between devices, swap(): return lax.ppermute(value, axis, [(k, k ^ bits) for k in range(SHARDS)])  36.4 us
    ppermute x21, waiting for transfers between devices, swap(): return lax.ppermute(value, axis, [(k, k ^ bits) for k in range(SHARDS)])  5.61 us
    pallas_call x1, Pallas kernels, inner_call(): pl.pallas_call(inner_kernel, in_specs=[IN_VMEM] * 5 + [pl.BlockSpec(memor...  5.19 us
    pallas_call x1, Pallas kernels, keys_call(): pl.pallas_call(keys_kernel, in_specs=[IN_SMEM] + [IN_VMEM] * 4, out_specs...  3.33 us
    pallas_call x1, Pallas kernels, whiten_call(): pl.pallas_call(whiten_kernel, in_specs=[IN_VMEM] * 2 + [pl.BlockSpec(memo...  2.06 us
    pallas_call x1, Pallas kernels, norm_call(): pl.pallas_call(norm_kernel, in_specs=[IN_SMEM] + [IN_VMEM] * 5, out_specs...  1.37 us
  transfers between devices with their start and end apart: 21, of which 8 were waited for; matrix products, arithmetic and copies ran while one was open for 0% of the time, Pallas kernels for 20%

profile of v6, /device:TPU:1, one launch (start us, length us, event | category | flops | bytes accessed | tf_op | source)
XLA Modules:
  0.0 58.5 jit_solution(9660534877084550538)
XLA Ops:
  0.7 0.7 %copy-done = f32[1,8,8,128]{3,2,1,0:T(8,128)S(1)} copy-done((f32[1,8,8,128]{3,2,1,0:T(8,128)S(1)}, f32[1,8,8,128]{3,2,1,0:T(8,128)}, u32[]{:S(2)}) %copy-start) | copy-done | bytes 32792
  1.4 7.7 %collective-permute-start.2 = (f32[8,8,128]{2,1,0:T(8,128)S(1)}, f32[8,8,128]{2,1,0:T(8,128)S(1)}, u32[]{:S(2)}, u32[]{:S(2)}) collective-permute-start(f32[8,8,128]{2,1,0:T(8,128)S(1)} %bitcast.7), channel_id=1, source_target_pairs={{0,8},{1,9},{2,10},{3,11},{4,12},{5,13},{6,14},{7,15},{8,0},{9,1},... | collective-permute-start | bytes 98312 | tf_op jit(solution)/shard_map/ppermute | solution.py:401
  9.1 1.2 %collective-permute-start = (f32[8,8,128]{2,1,0:T(8,128)S(1)}, f32[8,8,128]{2,1,0:T(8,128)S(1)}, u32[]{:S(2)}, u32[]{:S(2)}) collective-permute-start(f32[8,8,128]{2,1,0:T(8,128)S(1)} %bitcast.9), channel_id=1, source_target_pairs={{0,4},{1,5},{2,6},{3,7},{4,0},{5,1},{6,2},{7,3},{8,12},{9,13},{10,... | collective-permute-start | bytes 98312 | tf_op jit(solution)/shard_map/ppermute | solution.py:401
  11.0 3.3 %keys_values.1 = (f32[33,8,128]{2,1,0:T(8,128)S(1)}, f32[33,8,128]{2,1,0:T(8,128)S(1)}, f32[33,8,128]{2,1,0:T(8,128)S(1)}, f32[33,8,128]{2,1,0:T(8,128)S(1)}, bf...) custom-call(s32[1]{0:T(128)S(6)} %copy.12.lengths_ref, ...), custom_call_target="tpu_custom_call" | custom-call | flops 3221225472 | bytes 16777216 | tf_op jit(solution)/shard_map/keys_values/pallas_call | solution.py:116
  14.9 2.8 %collective-permute-start.3 = (f32[33,8,128]{2,1,0:T(8,128)S(1)}, f32[33,8,128]{2,1,0:T(8,128)S(1)}, u32[]{:S(2)}, u32[]{:S(2)}) collective-permute-start(f32[33,8,128]{2,1,0:T(8,128)S(1)} %get-tuple-element.44), channel_id=1, source_target_pairs={{0,32},{16,48},{32,0},{48,16},{64,96},{80,112},{96,64},{112,80},{1... | collective-permute-start | bytes 405512 | tf_op jit(solution)/shard_map/ppermute | solution.py:401
  18.6 2.9 %collective-permute-start.6 = (f32[8,8,128]{2,1,0:T(8,128)S(1)}, f32[8,8,128]{2,1,0:T(8,128)S(1)}, u32[]{:S(2)}, u32[]{:S(2)}) collective-permute-start(f32[8,8,128]{2,1,0:T(8,128)S(1)} %get-tuple-element.47), channel_id=1, source_target_pairs={{0,3},{1,2},{2,1},{3,0},{4,7},{5,6},{6,5},{7,4},{8,11},{9,10},{10,... | collective-permute-start | bytes 98312 | tf_op jit(solution)/shard_map/ppermute | solution.py:401
  21.4 1.1 %collective-permute-start.7 = (f32[8,8,128]{2,1,0:T(8,128)S(1)}, f32[8,8,128]{2,1,0:T(8,128)S(1)}, u32[]{:S(2)}, u32[]{:S(2)}) collective-permute-start(f32[8,8,128]{2,1,0:T(8,128)S(1)} %get-tuple-element.48), channel_id=1, source_target_pairs={{0,2},{1,3},{2,0},{3,1},{4,6},{5,7},{6,4},{7,5},{8,10},{9,11},{10,... | collective-permute-start | bytes 98312 | tf_op jit(solution)/shard_map/ppermute | solution.py:401
  22.5 0.8 %collective-permute-done.6.refs_8_ = f32[8,8,128]{2,1,0:T(8,128)S(1)} collective-permute-done((f32[8,8,128]{2,1,0:T(8,128)S(1)}, f32[8,8,128]{2,1,0:T(8,128)S(1)}, u32[]{:S(2)}, u32[]{:S(2)}) %collective-permute-start.6) | collective-permute-done | bytes 32800 | tf_op jit(solution)/shard_map/ppermute | solution.py:401
  23.3 1.2 %collective-permute-start.8 = (f32[8,8,128]{2,1,0:T(8,128)S(1)}, f32[8,8,128]{2,1,0:T(8,128)S(1)}, u32[]{:S(2)}, u32[]{:S(2)}) collective-permute-start(f32[8,8,128]{2,1,0:T(8,128)S(1)} %get-tuple-element.49), channel_id=1, source_target_pairs={{0,1},{1,0},{2,3},{3,2},{4,5},{5,4},{6,7},{7,6},{8,9},{9,8},{10,11... | collective-permute-start | bytes 98312 | tf_op jit(solution)/shard_map/ppermute | solution.py:401
  24.6 0.7 %collective-permute-done.8.refs_10_ = f32[8,8,128]{2,1,0:T(8,128)S(1)} collective-permute-done((f32[8,8,128]{2,1,0:T(8,128)S(1)}, f32[8,8,128]{2,1,0:T(8,128)S(1)}, u32[]{:S(2)}, u32[]{:S(2)}) %collective-permute-start.8) | collective-permute-done | bytes 32800 | tf_op jit(solution)/shard_map/ppermute | solution.py:401
  25.6 3.0 %collective-permute-start.11 = (f32[41,8,128]{2,1,0:T(8,128)S(1)}, f32[41,8,128]{2,1,0:T(8,128)S(1)}, u32[]{:S(2)}, u32[]{:S(2)}) collective-permute-start(f32[41,8,128]{2,1,0:T(8,128)S(1)} %get-tuple-element.50.after_ref.refs_0_), channel_id=1, source_target_pairs={{0,128},{16,144},{32,160},{48,176},{64,192},{80,208},{96,224},{112... | collective-permute-start | bytes 503816 | tf_op jit(solution)/shard_map/ppermute | solution.py:401
  29.4 5.2 %queries_inner.1.refs_5_.mixed_ref = bf16[2,512,1024]{2,1,0:T(8,128)(2,1)S(1)} custom-call(bf16[512,1024]{1,0:T(8,128)(2,1)S(1)} %bitcast.18, bf16[1024,1024]{1,0:T(8,128)(2,1)S(1)} %copy-done.5, bf16[1024,512]{1,0:T(8,128)(2,1)S(1)} %get-tuple-element.31.keys_ref, bf16[512,1024]{1,0:T(8,128)(2,1)S(1)} %get-tuple-element.32.values_ref, ...), custom_call_target="tpu_custom_call" | custom-call | flops 3221225472 | bytes 5242880 | tf_op jit(solution)/shard_map/queries_inner/pallas_call | solution.py:149
  34.6 0.8 %collective-permute-done.10.refs_2_ = f32[41,8,128]{2,1,0:T(8,128)S(1)} collective-permute-done((f32[41,8,128]{2,1,0:T(8,128)S(1)}, f32[41,8,128]{2,1,0:T(8,128)S(1)}, u32[]{:S(2)}, u32[]{:S(2)}) %collective-permute-start.10) | collective-permute-done | bytes 167968 | tf_op jit(solution)/shard_map/ppermute | solution.py:401
  35.4 1.1 %collective-permute-done.9.refs_1_ = f32[41,8,128]{2,1,0:T(8,128)S(1)} collective-permute-done((f32[41,8,128]{2,1,0:T(8,128)S(1)}, f32[41,8,128]{2,1,0:T(8,128)S(1)}, u32[]{:S(2)}, u32[]{:S(2)}) %collective-permute-start.9) | collective-permute-done | bytes 167968 | tf_op jit(solution)/shard_map/ppermute | solution.py:401
  36.7 3.0 %collective-permute-start.12 = (f32[32,8,128]{2,1,0:T(8,128)S(1)}, f32[32,8,128]{2,1,0:T(8,128)S(1)}, u32[]{:S(2)}, u32[]{:S(2)}) collective-permute-start(f32[32,8,128]{2,1,0:T(8,128)S(1)} %get-tuple-element.53), channel_id=1, source_target_pairs={{0,32},{16,48},{32,0},{48,16},{64,96},{80,112},{96,64},{112,80},{1... | collective-permute-start | bytes 393224 | tf_op jit(solution)/shard_map/ppermute | solution.py:401
  40.6 3.7 %collective-permute-start.17 = (f32[8,8,128]{2,1,0:T(8,128)S(1)}, f32[8,8,128]{2,1,0:T(8,128)S(1)}, u32[]{:S(2)}, u32[]{:S(2)}) collective-permute-start(f32[8,8,128]{2,1,0:T(8,128)S(1)} %get-tuple-element.56.refs_0_), channel_id=1, source_target_pairs={{0,8},{1,9},{2,10},{3,11},{4,12},{5,13},{6,14},{7,15},{8,0},{9,1},... | collective-permute-start | bytes 98312 | tf_op jit(solution)/shard_map/ppermute | solution.py:401
  44.3 0.7 %collective-permute-start.16 = (f32[8,8,128]{2,1,0:T(8,128)S(1)}, f32[8,8,128]{2,1,0:T(8,128)S(1)}, u32[]{:S(2)}, u32[]{:S(2)}) collective-permute-start(f32[8,8,128]{2,1,0:T(8,128)S(1)} %get-tuple-element.56.refs_0_), channel_id=1, source_target_pairs={{0,12},{1,13},{2,14},{3,15},{4,8},{5,9},{6,10},{7,11},{8,4},{9,5},... | collective-permute-start | bytes 98312 | tf_op jit(solution)/shard_map/ppermute | solution.py:401
  45.0 1.2 %collective-permute-start.15 = (f32[8,8,128]{2,1,0:T(8,128)S(1)}, f32[8,8,128]{2,1,0:T(8,128)S(1)}, u32[]{:S(2)}, u32[]{:S(2)}) collective-permute-start(f32[8,8,128]{2,1,0:T(8,128)S(1)} %get-tuple-element.56.refs_0_), channel_id=1, source_target_pairs={{0,4},{1,5},{2,6},{3,7},{4,0},{5,1},{6,2},{7,3},{8,12},{9,13},{10,... | collective-permute-start | bytes 98312 | tf_op jit(solution)/shard_map/ppermute | solution.py:401
  46.5 1.4 %cross_norm.1.refs_4_.normed_ref = bf16[512,1024]{1,0:T(8,128)(2,1)S(1)} custom-call(s32[1]{0:T(128)S(6)} %copy.12.lengths_ref, bf16[2,512,1024]{2,1,0:T(8,128)(2,1)S(1)} %queries_inner.1.refs_5_.mixed_ref, f32[32,8,128]{2,1,0:T(8,128)S(1)} %get-tuple-element.52.refs_0_, f32[32,8,128]{2,1,0:T(8,128)S(1)} %collective-permute-done.12.refs_1_, ...), custom_call_target="tpu_custom_call" | custom-call | flops 2147483648 | bytes 4194304 | tf_op jit(solution)/shard_map/cross_norm/pallas_call | solution.py:300
  47.9 1.3 %collective-permute-done.16.refs_2_ = f32[8,8,128]{2,1,0:T(8,128)S(1)} collective-permute-done((f32[8,8,128]{2,1,0:T(8,128)S(1)}, f32[8,8,128]{2,1,0:T(8,128)S(1)}, u32[]{:S(2)}, u32[]{:S(2)}) %collective-permute-start.16) | collective-permute-done | bytes 32800 | tf_op jit(solution)/shard_map/ppermute | solution.py:401
  49.6 1.5 %collective-permute-start.19 = (f32[8,8,128]{2,1,0:T(8,128)S(1)}, f32[8,8,128]{2,1,0:T(8,128)S(1)}, u32[]{:S(2)}, u32[]{:S(2)}) collective-permute-start(f32[8,8,128]{2,1,0:T(8,128)S(1)} %get-tuple-element.58), channel_id=1, source_target_pairs={{0,2},{1,3},{2,0},{3,1},{4,6},{5,7},{6,4},{7,5},{8,10},{9,11},{10,... | collective-permute-start | bytes 98312 | tf_op jit(solution)/shard_map/ppermute | solution.py:401
  51.1 3.9 %collective-permute-start.20 = (f32[8,8,128]{2,1,0:T(8,128)S(1)}, f32[8,8,128]{2,1,0:T(8,128)S(1)}, u32[]{:S(2)}, u32[]{:S(2)}) collective-permute-start(f32[8,8,128]{2,1,0:T(8,128)S(1)} %get-tuple-element.59), channel_id=1, source_target_pairs={{0,3},{1,2},{2,1},{3,0},{4,7},{5,6},{6,5},{7,4},{8,11},{9,10},{10,... | collective-permute-start | bytes 98312 | tf_op jit(solution)/shard_map/ppermute | solution.py:401
  55.0 2.1 %whiten_rows.1 = bf16[512,1024]{1,0:T(8,128)(2,1)} custom-call(bf16[512,1024]{1,0:T(8,128)(2,1)S(1)} %cross_norm.1.refs_4_.normed_ref, bf16[1024,1024]{1,0:T(8,128)(2,1)S(1)} %bitcast.16, f32[8,8,128]{2,1,0:T(8,128)S(1)} %get-tuple-element.57.after_ref), custom_call_target="tpu_custom_call" | custom-call | flops 2147483648 | bytes 4194304 | tf_op jit(solution)/shard_map/whiten_rows/pallas_call | solution.py:325
  57.6 0.8 %kept_rows.1 = f32[1,8,8,128]{3,2,1,0:T(8,128)} custom-call(s32[1,16]{1,0:T(1,128)S(1)} %bitcast.13, f32[8,8,128]{2,1,0:T(8,128)S(1)} %get-tuple-element.56.refs_0_, f32[8,8,128]{2,1,0:T(8,128)S(1)} %collective-permute-done.15.refs_1_, f32[8,8,128]{2,1,0:T(8,128)S(1)} %collective-permute-done.16.refs_2_, f32[8,8,128]{2,1,0:T(8,128)S(1)} %collective-permute-done.17.refs_3_, ...), custom_call_target="tpu_custom_call" | custom-call | flops 1024 | bytes 131072 | tf_op jit(solution)/shard_map/kept_rows/pallas_call | solution.py:388
  (46 shorter events, 4.8 us)
Async XLA Ops:
  0.6 10.3 %copy-start.3 = (bf16[1024,1024]{1,0:T(8,128)(2,1)S(1)}, bf16[1024,1024]{1,0:T(8,128)(2,1)}, u32[]{:S(2)}) copy-start(bf16[1024,1024]{1,0:T(8,128)(2,1)} %w_key_ref.1) | copy-start | bytes 6291460
  0.7 10.3 %copy-start.4 = (bf16[1024,1024]{1,0:T(8,128)(2,1)S(1)}, bf16[1024,1024]{1,0:T(8,128)(2,1)}, u32[]{:S(2)}) copy-start(bf16[1024,1024]{1,0:T(8,128)(2,1)} %w_value_ref.1) | copy-start | bytes 6291460
  1.4 13.0 %collective-permute-start.2 = (f32[8,8,128]{2,1,0:T(8,128)S(1)}, f32[8,8,128]{2,1,0:T(8,128)S(1)}, u32[]{:S(2)}, u32[]{:S(2)}) collective-permute-start(f32[8,8,128]{2,1,0:T(8,128)S(1)} %bitcast.7), channel_id=1, source_target_pairs={{0,8},{1,9},{2,10},{3,11},{4,12},{5,13},{6,14},{7,15},{8,0},{9,1},... | collective-permute-start | bytes 98312 | tf_op jit(solution)/shard_map/ppermute | solution.py:401
  9.1 5.3 %collective-permute-start.1 = (f32[8,8,128]{2,1,0:T(8,128)S(1)}, f32[8,8,128]{2,1,0:T(8,128)S(1)}, u32[]{:S(2)}, u32[]{:S(2)}) collective-permute-start(f32[8,8,128]{2,1,0:T(8,128)S(1)} %bitcast.8), channel_id=1, source_target_pairs={{0,12},{1,13},{2,14},{3,15},{4,8},{5,9},{6,10},{7,11},{8,4},{9,5},... | collective-permute-start | bytes 98312 | tf_op jit(solution)/shard_map/ppermute | solution.py:401
  9.1 5.3 %collective-permute-start = (f32[8,8,128]{2,1,0:T(8,128)S(1)}, f32[8,8,128]{2,1,0:T(8,128)S(1)}, u32[]{:S(2)}, u32[]{:S(2)}) collective-permute-start(f32[8,8,128]{2,1,0:T(8,128)S(1)} %bitcast.9), channel_id=1, source_target_pairs={{0,4},{1,5},{2,6},{3,7},{4,0},{5,1},{6,2},{7,3},{8,12},{9,13},{10,... | collective-permute-start | bytes 98312 | tf_op jit(solution)/shard_map/ppermute | solution.py:401
  11.0 18.4 %copy-start.5 = (bf16[1024,1024]{1,0:T(8,128)(2,1)S(1)}, bf16[1024,1024]{1,0:T(8,128)(2,1)}, u32[]{:S(2)}) copy-start(bf16[1024,1024]{1,0:T(8,128)(2,1)} %w_query_ref.1) | copy-start | bytes 6291460
  14.9 10.5 %collective-permute-start.3 = (f32[33,8,128]{2,1,0:T(8,128)S(1)}, f32[33,8,128]{2,1,0:T(8,128)S(1)}, u32[]{:S(2)}, u32[]{:S(2)}) collective-permute-start(f32[33,8,128]{2,1,0:T(8,128)S(1)} %get-tuple-element.44), channel_id=1, source_target_pairs={{0,32},{16,48},{32,0},{48,16},{64,96},{80,112},{96,64},{112,80},{1... | collective-permute-start | bytes 405512 | tf_op jit(solution)/shard_map/ppermute | solution.py:401
  17.7 7.7 %collective-permute-start.4 = (f32[33,8,128]{2,1,0:T(8,128)S(1)}, f32[33,8,128]{2,1,0:T(8,128)S(1)}, u32[]{:S(2)}, u32[]{:S(2)}) collective-permute-start(f32[33,8,128]{2,1,0:T(8,128)S(1)} %get-tuple-element.45), channel_id=1, source_target_pairs={{0,16},{16,0},{32,48},{48,32},{64,80},{80,64},{96,112},{112,96},{1... | collective-permute-start | bytes 405512 | tf_op jit(solution)/shard_map/ppermute | solution.py:401
  18.0 7.4 %collective-permute-start.5 = (f32[33,8,128]{2,1,0:T(8,128)S(1)}, f32[33,8,128]{2,1,0:T(8,128)S(1)}, u32[]{:S(2)}, u32[]{:S(2)}) collective-permute-start(f32[33,8,128]{2,1,0:T(8,128)S(1)} %get-tuple-element.46), channel_id=1, source_target_pairs={{0,48},{16,32},{32,16},{48,0},{64,112},{80,96},{96,80},{112,64},{1... | collective-permute-start | bytes 405512 | tf_op jit(solution)/shard_map/ppermute | solution.py:401
  18.6 4.8 %collective-permute-start.6 = (f32[8,8,128]{2,1,0:T(8,128)S(1)}, f32[8,8,128]{2,1,0:T(8,128)S(1)}, u32[]{:S(2)}, u32[]{:S(2)}) collective-permute-start(f32[8,8,128]{2,1,0:T(8,128)S(1)} %get-tuple-element.47), channel_id=1, source_target_pairs={{0,3},{1,2},{2,1},{3,0},{4,7},{5,6},{6,5},{7,4},{8,11},{9,10},{10,... | collective-permute-start | bytes 98312 | tf_op jit(solution)/shard_map/ppermute | solution.py:401
  21.4 3.2 %collective-permute-start.7 = (f32[8,8,128]{2,1,0:T(8,128)S(1)}, f32[8,8,128]{2,1,0:T(8,128)S(1)}, u32[]{:S(2)}, u32[]{:S(2)}) collective-permute-start(f32[8,8,128]{2,1,0:T(8,128)S(1)} %get-tuple-element.48), channel_id=1, source_target_pairs={{0,2},{1,3},{2,0},{3,1},{4,6},{5,7},{6,4},{7,5},{8,10},{9,11},{10,... | collective-permute-start | bytes 98312 | tf_op jit(solution)/shard_map/ppermute | solution.py:401
  23.3 2.0 %collective-permute-start.8 = (f32[8,8,128]{2,1,0:T(8,128)S(1)}, f32[8,8,128]{2,1,0:T(8,128)S(1)}, u32[]{:S(2)}, u32[]{:S(2)}) collective-permute-start(f32[8,8,128]{2,1,0:T(8,128)S(1)} %get-tuple-element.49), channel_id=1, source_target_pairs={{0,1},{1,0},{2,3},{3,2},{4,5},{5,4},{6,7},{7,6},{8,9},{9,8},{10,11... | collective-permute-start | bytes 98312 | tf_op jit(solution)/shard_map/ppermute | solution.py:401
  25.6 9.0 %collective-permute-start.11 = (f32[41,8,128]{2,1,0:T(8,128)S(1)}, f32[41,8,128]{2,1,0:T(8,128)S(1)}, u32[]{:S(2)}, u32[]{:S(2)}) collective-permute-start(f32[41,8,128]{2,1,0:T(8,128)S(1)} %get-tuple-element.50.after_ref.refs_0_), channel_id=1, source_target_pairs={{0,128},{16,144},{32,160},{48,176},{64,192},{80,208},{96,224},{112... | collective-permute-start | bytes 503816 | tf_op jit(solution)/shard_map/ppermute | solution.py:401
  28.6 6.8 %collective-permute-start.10 = (f32[41,8,128]{2,1,0:T(8,128)S(1)}, f32[41,8,128]{2,1,0:T(8,128)S(1)}, u32[]{:S(2)}, u32[]{:S(2)}) collective-permute-start(f32[41,8,128]{2,1,0:T(8,128)S(1)} %get-tuple-element.50.after_ref.refs_0_), channel_id=1, source_target_pairs={{0,64},{16,80},{32,96},{48,112},{64,0},{80,16},{96,32},{112,48},{1... | collective-permute-start | bytes 503816 | tf_op jit(solution)/shard_map/ppermute | solution.py:401
  29.0 7.5 %collective-permute-start.9 = (f32[41,8,128]{2,1,0:T(8,128)S(1)}, f32[41,8,128]{2,1,0:T(8,128)S(1)}, u32[]{:S(2)}, u32[]{:S(2)}) collective-permute-start(f32[41,8,128]{2,1,0:T(8,128)S(1)} %get-tuple-element.50.after_ref.refs_0_), channel_id=1, source_target_pairs={{0,192},{16,208},{32,224},{48,240},{64,128},{80,144},{96,160},{112... | collective-permute-start | bytes 503816 | tf_op jit(solution)/shard_map/ppermute | solution.py:401
  36.7 8.3 %collective-permute-start.12 = (f32[32,8,128]{2,1,0:T(8,128)S(1)}, f32[32,8,128]{2,1,0:T(8,128)S(1)}, u32[]{:S(2)}, u32[]{:S(2)}) collective-permute-start(f32[32,8,128]{2,1,0:T(8,128)S(1)} %get-tuple-element.53), channel_id=1, source_target_pairs={{0,32},{16,48},{32,0},{48,16},{64,96},{80,112},{96,64},{112,80},{1... | collective-permute-start | bytes 393224 | tf_op jit(solution)/shard_map/ppermute | solution.py:401
  39.7 6.5 %collective-permute-start.13 = (f32[32,8,128]{2,1,0:T(8,128)S(1)}, f32[32,8,128]{2,1,0:T(8,128)S(1)}, u32[]{:S(2)}, u32[]{:S(2)}) collective-permute-start(f32[32,8,128]{2,1,0:T(8,128)S(1)} %get-tuple-element.54), channel_id=1, source_target_pairs={{0,16},{16,0},{32,48},{48,32},{64,80},{80,64},{96,112},{112,96},{1... | collective-permute-start | bytes 393224 | tf_op jit(solution)/shard_map/ppermute | solution.py:401
  40.1 6.5 %collective-permute-start.14 = (f32[32,8,128]{2,1,0:T(8,128)S(1)}, f32[32,8,128]{2,1,0:T(8,128)S(1)}, u32[]{:S(2)}, u32[]{:S(2)}) collective-permute-start(f32[32,8,128]{2,1,0:T(8,128)S(1)} %get-tuple-element.55), channel_id=1, source_target_pairs={{0,48},{16,32},{32,16},{48,0},{64,112},{80,96},{96,80},{112,64},{1... | collective-permute-start | bytes 393224 | tf_op jit(solution)/shard_map/ppermute | solution.py:401
  40.6 7.3 %collective-permute-start.17 = (f32[8,8,128]{2,1,0:T(8,128)S(1)}, f32[8,8,128]{2,1,0:T(8,128)S(1)}, u32[]{:S(2)}, u32[]{:S(2)}) collective-permute-start(f32[8,8,128]{2,1,0:T(8,128)S(1)} %get-tuple-element.56.refs_0_), channel_id=1, source_target_pairs={{0,8},{1,9},{2,10},{3,11},{4,12},{5,13},{6,14},{7,15},{8,0},{9,1},... | collective-permute-start | bytes 98312 | tf_op jit(solution)/shard_map/ppermute | solution.py:401
  44.3 4.9 %collective-permute-start.16 = (f32[8,8,128]{2,1,0:T(8,128)S(1)}, f32[8,8,128]{2,1,0:T(8,128)S(1)}, u32[]{:S(2)}, u32[]{:S(2)}) collective-permute-start(f32[8,8,128]{2,1,0:T(8,128)S(1)} %get-tuple-element.56.refs_0_), channel_id=1, source_target_pairs={{0,12},{1,13},{2,14},{3,15},{4,8},{5,9},{6,10},{7,11},{8,4},{9,5},... | collective-permute-start | bytes 98312 | tf_op jit(solution)/shard_map/ppermute | solution.py:401
  45.0 4.2 %collective-permute-start.15 = (f32[8,8,128]{2,1,0:T(8,128)S(1)}, f32[8,8,128]{2,1,0:T(8,128)S(1)}, u32[]{:S(2)}, u32[]{:S(2)}) collective-permute-start(f32[8,8,128]{2,1,0:T(8,128)S(1)} %get-tuple-element.56.refs_0_), channel_id=1, source_target_pairs={{0,4},{1,5},{2,6},{3,7},{4,0},{5,1},{6,2},{7,3},{8,12},{9,13},{10,... | collective-permute-start | bytes 98312 | tf_op jit(solution)/shard_map/ppermute | solution.py:401
  49.6 7.5 %collective-permute-start.19 = (f32[8,8,128]{2,1,0:T(8,128)S(1)}, f32[8,8,128]{2,1,0:T(8,128)S(1)}, u32[]{:S(2)}, u32[]{:S(2)}) collective-permute-start(f32[8,8,128]{2,1,0:T(8,128)S(1)} %get-tuple-element.58), channel_id=1, source_target_pairs={{0,2},{1,3},{2,0},{3,1},{4,6},{5,7},{6,4},{7,5},{8,10},{9,11},{10,... | collective-permute-start | bytes 98312 | tf_op jit(solution)/shard_map/ppermute | solution.py:401
  51.1 6.5 %collective-permute-start.20 = (f32[8,8,128]{2,1,0:T(8,128)S(1)}, f32[8,8,128]{2,1,0:T(8,128)S(1)}, u32[]{:S(2)}, u32[]{:S(2)}) collective-permute-start(f32[8,8,128]{2,1,0:T(8,128)S(1)} %get-tuple-element.59), channel_id=1, source_target_pairs={{0,3},{1,2},{2,1},{3,0},{4,7},{5,6},{6,5},{7,4},{8,11},{9,10},{10,... | collective-permute-start | bytes 98312 | tf_op jit(solution)/shard_map/ppermute | solution.py:401
  55.0 2.6 %collective-permute-start.18 = (f32[8,8,128]{2,1,0:T(8,128)S(1)}, f32[8,8,128]{2,1,0:T(8,128)S(1)}, u32[]{:S(2)}, u32[]{:S(2)}) collective-permute-start(f32[8,8,128]{2,1,0:T(8,128)S(1)} %get-tuple-element.57.after_ref), channel_id=1, source_target_pairs={{0,1},{1,0},{2,3},{3,2},{4,5},{5,4},{6,7},{7,6},{8,9},{9,8},{10,11... | collective-permute-start | bytes 98312 | tf_op jit(solution)/shard_map/ppermute | solution.py:401
  (6 other events, 36.0 us)
